TPU v7x, 512 devices: a whole 4x8x8 slice. The times are simulated.
512 devices in a mesh: ctx: 128 (over z_lo, x, y), head: 2 (over z_hi), rep: 2 (over core).
Axes of the slice: x: 4, y: 8, z: 8 (z_hi: 2, z_lo: 4; z = z_hi * 4 + z_lo), core: 2. Of those that a mesh axis runs over, the one named last changes fastest.
Arguments:
- seq_values: bfloat16 [65536, 4096], P(('rep', 'ctx'), 'head'), parts along dimension 0, may hold values from -6 to 6
- seq_gate: bfloat16 [65536, 4096], P(('rep', 'ctx'), 'head'), parts along dimension 0, may hold values from -6 to 6
- seq_keys: bfloat16 [65536, 128], P(('rep', 'ctx')), parts along dimension 0, may hold values from -6 to 6
- seq_queries: bfloat16 [65536, 128], P(('rep', 'ctx')), parts along dimension 0, may hold values from -0.5 to 0.5
- level_weights: bfloat16 [16, 64, 65536], P(None, 'head', ('rep', 'ctx')), parts along dimension 2, may hold values from 0 to 4
- skip_gain: float32 [64], P('head'), may hold values from 0.5 to 2
- norm_gain: float32 [4096], P('head'), may hold values from 0.5 to 1.5
- out_weight: bfloat16 [4096, 2048], P('head', 'ctx'), may hold values from -0.09375 to 0.09375
Outputs:
- mixer_out: bfloat16 [65536, 2048], P(('rep', 'ctx'), 'head'), parts along dimension 0
There are 2 independent parts, one for each index of `rep`. A program takes and returns all parts, laid end to end along the dimension named above; an argument that names none is the same for every part. Nothing has to cross between parts.
All inputs are finite; a program needn't handle non-finite values.
Results may differ from a plain program's by a relative error of at most 0.0054.
Values may be sent and summed in bfloat16 or wider, within the bound.
No kernel may reach another device: no remote copies, remote signals or barrier semaphores. Data moves between devices by JAX's collectives and lax.ppermute only.
A program may use at most 64 MiB of HBM per device.

v0:
```python
import jax
import jax.numpy as jnp
from jax import lax
from jax.sharding import PartitionSpec as P

epsilon = 1e-05


def swapped(value, axis, bit):
    return lax.ppermute(value, axis, [(i, i ^ 1 << bit) for i in range(lax.axis_size(axis))])


def shifted(value, axis, steps):
    count = lax.axis_size(axis)
    initial, last = (max(0, -steps), min(count, count - steps))
    return lax.ppermute(value, axis, [(source, source + steps) for source in range(initial, last)])


def bit_span(differ, count):
    level_of = jnp.zeros_like(differ)
    for level_bit in range(count):
        level_of = level_of + (jnp.right_shift(differ, level_bit) > 0).astype(jnp.int32)
    return level_of


def on_device(
    seq_values, seq_gate, seq_keys, seq_queries, level_weights, skip_gain, norm_gain, out_weight
):
    tok_rows = seq_values.shape[0]
    width = seq_values.shape[1]
    head_count = skip_gain.shape[0]
    head_size = width // head_count
    local_bits = tok_rows.bit_length() - 1
    ctx_size = lax.axis_size("ctx")
    far_levels = ctx_size.bit_length() - 1
    weights = level_weights.astype(jnp.float32)
    places = jnp.arange(tok_rows, dtype=jnp.int32)
    differ = jnp.bitwise_xor(places[:, None], places[None, :])
    level_of = bit_span(differ, local_bits)
    causal = places[None, :] <= places[:, None]
    onehot = (
        (level_of[None] == jnp.arange(local_bits + 1, dtype=jnp.int32)[:, None, None])
        & causal[None]
    ).astype(jnp.float32)
    mixing = jnp.einsum(
        "lht,lts->hts", weights[: local_bits + 1], onehot, precision=lax.Precision.HIGHEST
    )
    scores = jnp.dot(seq_queries, seq_keys.T, preferred_element_type=jnp.float32)
    weighted = (mixing * scores[None]).astype(jnp.bfloat16)
    value_heads = seq_values.reshape(tok_rows, head_count, head_size)
    mixed = jnp.einsum("hts,shp->thp", weighted, value_heads, preferred_element_type=jnp.float32)
    mixed = mixed + skip_gain[None, :, None] * value_heads.astype(jnp.float32)
    states = jnp.dot(seq_keys.T, seq_values, preferred_element_type=jnp.float32)
    query_f32 = seq_queries.astype(jnp.float32)
    my_index = lax.axis_index("ctx")

    def read_level(mixed_in, level_state, level_bit):
        is_upper = jnp.bitwise_and(jnp.right_shift(my_index, level_bit), 1).astype(jnp.float32)
        readout = jnp.dot(query_f32, level_state, precision=lax.Precision.HIGHEST).reshape(
            tok_rows, head_count, head_size
        )
        scale_t = weights[local_bits + 1 + level_bit].T * is_upper
        return mixed_in + scale_t[:, :, None] * readout

    for level_bit in range(far_levels - 1):
        received = swapped(states, "ctx", level_bit)
        mixed = read_level(mixed, received, level_bit)
        states = states + received
    top_bit = far_levels - 1
    received = shifted(states, "ctx", 1 << top_bit)
    mixed = read_level(mixed, received, top_bit)
    gated = mixed.reshape(tok_rows, width) * jax.nn.silu(seq_gate.astype(jnp.float32))
    mean_sq = jnp.mean(gated * gated, axis=1, keepdims=True)
    normed = (gated * lax.rsqrt(mean_sq + epsilon) * norm_gain[None, :]).astype(jnp.bfloat16)
    partial_out = jnp.dot(
        normed,
        lax.all_gather(out_weight, "ctx", axis=1, tiled=True),
        preferred_element_type=jnp.float32,
    )
    result = lax.psum_scatter(partial_out, "head", scatter_dimension=1, tiled=True)
    return result.astype(jnp.bfloat16)


def solution(mesh):
    placed = (
        P(("rep", "ctx"), "head"),
        P(("rep", "ctx"), "head"),
        P(("rep", "ctx"), None),
        P(("rep", "ctx"), None),
        P(None, "head", ("rep", "ctx")),
        P("head"),
        P("head"),
        P("head", "ctx"),
    )
    return jax.shard_map(
        on_device, mesh=mesh, in_specs=placed, out_specs=P(("rep", "ctx"), "head"), check_vma=False
    )
```

profile of v0, /device:TPU:1, one launch (start us, length us, event | category | flops | bytes accessed | tf_op | source)
XLA Modules:
  0.0 827.2 jit_solution(14411478515072317287)
XLA Ops:
  8.9 4.0 collective-permute-start
  12.9 18.6 %collective-permute-done = f32[128,2048]{1,0:T(8,128)S(1)} collective-permute-done((f32[128,2048]{1,0:T(8,128)S(1)}, f32[128,2048]{1,0:T(8,128)S(1)}, u32[]{:S(2)}, u32[]{:S(2)}) %collective-permute-start) | collective-permute-done | bytes 1048608 | tf_op jit(solution)/shard_map/ppermute | solution.py:10
  31.7 9.9 %collective-permute-start.1 = (f32[128,2048]{1,0:T(8,128)S(1)}, f32[128,2048]{1,0:T(8,128)S(1)}, u32[]{:S(2)}, u32[]{:S(2)}) collective-permute-start(f32[128,2048]{1,0:T(8,128)S(1)} %add.117), channel_id=1, source_target_pairs={{0,8},{4,12},{8,0},{12,4},{16,24},{20,28},{24,16},{28,20},{32,40},... | collective-permute-start | bytes 3145736 | tf_op jit(solution)/shard_map/ppermute | solution.py:10
  41.6 50.3 %collective-permute-done.1 = f32[128,2048]{1,0:T(8,128)S(1)} collective-permute-done((f32[128,2048]{1,0:T(8,128)S(1)}, f32[128,2048]{1,0:T(8,128)S(1)}, u32[]{:S(2)}, u32[]{:S(2)}) %collective-permute-start.1) | collective-permute-done | bytes 1048608 | tf_op jit(solution)/shard_map/ppermute | solution.py:10
  92.1 9.3 %collective-permute-start.2 = (f32[128,2048]{1,0:T(8,128)S(1)}, f32[128,2048]{1,0:T(8,128)S(1)}, u32[]{:S(2)}, u32[]{:S(2)}) collective-permute-start(f32[128,2048]{1,0:T(8,128)S(1)} %add.119), channel_id=1, source_target_pairs={{0,16},{4,20},{8,24},{12,28},{16,0},{20,4},{24,8},{28,12},{32,48},... | collective-permute-start | bytes 3145736 | tf_op jit(solution)/shard_map/ppermute | solution.py:10
  101.4 50.0 %collective-permute-done.2 = f32[128,2048]{1,0:T(8,128)S(1)} collective-permute-done((f32[128,2048]{1,0:T(8,128)S(1)}, f32[128,2048]{1,0:T(8,128)S(1)}, u32[]{:S(2)}, u32[]{:S(2)}) %collective-permute-start.2) | collective-permute-done | bytes 1048608 | tf_op jit(solution)/shard_map/ppermute | solution.py:10
  152.5 3.8 collective-permute-start.3
  159.4 2.8 copy.12
  163.3 18.1 %collective-permute-done.3 = f32[128,2048]{1,0:T(8,128)} collective-permute-done((f32[128,2048]{1,0:T(8,128)}, f32[128,2048]{1,0:T(8,128)}, u32[]{:S(2)}, u32[]{:S(2)}) %collective-permute-start.3) | collective-permute-done | bytes 1048608 | tf_op jit(solution)/shard_map/ppermute | solution.py:10
  183.1 7.2 collective-permute-start.4
  192.5 24.9 %collective-permute-done.4 = f32[128,2048]{1,0:T(8,128)S(1)} collective-permute-done((f32[128,2048]{1,0:T(8,128)S(1)}, f32[128,2048]{1,0:T(8,128)S(1)}, u32[]{:S(2)}, u32[]{:S(2)}) %collective-permute-start.4) | collective-permute-done | bytes 1048608 | tf_op jit(solution)/shard_map/ppermute | solution.py:10
  217.5 5.5 collective-permute-start.5
  223.0 6.1 fusion.2
  231.4 12.1 %collective-permute-done.5 = f32[128,2048]{1,0:T(8,128)S(1)} collective-permute-done((f32[128,2048]{1,0:T(8,128)S(1)}, f32[128,2048]{1,0:T(8,128)S(1)}, u32[]{:S(2)}, u32[]{:S(2)}) %collective-permute-start.5) | collective-permute-done | bytes 1048608 | tf_op jit(solution)/shard_map/ppermute | solution.py:10
  243.6 4.0 collective-permute-start.6
  248.7 2.3 fusion.35
  253.0 12.9 %collective-permute-done.6 = f32[128,2048]{1,0:T(8,128)S(1)} collective-permute-done((f32[128,2048]{1,0:T(8,128)S(1)}, f32[128,2048]{1,0:T(8,128)S(1)}, u32[]{:S(2)}, u32[]{:S(2)}) %collective-permute-start.6) | collective-permute-done | bytes 1048608 | tf_op jit(solution)/shard_map/ppermute | solution.py:16
  265.9 2.4 fusion.38
  268.3 6.2 fusion.18
  274.5 2.0 copy.10
  277.3 391.4 %all-gather.2.cloned.1.call-done = bf16[2048,2048]{0,1:T(8,128)(2,1)} async-done(((bf16[2048,16]{0,1:T(8,128)(2,1)}), bf16[2048,2048]{0,1:T(8,128)(2,1)}) %all-gather.2.cloned.1.call-update) | async-done | bytes 8388624 | tf_op jit(solution)/shard_map/all_gather | solution.py:77
  668.7 7.4 fusion.19
  676.1 142.2 %reduce-scatter.2.cloned.1.call-done = f32[256,1024]{1,0:T(8,128)} async-done(((f32[256,2048]{1,0:T(8,128)}), f32[256,1024]{1,0:T(8,128)}) %reduce-scatter.2.cloned.1.call-update) | async-done | bytes 1048592 | tf_op jit(solution)/shard_map/reduce_scatter | solution.py:80
  818.3 2.1 convert_element_type.121
  (45 shorter events, 18.0 us)
Async XLA Ops:
  6.5 183.8 %copy-start = (bf16[256,128]{1,0:T(8,128)(2,1)S(1)}, bf16[256,128]{1,0:T(8,128)(2,1)}, u32[]{:S(2)}) copy-start(bf16[256,128]{1,0:T(8,128)(2,1)} %param.11) | copy-start | bytes 196612
  6.5 662.1 %all-gather.2.cloned.1.call-start = ((), (), s32[]{:S(2)}) async-start(), calls=%async_computation.1 | async-start | bytes 8454144 | tf_op jit(solution)/shard_map/all_gather | solution.py:77
  7.3 811.0 %reduce-scatter.2.cloned.1.call-start = ((), (), s32[]{:S(2)}) async-start(), calls=%async_computation.2 | async-start | bytes 3145728 | tf_op jit(solution)/shard_map/reduce_scatter | solution.py:80
  8.9 22.6 %collective-permute-start = (f32[128,2048]{1,0:T(8,128)S(1)}, f32[128,2048]{1,0:T(8,128)S(1)}, u32[]{:S(2)}, u32[]{:S(2)}) collective-permute-start(f32[128,2048]{1,0:T(8,128)S(1)} %fusion.31), channel_id=1, source_target_pairs={{0,4},{4,0},{8,12},{12,8},{16,20},{20,16},{24,28},{28,24},{32,36},... | collective-permute-start | bytes 3145736 | tf_op jit(solution)/shard_map/ppermute | solution.py:10
  31.7 60.3 %collective-permute-start.1 = (f32[128,2048]{1,0:T(8,128)S(1)}, f32[128,2048]{1,0:T(8,128)S(1)}, u32[]{:S(2)}, u32[]{:S(2)}) collective-permute-start(f32[128,2048]{1,0:T(8,128)S(1)} %add.117), channel_id=1, source_target_pairs={{0,8},{4,12},{8,0},{12,4},{16,24},{20,28},{24,16},{28,20},{32,40},... | collective-permute-start | bytes 3145736 | tf_op jit(solution)/shard_map/ppermute | solution.py:10
  91.9 60.6 %copy-start.1 = (f32[128,2048]{1,0:T(8,128)}, f32[128,2048]{1,0:T(8,128)S(1)}, u32[]{:S(2)}) copy-start(f32[128,2048]{1,0:T(8,128)S(1)} %collective-permute-done.1) | copy-start | bytes 3145732
  92.1 65.8 %copy-start.5 = (bf16[16,32,256]{2,1,0:T(8,128)(2,1)S(1)}, bf16[16,32,256]{2,1,0:T(8,128)(2,1)}, u32[]{:S(2)}) copy-start(bf16[16,32,256]{2,1,0:T(8,128)(2,1)} %param.12) | copy-start | bytes 786436
  92.1 59.3 %collective-permute-start.2 = (f32[128,2048]{1,0:T(8,128)S(1)}, f32[128,2048]{1,0:T(8,128)S(1)}, u32[]{:S(2)}, u32[]{:S(2)}) collective-permute-start(f32[128,2048]{1,0:T(8,128)S(1)} %add.119), channel_id=1, source_target_pairs={{0,16},{4,20},{8,24},{12,28},{16,0},{20,4},{24,8},{28,12},{32,48},... | collective-permute-start | bytes 3145736 | tf_op jit(solution)/shard_map/ppermute | solution.py:10
  152.5 28.8 %collective-permute-start.3 = (f32[128,2048]{1,0:T(8,128)}, f32[128,2048]{1,0:T(8,128)}, u32[]{:S(2)}, u32[]{:S(2)}) collective-permute-start(f32[128,2048]{1,0:T(8,128)} %add.121), channel_id=1, source_target_pairs={{0,32},{4,36},{8,40},{12,44},{16,48},{20,52},{24,56},{28,60},{32,0... | collective-permute-start | bytes 3145736 | tf_op jit(solution)/shard_map/ppermute | solution.py:10
  162.1 28.2 %copy-start.6 = (bf16[256,128]{1,0:T(8,128)(2,1)S(1)}, bf16[256,128]{1,0:T(8,128)(2,1)}, u32[]{:S(2)}) copy-start(bf16[256,128]{1,0:T(8,128)(2,1)} %param.10) | copy-start | bytes 196612
  163.3 27.6 %copy-start.3 = (bf16[9,32,256]{1,0,2:T(8,128)(2,1)S(1)}, bf16[9,32,256]{1,0,2:T(8,128)(2,1)}, u32[]{:S(2)}) copy-start(bf16[9,32,256]{1,0,2:T(8,128)(2,1)} %copy.12) | copy-start | bytes 442372
  183.1 34.3 %collective-permute-start.4 = (f32[128,2048]{1,0:T(8,128)S(1)}, f32[128,2048]{1,0:T(8,128)S(1)}, u32[]{:S(2)}, u32[]{:S(2)}) collective-permute-start(f32[128,2048]{1,0:T(8,128)S(1)} %add.123), channel_id=1, source_target_pairs={{0,64},{4,68},{8,72},{12,76},{16,80},{20,84},{24,88},{28,92},{32,9... | collective-permute-start | bytes 3145736 | tf_op jit(solution)/shard_map/ppermute | solution.py:10
  217.5 26.0 %collective-permute-start.5 = (f32[128,2048]{1,0:T(8,128)S(1)}, f32[128,2048]{1,0:T(8,128)S(1)}, u32[]{:S(2)}, u32[]{:S(2)}) collective-permute-start(f32[128,2048]{1,0:T(8,128)S(1)} %add.125), channel_id=1, source_target_pairs={{0,128},{4,132},{8,136},{12,140},{16,144},{20,148},{24,152},{28,15... | collective-permute-start | bytes 3145736 | tf_op jit(solution)/shard_map/ppermute | solution.py:10
  229.1 1.2 copy-start.2
  243.6 22.3 %collective-permute-start.6 = (f32[128,2048]{1,0:T(8,128)S(1)}, f32[128,2048]{1,0:T(8,128)S(1)}, u32[]{:S(2)}, u32[]{:S(2)}) collective-permute-start(f32[128,2048]{1,0:T(8,128)S(1)} %add.127), channel_id=1, source_target_pairs={{0,256},{4,260},{8,264},{12,268},{16,272},{20,276},{24,280},{28,28... | collective-permute-start | bytes 3145736 | tf_op jit(solution)/shard_map/ppermute | solution.py:16
  253.0 15.3 %copy-start.7 = (f32[32]{0:T(128)S(1)}, f32[32]{0:T(128)}, u32[]{:S(2)}) copy-start(f32[32]{0:T(128)} %param.13) | copy-start | bytes 388
  274.5 2.0 copy-start.4
  276.5 392.2 %copy-start.8 = (f32[2048]{0:T(1024)S(1)}, f32[2048]{0:T(1024)}, u32[]{:S(2)}) copy-start(f32[2048]{0:T(1024)} %param.14) | copy-start | bytes 24580
Sparse Core Ops, SparseCore 0:
  9.4 659.1 all-gather.1
  676.2 142.0 reduce-scatter.1
where the time goes:
time: 828 us; the launch traced here: 827 us
  waiting for transfers between devices  721 us (87%)
  starting transfers between devices  43.8 us (5%)
  matrix products  26.6 us (3%)
  other arithmetic  14.7 us (2%)
  between operations  13.7 us (2%)
    all_gather x1, waiting for transfers between devices, on_device(): lax.all_gather(out_weight, 'ctx', axis=1, tiled=True)  391 us
    ppermute x6, waiting for transfers between devices, swapped(): lax.ppermute(value, axis, [(i, i ^ 1 << bit) for i in range(lax.axis_size...  174 us
    reduce_scatter x1, waiting for transfers between devices, on_device(): lax.psum_scatter(partial_out, 'head', scatter_dimension=1, tiled=True)  142 us
    ppermute x6, starting transfers between devices, swapped(): lax.ppermute(value, axis, [(i, i ^ 1 << bit) for i in range(lax.axis_size...  39.8 us
  transfers between devices with their start and end apart: 9, of which 9 were waited for; matrix products, arithmetic and copies ran while one was open for 5% of the time, Pallas kernels for 0%

commit v1 on v0

v1 whole, which is shorter than its diff:
```python
import functools

import jax
import jax.numpy as jnp
from jax import lax
from jax.experimental import pallas as pl
from jax.experimental.pallas import tpu as pltpu
from jax.sharding import Mesh, PartitionSpec as P

epsilon = 1e-05
LOCAL_LEVELS = 9
NN = (((1,), (0,)), ((), ()))
NT = (((1,), (1,)), ((), ()))
f32 = jnp.float32
bf16 = jnp.bfloat16


def params(mib, steps=1):
    return pltpu.CompilerParams(
        vmem_limit_bytes=mib * 2**20, dimension_semantics=("arbitrary",) * steps
    )


def cost(flops, moved):
    return pl.CostEstimate(flops=flops, bytes_accessed=moved, transcendentals=0)


def swapped(value, axis, mask):
    return lax.ppermute(value, axis, [(i, i ^ mask) for i in range(lax.axis_size(axis))])


def dot(a, b, dims):
    return lax.dot_general(a, b, dims, preferred_element_type=f32)


def state_kernel(values_ref, keys_ref, vt_ref, st_ref, sb_ref):
    vt = values_ref[...].T
    vt_ref[...] = vt
    st = dot(vt, keys_ref[...], NN)
    st_ref[...] = st
    sb_ref[...] = st.astype(bf16)


def own_state(values, keys, chunk, chunks):
    tok, width = values.shape
    cols = width // chunks
    n = keys.shape[1]
    return pl.pallas_call(
        state_kernel,
        grid=(1,),
        in_specs=[
            pl.BlockSpec((tok, cols), lambda i: (0, chunk)),
            pl.BlockSpec((tok, n), lambda i: (0, 0)),
        ],
        out_specs=[
            pl.BlockSpec((cols, tok), lambda i: (0, 0)),
            pl.BlockSpec((cols, n), lambda i: (0, 0)),
            pl.BlockSpec((cols, n), lambda i: (0, 0)),
        ],
        out_shape=[
            jax.ShapeDtypeStruct((cols, tok), bf16),
            jax.ShapeDtypeStruct((cols, n), f32),
            jax.ShapeDtypeStruct((cols, n), bf16),
        ],
        compiler_params=params(24),
        cost_estimate=cost(2 * tok * cols * n, 4 * tok * cols),
        name="own_state",
    )(values, keys)


def local_kernel(heads, half, skip_ref, vt_ref, gate_ref, keys_ref, query_ref, w_ref, acc_ref, silu_ref, score_ref):
    size = vt_ref.shape[0] // heads
    first = pl.program_id(0) * heads

    @pl.when(pl.program_id(0) == 0)
    def _():
        scores = dot(keys_ref[...], query_ref[...], NT)
        s = lax.broadcasted_iota(jnp.int32, scores.shape, 0)
        t = lax.broadcasted_iota(jnp.int32, scores.shape, 1)
        score_ref[...] = jnp.where(s <= t, scores, 0.0)

    gate = gate_ref[...].astype(f32)
    silu_ref[...] = (gate / (1.0 + jnp.exp(-gate))).T

    s = lax.broadcasted_iota(jnp.int32, (half, half), 0)
    t = lax.broadcasted_iota(jnp.int32, (half, half), 1)
    differ = s ^ t
    low = score_ref[:half, :half]
    cross = score_ref[:half, half:]
    high = score_ref[half:, half:]
    for h in range(heads):
        w = w_ref[:, h, :].astype(f32)

        def mix(level, lo):
            return jnp.broadcast_to(w[level : level + 1, lo : lo + half], (half, half))

        def diagonal(lo, scores):
            m = mix(0, lo)
            for level in range(1, LOCAL_LEVELS - 1):
                m = jnp.where(differ >= (1 << (level - 1)), mix(level, lo), m)
            return (m * scores).astype(bf16)

        vt = vt_ref[h * size : (h + 1) * size, :]
        skip = skip_ref[first + h]
        near = dot(vt[:, :half], diagonal(0, low), NN)
        right = jnp.concatenate(
            [(mix(LOCAL_LEVELS - 1, half) * cross).astype(bf16), diagonal(half, high)], axis=0
        )
        far = dot(vt, right, NN)
        rows = slice(h * size, (h + 1) * size)
        acc_ref[rows, :half] = near + skip * vt[:, :half].astype(f32)
        acc_ref[rows, half:] = far + skip * vt[:, half:].astype(f32)


def local_part(vt, gate, keys, query, weights, skip, chunk, head_size):
    cols, tok = vt.shape
    n = keys.shape[1]
    heads = 8
    rows = heads * head_size
    steps = cols // rows
    return pl.pallas_call(
        functools.partial(local_kernel, heads, tok // 2),
        grid=(steps,),
        in_specs=[
            pl.BlockSpec(memory_space=pltpu.SMEM),
            pl.BlockSpec((rows, tok), lambda i: (i, 0)),
            pl.BlockSpec((tok, rows), lambda i: (0, chunk * steps + i)),
            pl.BlockSpec((tok, n), lambda i: (0, 0)),
            pl.BlockSpec((tok, n), lambda i: (0, 0)),
            pl.BlockSpec((16, heads, tok), lambda i: (0, chunk * steps + i, 0)),
        ],
        out_specs=[
            pl.BlockSpec((rows, tok), lambda i: (i, 0)),
            pl.BlockSpec((rows, tok), lambda i: (i, 0)),
        ],
        out_shape=[jax.ShapeDtypeStruct((cols, tok), f32)] * 2,
        scratch_shapes=[pltpu.VMEM((tok, tok), f32)],
        compiler_params=params(24),
        cost_estimate=cost(8 * tok * tok * cols, 12 * tok * cols),
        name="local_part",
    )(skip[chunk * steps * heads : (chunk + 1) * steps * heads], vt, gate, keys, query, weights)


def read_levels(acc, states, weights, query):
    heads = weights.shape[1]
    rows, tok = acc.shape
    size = rows // heads
    for level, state in enumerate(states):
        part = dot(state, query, NT).reshape(heads, size, tok)
        acc = acc + (part * weights[level][:, None, :]).reshape(rows, tok)
    return acc


def far_kernel(count, *refs):
    states = [ref[...] for ref in refs[:count]]
    acc_ref, query_ref, w_ref, out_ref = refs[count:]
    out_ref[...] = read_levels(acc_ref[...], states, w_ref[...].astype(f32), query_ref[...])


def far_part(acc, states, weights, query, head_size):
    cols, tok = acc.shape
    n = query.shape[1]
    heads = 8
    rows = heads * head_size
    count = len(states)
    return pl.pallas_call(
        functools.partial(far_kernel, count),
        grid=(cols // rows,),
        in_specs=[pl.BlockSpec((rows, n), lambda i: (i, 0))] * count
        + [
            pl.BlockSpec((rows, tok), lambda i: (i, 0)),
            pl.BlockSpec((tok, n), lambda i: (0, 0)),
            pl.BlockSpec((count, heads, tok), lambda i: (0, i, 0)),
        ],
        out_specs=pl.BlockSpec((rows, tok), lambda i: (i, 0)),
        out_shape=jax.ShapeDtypeStruct((cols, tok), f32),
        compiler_params=params(24),
        cost_estimate=cost(2 * count * cols * n * tok, 8 * cols * tok),
        name="far_part",
    )(*states, acc, query, weights)


def project(where_ref, pieces, normed_ref, out_ref):
    mine = where_ref[1]
    half = normed_ref.shape[1]
    width = pieces[0].shape[1]
    for k in range(len(pieces) // 2):
        block = dot(pieces[2 * k][0], normed_ref[mine], NN)
        block = block + dot(pieces[2 * k + 1][0], normed_ref[1 - mine], NN)
        at = pl.multiple_of((where_ref[0] ^ k) * width, width)
        out_ref[:, pl.ds(at, width)] = block.T.astype(out_ref.dtype)


def finish_kernel(where_ref, *refs):
    pieces = refs[:8]
    acc_refs, silu_refs, state_refs = refs[8:10], refs[10:12], refs[12:14]
    w_ref, query_ref, gain_ref = refs[14:17]
    out_ref, normed_ref = refs[17:19]

    @pl.when(pl.program_id(0) == 0)
    def _():
        rows, tok = acc_refs[0].shape
        heads = w_ref.shape[1] // 2
        squares = jnp.zeros((1, tok), f32)
        gated = []
        for c in range(2):
            w = w_ref[:, c * heads : (c + 1) * heads, :].astype(f32)
            mixed = read_levels(acc_refs[c][...], [state_refs[c][...]], w, query_ref[...])
            part = mixed * silu_refs[c][...]
            squares = squares + jnp.sum(part * part, axis=0, keepdims=True)
            gated.append(part)
        scale = lax.rsqrt(squares / (2 * rows) + epsilon)
        for c in range(2):
            gain = gain_ref[c * rows : (c + 1) * rows, :]
            normed_ref[c] = (gated[c] * scale * gain).astype(bf16)

    project(where_ref, pieces, normed_ref, out_ref)


def keep_kernel(where_ref, *refs):
    project(where_ref, refs[:8], refs[8], refs[9])


def piece_specs(pieces, offset):
    _, cols, depth = pieces[0].shape
    return [
        pl.BlockSpec((1, cols, depth), lambda i, where: (where[offset] + i, 0, 0)) for _ in pieces
    ]


def finish(where, pieces, accs, silus, states, weights, query, gain):
    rows, tok = accs[0].shape
    z_size, cols, depth = pieces[0].shape
    steps = z_size // 2
    wide = cols * len(pieces) // 2

    def whole(array):
        return pl.BlockSpec(array.shape, lambda i, where: (0,) * array.ndim)

    others = [*accs, *silus, *states, weights, query, gain]
    return pl.pallas_call(
        finish_kernel,
        grid_spec=pltpu.PrefetchScalarGridSpec(
            num_scalar_prefetch=1,
            grid=(steps,),
            in_specs=piece_specs(pieces, 2) + [whole(a) for a in others],
            out_specs=[
                pl.BlockSpec((tok, wide), lambda i, where: (0, i)),
                pl.BlockSpec((2, rows, tok), lambda i, where: (0, 0, 0)),
            ],
        ),
        out_shape=[
            jax.ShapeDtypeStruct((tok, wide * steps), bf16),
            jax.ShapeDtypeStruct((2, rows, tok), bf16),
        ],
        compiler_params=params(40),
        cost_estimate=cost(2 * tok * 2 * rows * wide * steps, 16 * 2**20),
        name="finish",
    )(where, *pieces, *others)


def keep(where, pieces, normed):
    _, rows, tok = normed.shape
    z_size, cols, depth = pieces[0].shape
    steps = z_size // 2
    wide = cols * len(pieces) // 2
    return pl.pallas_call(
        keep_kernel,
        grid_spec=pltpu.PrefetchScalarGridSpec(
            num_scalar_prefetch=1,
            grid=(steps,),
            in_specs=piece_specs(pieces, 3)
            + [pl.BlockSpec((2, rows, tok), lambda i, where: (0, 0, 0))],
            out_specs=pl.BlockSpec((tok, wide), lambda i, where: (0, i)),
        ),
        out_shape=jax.ShapeDtypeStruct((tok, wide * steps), f32),
        compiler_params=params(40),
        cost_estimate=cost(2 * tok * 2 * rows * wide * steps, 8 * 2**20),
        name="keep",
    )(where, *pieces, normed)


def gathered_weight(out_weight):
    z_size, y_size = lax.axis_size("zl"), lax.axis_size("y")
    rows, cols = out_weight.shape
    mine = lax.axis_index("rep")
    half = lax.dynamic_slice_in_dim(out_weight, mine * (rows // 2), rows // 2, 0).T
    spread = jnp.broadcast_to(half[None], (z_size * y_size, cols, rows // 2))
    got = lax.all_to_all(spread, ("zl", "y"), 0, 0, tiled=True)
    own = got.reshape(z_size, y_size * cols, rows // 2)
    pieces = []
    for k in range(lax.axis_size("x")):
        piece = own if k == 0 else swapped(own, "x", k)
        pieces += [piece, swapped(piece, "rep", 1)]
    return pieces


def on_device(
    seq_values, seq_gate, seq_keys, seq_queries, level_weights, skip_gain, norm_gain, out_weight
):
    width = seq_values.shape[1]
    head_count = skip_gain.shape[0]
    head_size = width // head_count
    chunks = 2
    chunk_heads = head_count // chunks
    axes = [("y", b) for b in range(3)] + [("x", b) for b in range(2)] + [("zl", b) for b in range(2)]
    uppers = jnp.stack([(lax.axis_index(a) >> b) & 1 for a, b in axes])
    far_weights = level_weights[LOCAL_LEVELS:] * uppers[:, None, None].astype(bf16)

    pieces = gathered_weight(out_weight)

    accs, silus, tops = [], [], []
    for c in range(chunks):
        vt, state, sent = own_state(seq_values, seq_keys, c, chunks)
        acc, silu = local_part(vt, seq_gate, seq_keys, seq_queries, level_weights, skip_gain, c, head_size)
        received = []
        for axis, bit in axes[:-1]:
            got = swapped(sent, axis, 1 << bit)
            received.append(got)
            state = state + got.astype(f32)
            sent = state.astype(bf16)
        axis, bit = axes[-1]
        step = 1 << bit
        top = lax.ppermute(sent, axis, [(i, i + step) for i in range(lax.axis_size(axis) - step)])
        heads = slice(c * chunk_heads, (c + 1) * chunk_heads)
        acc = far_part(acc, received[:3], far_weights[:3, heads], seq_queries, head_size)
        acc = far_part(acc, received[3:], far_weights[3:6, heads], seq_queries, head_size)
        accs.append(acc)
        silus.append(silu)
        tops.append(top)

    head = lax.axis_index("head")
    z_half = lax.axis_size("zl") // 2
    where = jnp.stack(
        [lax.axis_index("x"), lax.axis_index("rep"), (1 - head) * z_half, head * z_half]
    ).astype(jnp.int32)
    to_send, normed = finish(
        where, pieces, accs, silus, tops, far_weights[6:], seq_queries, norm_gain[:, None]
    )
    got = swapped(to_send, "head", 1)
    kept = keep(where, pieces, normed)
    return (kept + got.astype(f32)).astype(bf16)


def solution(mesh):
    grid = Mesh(mesh.devices.reshape(4, 4, 8, 2, 2), ("zl", "x", "y", "head", "rep"))
    ctx = ("zl", "x", "y")
    tokens = ("rep", *ctx)
    placed = (
        P(tokens, "head"),
        P(tokens, "head"),
        P(tokens, None),
        P(tokens, None),
        P(None, "head", tokens),
        P("head"),
        P("head"),
        P("head", ctx),
    )
    return jax.shard_map(
        on_device, mesh=grid, in_specs=placed, out_specs=P(tokens, "head"), check_vma=False
    )
```

time: 828 us -> 267 us (0.32)
  the two profiles are of different devices: /device:TPU:1 before, /device:TPU:220 now
where the time goes in v1:
time: 267 us; the launch traced here: 266 us
  waiting for transfers between devices  121 us (45%)
  starting transfers between devices  101 us (38%)
  Pallas kernels  21.8 us (8%)
  other arithmetic  11.9 us (4%)
  local copies, waits for them, and re-layouts  10.3 us (4%)
    ppermute x20, waiting for transfers between devices, swapped(): lax.ppermute(value, axis, [(i, i ^ mask) for i in range(lax.axis_size(axi...  104 us
    ppermute x20, starting transfers between devices, swapped(): lax.ppermute(value, axis, [(i, i ^ mask) for i in range(lax.axis_size(axi...  87.6 us
    ppermute x2, waiting for transfers between devices, on_device(): lax.ppermute(sent, axis, [(i, i + step) for i in range(lax.axis_size(axis...  16.5 us
    all_to_all x1, starting transfers between devices, gathered_weight(): got = lax.all_to_all(spread, ('zl', 'y'), 0, 0, tiled=True)  10.4 us
    convert_element_type x12, other arithmetic, on_device(): sent = state.astype(bf16)  8.74 us
    unnamed x70, local copies, waits for them, and re-layouts  7.56 us
    pallas_call x1, Pallas kernels, finish(): pl.pallas_call(finish_kernel, grid_spec=pltpu.PrefetchScalarGridSpec(num_...  5.8 us
  transfers between devices with their start and end apart: 23, of which 10 were waited for; matrix products, arithmetic and copies ran while one was open for 5% of the time, Pallas kernels for 6%

profile of v1, /device:TPU:220, one launch (start us, length us, event | category | flops | bytes accessed | tf_op | source)
XLA Modules:
  0.0 266.1 jit_solution(996661993538419119)
XLA Ops:
  2.0 10.4 %all-to-all-start = ((bf16[32,16,1024]{2,1,0:T(8,128)(2,1)}), bf16[32,16,1024]{2,1,0:T(8,128)(2,1)S(1)}, u32[]{:S(2)}, u32[]{:S(2)}) async-start(bf16[32,16,1024]{2,1,0:T(8,128)(2,1)} %broadcast_in_dim.4), calls=%async_computation | async-start | bytes 2097152 | tf_op jit(solution)/shard_map/all_to_all | solution.py:289
  18.6 3.4 %collective-permute-start.7 = (bf16[1024,128]{1,0:T(8,128)(2,1)}, bf16[1024,128]{1,0:T(8,128)(2,1)S(1)}, u32[]{:S(2)}, u32[]{:S(2)}) collective-permute-start(bf16[1024,128]{1,0:T(8,128)(2,1)} %get-tuple-element.18), channel_id=1, source_target_pairs={{0,4},{4,0},{8,12},{12,8},{16,20},{20,16},{24,28},{28,24},{1,5},{5... | collective-permute-start | bytes 786440 | tf_op jit(solution)/shard_map/ppermute | solution.py:29
  22.1 19.6 %collective-permute-done.13.refs_0_ = bf16[1024,128]{1,0:T(8,128)(2,1)S(1)} collective-permute-done((bf16[1024,128]{1,0:T(8,128)(2,1)}, bf16[1024,128]{1,0:T(8,128)(2,1)S(1)}, u32[]{:S(2)}, u32[]{:S(2)}) %collective-permute-start.13) | collective-permute-done | bytes 262176 | tf_op jit(solution)/shard_map/ppermute | solution.py:29
  41.9 3.4 %collective-permute-start.14 = (bf16[1024,128]{1,0:T(8,128)(2,1)S(1)}, bf16[1024,128]{1,0:T(8,128)(2,1)S(1)}, u32[]{:S(2)}, u32[]{:S(2)}) collective-permute-start(bf16[1024,128]{1,0:T(8,128)(2,1)S(1)} %fusion.3), channel_id=1, source_target_pairs={{0,8},{4,12},{8,0},{12,4},{16,24},{20,28},{24,16},{28,20},{1,9},{5... | collective-permute-start | bytes 786440 | tf_op jit(solution)/shard_map/ppermute | solution.py:29
  48.2 3.7 %collective-permute-start.8 = (bf16[1024,128]{1,0:T(8,128)(2,1)}, bf16[1024,128]{1,0:T(8,128)(2,1)S(1)}, u32[]{:S(2)}, u32[]{:S(2)}) collective-permute-start(bf16[1024,128]{1,0:T(8,128)(2,1)} %fusion), channel_id=1, source_target_pairs={{0,8},{4,12},{8,0},{12,4},{16,24},{20,28},{24,16},{28,20},{1,9},{5... | collective-permute-start | bytes 786440 | tf_op jit(solution)/shard_map/ppermute | solution.py:29
  51.9 11.9 %collective-permute-done.14.refs_1_ = bf16[1024,128]{1,0:T(8,128)(2,1)S(1)} collective-permute-done((bf16[1024,128]{1,0:T(8,128)(2,1)S(1)}, bf16[1024,128]{1,0:T(8,128)(2,1)S(1)}, u32[]{:S(2)}, u32[]{:S(2)}) %collective-permute-start.14) | collective-permute-done | bytes 262176 | tf_op jit(solution)/shard_map/ppermute | solution.py:29
  64.6 6.9 %collective-permute-start.15 = (bf16[1024,128]{1,0:T(8,128)(2,1)}, bf16[1024,128]{1,0:T(8,128)(2,1)S(1)}, u32[]{:S(2)}, u32[]{:S(2)}) collective-permute-start(bf16[1024,128]{1,0:T(8,128)(2,1)} %fusion.7), channel_id=1, source_target_pairs={{0,16},{4,20},{8,24},{12,28},{16,0},{20,4},{24,8},{28,12},{1,17},{... | collective-permute-start | bytes 786440 | tf_op jit(solution)/shard_map/ppermute | solution.py:29
  72.4 2.8 %collective-permute-start.9 = (bf16[1024,128]{1,0:T(8,128)(2,1)}, bf16[1024,128]{1,0:T(8,128)(2,1)}, u32[]{:S(2)}, u32[]{:S(2)}) collective-permute-start(bf16[1024,128]{1,0:T(8,128)(2,1)} %fusion.6), channel_id=1, source_target_pairs={{0,16},{4,20},{8,24},{12,28},{16,0},{20,4},{24,8},{28,12},{1,17},{... | collective-permute-start | bytes 786440 | tf_op jit(solution)/shard_map/ppermute | solution.py:29
  75.2 11.2 %collective-permute-done.15.refs_2_ = bf16[1024,128]{1,0:T(8,128)(2,1)S(1)} collective-permute-done((bf16[1024,128]{1,0:T(8,128)(2,1)}, bf16[1024,128]{1,0:T(8,128)(2,1)S(1)}, u32[]{:S(2)}, u32[]{:S(2)}) %collective-permute-start.15) | collective-permute-done | bytes 262176 | tf_op jit(solution)/shard_map/ppermute | solution.py:29
  87.2 3.1 %collective-permute-start.16 = (bf16[1024,128]{1,0:T(8,128)(2,1)}, bf16[1024,128]{1,0:T(8,128)(2,1)}, u32[]{:S(2)}, u32[]{:S(2)}) collective-permute-start(bf16[1024,128]{1,0:T(8,128)(2,1)} %fusion.4), channel_id=1, source_target_pairs={{0,32},{32,0},{64,96},{96,64},{1,33},{33,1},{65,97},{97,65},{2,34}... | collective-permute-start | bytes 786440 | tf_op jit(solution)/shard_map/ppermute | solution.py:29
  90.4 2.7 %collective-permute-start.1 = (bf16[4,128,1024]{2,1,0:T(8,128)(2,1)S(1)}, bf16[4,128,1024]{2,1,0:T(8,128)(2,1)}, u32[]{:S(2)}, u32[]{:S(2)}) collective-permute-start(bf16[4,128,1024]{2,1,0:T(8,128)(2,1)S(1)} %bitcast.15), channel_id=1, source_target_pairs={{0,32},{32,0},{64,96},{96,64},{1,33},{33,1},{65,97},{97,65},{2,34}... | collective-permute-start | bytes 3145736 | tf_op jit(solution)/shard_map/ppermute | solution.py:29
  95.5 4.1 %collective-permute-start.5 = (bf16[4,128,1024]{2,1,0:T(8,128)(2,1)S(1)}, bf16[4,128,1024]{2,1,0:T(8,128)(2,1)}, u32[]{:S(2)}, u32[]{:S(2)}) collective-permute-start(bf16[4,128,1024]{2,1,0:T(8,128)(2,1)S(1)} %bitcast.17), channel_id=1, source_target_pairs={{0,96},{32,64},{64,32},{96,0},{1,97},{33,65},{65,33},{97,1},{2,98}... | collective-permute-start | bytes 3145736 | tf_op jit(solution)/shard_map/ppermute | solution.py:29
  100.7 3.9 %collective-permute-start.10 = (bf16[1024,128]{1,0:T(8,128)(2,1)S(1)}, bf16[1024,128]{1,0:T(8,128)(2,1)S(1)}, u32[]{:S(2)}, u32[]{:S(2)}) collective-permute-start(bf16[1024,128]{1,0:T(8,128)(2,1)S(1)} %fusion.1), channel_id=1, source_target_pairs={{0,32},{32,0},{64,96},{96,64},{1,33},{33,1},{65,97},{97,65},{2,34}... | collective-permute-start | bytes 786440 | tf_op jit(solution)/shard_map/ppermute | solution.py:29
  107.7 40.0 %collective-permute-done.10.refs_0_ = bf16[1024,128]{1,0:T(8,128)(2,1)S(1)} collective-permute-done((bf16[1024,128]{1,0:T(8,128)(2,1)S(1)}, bf16[1024,128]{1,0:T(8,128)(2,1)S(1)}, u32[]{:S(2)}, u32[]{:S(2)}) %collective-permute-start.10) | collective-permute-done | bytes 262176 | tf_op jit(solution)/shard_map/ppermute | solution.py:29
  151.2 2.6 collective-permute-start.18
  154.4 4.3 %collective-permute-done.11.refs_1_ = bf16[1024,128]{1,0:T(8,128)(2,1)S(1)} collective-permute-done((bf16[1024,128]{1,0:T(8,128)(2,1)S(1)}, bf16[1024,128]{1,0:T(8,128)(2,1)S(1)}, u32[]{:S(2)}, u32[]{:S(2)}) %collective-permute-start.11) | collective-permute-done | bytes 262176 | tf_op jit(solution)/shard_map/ppermute | solution.py:29
  167.5 2.5 collective-permute-start.12
  174.7 3.0 %collective-permute-done.12.refs_2_ = bf16[1024,128]{1,0:T(8,128)(2,1)S(1)} collective-permute-done((bf16[1024,128]{1,0:T(8,128)(2,1)S(1)}, bf16[1024,128]{1,0:T(8,128)(2,1)S(1)}, u32[]{:S(2)}, u32[]{:S(2)}) %collective-permute-start.12) | collective-permute-done | bytes 262176 | tf_op jit(solution)/shard_map/ppermute | solution.py:29
  186.8 12.5 %collective-permute-done.20.refs_13_ = bf16[1024,128]{1,0:T(8,128)(2,1)S(1)} collective-permute-done((bf16[1024,128]{1,0:T(8,128)(2,1)}, bf16[1024,128]{1,0:T(8,128)(2,1)S(1)}, u32[]{:S(2)}, u32[]{:S(2)}) %collective-permute-start.20) | collective-permute-done | bytes 262176 | tf_op jit(solution)/shard_map/ppermute | solution.py:324
  206.2 4.1 %collective-permute-done.19.refs_12_ = bf16[1024,128]{1,0:T(8,128)(2,1)S(1)} collective-permute-done((bf16[1024,128]{1,0:T(8,128)(2,1)S(1)}, bf16[1024,128]{1,0:T(8,128)(2,1)S(1)}, u32[]{:S(2)}, u32[]{:S(2)}) %collective-permute-start.19) | collective-permute-done | bytes 262176 | tf_op jit(solution)/shard_map/ppermute | solution.py:324
  210.9 5.8 %finish.1 = (bf16[256,1024]{1,0:T(8,128)(2,1)S(1)}, bf16[2,1024,256]{2,1,0:T(8,128)(2,1)S(1)}) custom-call(s32[4]{0:T(128)S(1)} %copy-done.25, bf16[4,128,1024]{2,1,0:T(8,128)(2,1)S(1)} %bitcast.19, bf16[4,128,1024]{2,1,0:T(8,128)(2,1)} %collective-permute-done.refs_1_, bf16[4,128,1024]{2,1,0:T(8,128)(2,1)} %collective-permute-done.1.refs_2_, ...), custom_call_target="tpu_custom_call" | custom-call | flops 1073741824 | bytes 16777216 | tf_op jit(solution)/shard_map/finish/pallas_call | solution.py:241
  216.7 30.8 %collective-permute-start.21 = (bf16[256,1024]{1,0:T(8,128)(2,1)S(1)}, bf16[256,1024]{1,0:T(8,128)(2,1)S(1)}, u32[]{:S(2)}, u32[]{:S(2)}) collective-permute-start(bf16[256,1024]{1,0:T(8,128)(2,1)S(1)} %get-tuple-element.28), channel_id=1, source_target_pairs={{0,2},{2,0},{1,3},{3,1},{4,6},{6,4},{5,7},{7,5},{8,10},{10,8},{9,1... | collective-permute-start | bytes 1572872 | tf_op jit(solution)/shard_map/ppermute | solution.py:29
  247.6 3.9 %keep.1 = f32[256,1024]{1,0:T(8,128)S(1)} custom-call(s32[4]{0:T(128)S(1)} %copy-done.25, bf16[4,128,1024]{2,1,0:T(8,128)(2,1)S(1)} %bitcast.20, bf16[4,128,1024]{2,1,0:T(8,128)(2,1)} %collective-permute-done.refs_1_, bf16[4,128,1024]{2,1,0:T(8,128)(2,1)} %collective-permute-done.1.refs_2_, bf16[4,128,1024]{2,1,0:T(8,128)(2,1)} %collective-permute-done.2.refs_3_, ...), custom_call_target="tpu_custom_call" | custom-call | flops 1073741824 | bytes 8388608 | tf_op jit(solution)/shard_map/keep/pallas_call | solution.py:267
  251.5 13.6 %collective-permute-done.21 = bf16[256,1024]{1,0:T(8,128)(2,1)S(1)} collective-permute-done((bf16[256,1024]{1,0:T(8,128)(2,1)S(1)}, bf16[256,1024]{1,0:T(8,128)(2,1)S(1)}, u32[]{:S(2)}, u32[]{:S(2)}) %collective-permute-start.21) | collective-permute-done | bytes 524320 | tf_op jit(solution)/shard_map/ppermute | solution.py:29
  (124 shorter events, 55.1 us)
Async XLA Ops:
  2.0 88.4 %all-to-all-start = ((bf16[32,16,1024]{2,1,0:T(8,128)(2,1)}), bf16[32,16,1024]{2,1,0:T(8,128)(2,1)S(1)}, u32[]{:S(2)}, u32[]{:S(2)}) async-start(bf16[32,16,1024]{2,1,0:T(8,128)(2,1)} %broadcast_in_dim.4), calls=%async_computation | async-start | bytes 2097152 | tf_op jit(solution)/shard_map/all_to_all | solution.py:289
  14.3 27.5 %collective-permute-start.13 = (bf16[1024,128]{1,0:T(8,128)(2,1)}, bf16[1024,128]{1,0:T(8,128)(2,1)S(1)}, u32[]{:S(2)}, u32[]{:S(2)}) collective-permute-start(bf16[1024,128]{1,0:T(8,128)(2,1)} %get-tuple-element.22), channel_id=1, source_target_pairs={{0,4},{4,0},{8,12},{12,8},{16,20},{20,16},{24,28},{28,24},{1,5},{5... | collective-permute-start | bytes 786440 | tf_op jit(solution)/shard_map/ppermute | solution.py:29
  18.6 28.8 %collective-permute-start.7 = (bf16[1024,128]{1,0:T(8,128)(2,1)}, bf16[1024,128]{1,0:T(8,128)(2,1)S(1)}, u32[]{:S(2)}, u32[]{:S(2)}) collective-permute-start(bf16[1024,128]{1,0:T(8,128)(2,1)} %get-tuple-element.18), channel_id=1, source_target_pairs={{0,4},{4,0},{8,12},{12,8},{16,20},{20,16},{24,28},{28,24},{1,5},{5... | collective-permute-start | bytes 786440 | tf_op jit(solution)/shard_map/ppermute | solution.py:29
  41.9 21.9 %collective-permute-start.14 = (bf16[1024,128]{1,0:T(8,128)(2,1)S(1)}, bf16[1024,128]{1,0:T(8,128)(2,1)S(1)}, u32[]{:S(2)}, u32[]{:S(2)}) collective-permute-start(bf16[1024,128]{1,0:T(8,128)(2,1)S(1)} %fusion.3), channel_id=1, source_target_pairs={{0,8},{4,12},{8,0},{12,4},{16,24},{20,28},{24,16},{28,20},{1,9},{5... | collective-permute-start | bytes 786440 | tf_op jit(solution)/shard_map/ppermute | solution.py:29
  48.2 23.5 %collective-permute-start.8 = (bf16[1024,128]{1,0:T(8,128)(2,1)}, bf16[1024,128]{1,0:T(8,128)(2,1)S(1)}, u32[]{:S(2)}, u32[]{:S(2)}) collective-permute-start(bf16[1024,128]{1,0:T(8,128)(2,1)} %fusion), channel_id=1, source_target_pairs={{0,8},{4,12},{8,0},{12,4},{16,24},{20,28},{24,16},{28,20},{1,9},{5... | collective-permute-start | bytes 786440 | tf_op jit(solution)/shard_map/ppermute | solution.py:29
  64.6 21.8 %collective-permute-start.15 = (bf16[1024,128]{1,0:T(8,128)(2,1)}, bf16[1024,128]{1,0:T(8,128)(2,1)S(1)}, u32[]{:S(2)}, u32[]{:S(2)}) collective-permute-start(bf16[1024,128]{1,0:T(8,128)(2,1)} %fusion.7), channel_id=1, source_target_pairs={{0,16},{4,20},{8,24},{12,28},{16,0},{20,4},{24,8},{28,12},{1,17},{... | collective-permute-start | bytes 786440 | tf_op jit(solution)/shard_map/ppermute | solution.py:29
  72.4 27.2 %collective-permute-start.9 = (bf16[1024,128]{1,0:T(8,128)(2,1)}, bf16[1024,128]{1,0:T(8,128)(2,1)}, u32[]{:S(2)}, u32[]{:S(2)}) collective-permute-start(bf16[1024,128]{1,0:T(8,128)(2,1)} %fusion.6), channel_id=1, source_target_pairs={{0,16},{4,20},{8,24},{12,28},{16,0},{20,4},{24,8},{28,12},{1,17},{... | collective-permute-start | bytes 786440 | tf_op jit(solution)/shard_map/ppermute | solution.py:29
  87.2 17.4 %collective-permute-start.16 = (bf16[1024,128]{1,0:T(8,128)(2,1)}, bf16[1024,128]{1,0:T(8,128)(2,1)}, u32[]{:S(2)}, u32[]{:S(2)}) collective-permute-start(bf16[1024,128]{1,0:T(8,128)(2,1)} %fusion.4), channel_id=1, source_target_pairs={{0,32},{32,0},{64,96},{96,64},{1,33},{33,1},{65,97},{97,65},{2,34}... | collective-permute-start | bytes 786440 | tf_op jit(solution)/shard_map/ppermute | solution.py:29
  90.4 70.2 %collective-permute-start.1 = (bf16[4,128,1024]{2,1,0:T(8,128)(2,1)S(1)}, bf16[4,128,1024]{2,1,0:T(8,128)(2,1)}, u32[]{:S(2)}, u32[]{:S(2)}) collective-permute-start(bf16[4,128,1024]{2,1,0:T(8,128)(2,1)S(1)} %bitcast.15), channel_id=1, source_target_pairs={{0,32},{32,0},{64,96},{96,64},{1,33},{33,1},{65,97},{97,65},{2,34}... | collective-permute-start | bytes 3145736 | tf_op jit(solution)/shard_map/ppermute | solution.py:29
  93.1 69.9 %collective-permute-start.3 = (bf16[4,128,1024]{2,1,0:T(8,128)(2,1)S(1)}, bf16[4,128,1024]{2,1,0:T(8,128)(2,1)}, u32[]{:S(2)}, u32[]{:S(2)}) collective-permute-start(bf16[4,128,1024]{2,1,0:T(8,128)(2,1)S(1)} %bitcast.16), channel_id=1, source_target_pairs={{0,64},{32,96},{64,0},{96,32},{1,65},{33,97},{65,1},{97,33},{2,66}... | collective-permute-start | bytes 3145736 | tf_op jit(solution)/shard_map/ppermute | solution.py:29
  95.5 69.4 %collective-permute-start.5 = (bf16[4,128,1024]{2,1,0:T(8,128)(2,1)S(1)}, bf16[4,128,1024]{2,1,0:T(8,128)(2,1)}, u32[]{:S(2)}, u32[]{:S(2)}) collective-permute-start(bf16[4,128,1024]{2,1,0:T(8,128)(2,1)S(1)} %bitcast.17), channel_id=1, source_target_pairs={{0,96},{32,64},{64,32},{96,0},{1,97},{33,65},{65,33},{97,1},{2,98}... | collective-permute-start | bytes 3145736 | tf_op jit(solution)/shard_map/ppermute | solution.py:29
  100.7 47.0 %collective-permute-start.10 = (bf16[1024,128]{1,0:T(8,128)(2,1)S(1)}, bf16[1024,128]{1,0:T(8,128)(2,1)S(1)}, u32[]{:S(2)}, u32[]{:S(2)}) collective-permute-start(bf16[1024,128]{1,0:T(8,128)(2,1)S(1)} %fusion.1), channel_id=1, source_target_pairs={{0,32},{32,0},{64,96},{96,64},{1,33},{33,1},{65,97},{97,65},{2,34}... | collective-permute-start | bytes 786440 | tf_op jit(solution)/shard_map/ppermute | solution.py:29
  105.8 45.3 %collective-permute-start.17 = (bf16[1024,128]{1,0:T(8,128)(2,1)S(1)}, bf16[1024,128]{1,0:T(8,128)(2,1)S(1)}, u32[]{:S(2)}, u32[]{:S(2)}) collective-permute-start(bf16[1024,128]{1,0:T(8,128)(2,1)S(1)} %get-tuple-element.29), channel_id=1, source_target_pairs={{0,64},{32,96},{64,0},{96,32},{1,65},{33,97},{65,1},{97,33},{2,66}... | collective-permute-start | bytes 786440 | tf_op jit(solution)/shard_map/ppermute | solution.py:29
  148.9 9.8 %collective-permute-start.11 = (bf16[1024,128]{1,0:T(8,128)(2,1)S(1)}, bf16[1024,128]{1,0:T(8,128)(2,1)S(1)}, u32[]{:S(2)}, u32[]{:S(2)}) collective-permute-start(bf16[1024,128]{1,0:T(8,128)(2,1)S(1)} %get-tuple-element.31), channel_id=1, source_target_pairs={{0,64},{32,96},{64,0},{96,32},{1,65},{33,97},{65,1},{97,33},{2,66}... | collective-permute-start | bytes 786440 | tf_op jit(solution)/shard_map/ppermute | solution.py:29
  151.2 16.3 %collective-permute-start.18 = (bf16[1024,128]{1,0:T(8,128)(2,1)S(1)}, bf16[1024,128]{1,0:T(8,128)(2,1)S(1)}, u32[]{:S(2)}, u32[]{:S(2)}) collective-permute-start(bf16[1024,128]{1,0:T(8,128)(2,1)S(1)} %fusion.5), channel_id=1, source_target_pairs={{0,128},{128,0},{256,384},{384,256},{1,129},{129,1},{257,385},{385... | collective-permute-start | bytes 786440 | tf_op jit(solution)/shard_map/ppermute | solution.py:29
  158.7 26.9 %copy-start.4 = (bf16[1024,128]{1,0:T(8,128)(2,1)}, bf16[1024,128]{1,0:T(8,128)(2,1)S(1)}, u32[]{:S(2)}) copy-start(bf16[1024,128]{1,0:T(8,128)(2,1)S(1)} %collective-permute-done.11.refs_1_) | copy-start | bytes 786436
  158.7 51.6 %collective-permute-start = (bf16[4,128,1024]{2,1,0:T(8,128)(2,1)S(1)}, bf16[4,128,1024]{2,1,0:T(8,128)(2,1)}, u32[]{:S(2)}, u32[]{:S(2)}) collective-permute-start(bf16[4,128,1024]{2,1,0:T(8,128)(2,1)S(1)} %bitcast.18), channel_id=1, source_target_pairs={{0,1},{1,0},{2,3},{3,2},{4,5},{5,4},{6,7},{7,6},{8,9},{9,8},{10,11... | collective-permute-start | bytes 3145736 | tf_op jit(solution)/shard_map/ppermute | solution.py:29
  160.6 49.7 %collective-permute-start.2 = (bf16[4,128,1024]{2,1,0:T(8,128)(2,1)}, bf16[4,128,1024]{2,1,0:T(8,128)(2,1)}, u32[]{:S(2)}, u32[]{:S(2)}) collective-permute-start(bf16[4,128,1024]{2,1,0:T(8,128)(2,1)} %collective-permute-done.1.refs_2_), channel_id=1, source_target_pairs={{0,1},{1,0},{2,3},{3,2},{4,5},{5,4},{6,7},{7,6},{8,9},{9,8},{10,11... | collective-permute-start | bytes 3145736 | tf_op jit(solution)/shard_map/ppermute | solution.py:29
  163.0 47.3 %collective-permute-start.4 = (bf16[4,128,1024]{2,1,0:T(8,128)(2,1)}, bf16[4,128,1024]{2,1,0:T(8,128)(2,1)}, u32[]{:S(2)}, u32[]{:S(2)}) collective-permute-start(bf16[4,128,1024]{2,1,0:T(8,128)(2,1)} %collective-permute-done.3.refs_4_), channel_id=1, source_target_pairs={{0,1},{1,0},{2,3},{3,2},{4,5},{5,4},{6,7},{7,6},{8,9},{9,8},{10,11... | collective-permute-start | bytes 3145736 | tf_op jit(solution)/shard_map/ppermute | solution.py:29
  165.0 45.4 %collective-permute-start.6 = (bf16[4,128,1024]{2,1,0:T(8,128)(2,1)}, bf16[4,128,1024]{2,1,0:T(8,128)(2,1)}, u32[]{:S(2)}, u32[]{:S(2)}) collective-permute-start(bf16[4,128,1024]{2,1,0:T(8,128)(2,1)} %collective-permute-done.5.refs_6_), channel_id=1, source_target_pairs={{0,1},{1,0},{2,3},{3,2},{4,5},{5,4},{6,7},{7,6},{8,9},{9,8},{10,11... | collective-permute-start | bytes 3145736 | tf_op jit(solution)/shard_map/ppermute | solution.py:29
  167.5 10.2 %collective-permute-start.12 = (bf16[1024,128]{1,0:T(8,128)(2,1)S(1)}, bf16[1024,128]{1,0:T(8,128)(2,1)S(1)}, u32[]{:S(2)}, u32[]{:S(2)}) collective-permute-start(bf16[1024,128]{1,0:T(8,128)(2,1)S(1)} %fusion.2), channel_id=1, source_target_pairs={{0,128},{128,0},{256,384},{384,256},{1,129},{129,1},{257,385},{385... | collective-permute-start | bytes 786440 | tf_op jit(solution)/shard_map/ppermute | solution.py:29
  177.8 21.5 %collective-permute-start.20 = (bf16[1024,128]{1,0:T(8,128)(2,1)}, bf16[1024,128]{1,0:T(8,128)(2,1)S(1)}, u32[]{:S(2)}, u32[]{:S(2)}) collective-permute-start(bf16[1024,128]{1,0:T(8,128)(2,1)} %add_convert_fusion.1), channel_id=1, source_target_pairs={{0,256},{128,384},{1,257},{129,385},{2,258},{130,386},{3,259},{131... | collective-permute-start | bytes 786440 | tf_op jit(solution)/shard_map/ppermute | solution.py:324
  199.3 11.0 %collective-permute-start.19 = (bf16[1024,128]{1,0:T(8,128)(2,1)S(1)}, bf16[1024,128]{1,0:T(8,128)(2,1)S(1)}, u32[]{:S(2)}, u32[]{:S(2)}) collective-permute-start(bf16[1024,128]{1,0:T(8,128)(2,1)S(1)} %add_convert_fusion.2), channel_id=1, source_target_pairs={{0,256},{128,384},{1,257},{129,385},{2,258},{130,386},{3,259},{131... | collective-permute-start | bytes 786440 | tf_op jit(solution)/shard_map/ppermute | solution.py:324
  216.7 48.4 %collective-permute-start.21 = (bf16[256,1024]{1,0:T(8,128)(2,1)S(1)}, bf16[256,1024]{1,0:T(8,128)(2,1)S(1)}, u32[]{:S(2)}, u32[]{:S(2)}) collective-permute-start(bf16[256,1024]{1,0:T(8,128)(2,1)S(1)} %get-tuple-element.28), channel_id=1, source_target_pairs={{0,2},{2,0},{1,3},{3,1},{4,6},{6,4},{5,7},{7,5},{8,10},{10,8},{9,1... | collective-permute-start | bytes 1572872 | tf_op jit(solution)/shard_map/ppermute | solution.py:29
  (34 other events, 188.0 us)

commit v2 on v1

v2 whole, which is shorter than its diff:
```python
import functools

import jax
import jax.numpy as jnp
from jax import lax
from jax.experimental import pallas as pl
from jax.experimental.pallas import tpu as pltpu
from jax.sharding import Mesh, PartitionSpec as P

epsilon = 1e-05
LOCAL_LEVELS = 9
NN = (((1,), (0,)), ((), ()))
NT = (((1,), (1,)), ((), ()))
f32 = jnp.float32
bf16 = jnp.bfloat16


def params(mib, steps=1):
    return pltpu.CompilerParams(
        vmem_limit_bytes=mib * 2**20, dimension_semantics=("arbitrary",) * steps
    )


def cost(flops, moved):
    return pl.CostEstimate(flops=flops, bytes_accessed=moved, transcendentals=0)


def swapped(value, axis, mask):
    return lax.ppermute(value, axis, [(i, i ^ mask) for i in range(lax.axis_size(axis))])


def dot(a, b, dims):
    return lax.dot_general(a, b, dims, preferred_element_type=f32)


def state_kernel(values_ref, keys_ref, vt_ref, sent_ref):
    vt = values_ref[...].T
    vt_ref[...] = vt
    sent_ref[...] = dot(vt, keys_ref[...], NN).astype(bf16)


def own_state(values, keys):
    tok, width = values.shape
    cols = width // 4
    n = keys.shape[1]
    return pl.pallas_call(
        state_kernel,
        grid=(4,),
        in_specs=[
            pl.BlockSpec((tok, cols), lambda i: (0, i)),
            pl.BlockSpec((tok, n), lambda i: (0, 0)),
        ],
        out_specs=[
            pl.BlockSpec((cols, tok), lambda i: (i, 0)),
            pl.BlockSpec((cols, n), lambda i: (i, 0)),
        ],
        out_shape=[
            jax.ShapeDtypeStruct((width, tok), bf16),
            jax.ShapeDtypeStruct((width, n), bf16),
        ],
        compiler_params=params(24),
        cost_estimate=cost(2 * tok * width * n, 4 * tok * width),
        name="own_state",
    )(values, keys)


def local_kernel(heads, half, skip_ref, vt_ref, gate_ref, keys_ref, query_ref, w_ref, acc_ref, silu_ref, score_ref):
    size = vt_ref.shape[0] // heads
    first = pl.program_id(0) * heads

    @pl.when(pl.program_id(0) == 0)
    def _():
        scores = dot(keys_ref[...], query_ref[...], NT)
        s = lax.broadcasted_iota(jnp.int32, scores.shape, 0)
        t = lax.broadcasted_iota(jnp.int32, scores.shape, 1)
        score_ref[...] = jnp.where(s <= t, scores, 0.0)

    gate = gate_ref[...].astype(f32)
    silu_ref[...] = (gate / (1.0 + jnp.exp(-gate))).T

    s = lax.broadcasted_iota(jnp.int32, (half, half), 0)
    t = lax.broadcasted_iota(jnp.int32, (half, half), 1)
    differ = s ^ t
    low = score_ref[:half, :half]
    cross = score_ref[:half, half:]
    high = score_ref[half:, half:]
    for h in range(heads):
        w = w_ref[:, h, :].astype(f32)

        def mix(level, lo):
            return jnp.broadcast_to(w[level : level + 1, lo : lo + half], (half, half))

        def diagonal(lo, scores):
            m = mix(0, lo)
            for level in range(1, LOCAL_LEVELS - 1):
                m = jnp.where(differ >= (1 << (level - 1)), mix(level, lo), m)
            return (m * scores).astype(bf16)

        vt = vt_ref[h * size : (h + 1) * size, :]
        skip = skip_ref[first + h]
        near = dot(vt[:, :half], diagonal(0, low), NN)
        right = jnp.concatenate(
            [(mix(LOCAL_LEVELS - 1, half) * cross).astype(bf16), diagonal(half, high)], axis=0
        )
        far = dot(vt, right, NN)
        rows = slice(h * size, (h + 1) * size)
        acc_ref[rows, :half] = near + skip * vt[:, :half].astype(f32)
        acc_ref[rows, half:] = far + skip * vt[:, half:].astype(f32)


def local_part(vt, gate, keys, query, weights, skip, head_size):
    cols, tok = vt.shape
    n = keys.shape[1]
    heads = 8
    rows = heads * head_size
    steps = cols // rows
    return pl.pallas_call(
        functools.partial(local_kernel, heads, tok // 2),
        grid=(steps,),
        in_specs=[
            pl.BlockSpec(memory_space=pltpu.SMEM),
            pl.BlockSpec((rows, tok), lambda i: (i, 0)),
            pl.BlockSpec((tok, rows), lambda i: (0, i)),
            pl.BlockSpec((tok, n), lambda i: (0, 0)),
            pl.BlockSpec((tok, n), lambda i: (0, 0)),
            pl.BlockSpec((16, heads, tok), lambda i: (0, i, 0)),
        ],
        out_specs=[
            pl.BlockSpec((rows, tok), lambda i: (i, 0)),
            pl.BlockSpec((rows, tok), lambda i: (i, 0)),
        ],
        out_shape=[jax.ShapeDtypeStruct((cols, tok), f32)] * 2,
        scratch_shapes=[pltpu.VMEM((tok, tok), f32)],
        compiler_params=params(24),
        cost_estimate=cost(8 * tok * tok * cols, 12 * tok * cols),
        name="local_part",
    )(skip, vt, gate, keys, query, weights)


def read_level(state, message, level, heads, n):
    rows, tok = state.shape[0], message.shape[1]
    part = dot(state, message[:n], NN).reshape(heads, rows // heads, tok)
    first = n + level * heads
    return (part * message[first : first + heads].astype(f32)[:, None, :]).reshape(rows, tok)


def sibling_sum(ref, index, bit):
    count = 1 << bit
    first = ((index >> bit) ^ 1) << bit
    if count == 1:
        return ref[first]
    total = ref[first].astype(f32)
    for k in range(1, count):
        total = total + ref[first + k].astype(f32)
    return total.astype(bf16)


def low_kernel(heads, where_ref, raw_ref, line_ref, message_ref, out_ref):
    n = raw_ref.shape[2]
    group = raw_ref.shape[0]
    local = {}
    for bit in range(3):
        for block in range(0, group, 2 << bit):
            local[bit, block] = sibling_sum(raw_ref, block + (1 << bit), bit)
    shared = [sibling_sum(line_ref, where_ref[0], bit) for bit in range(2)]
    for j in range(group):
        message = message_ref[j]
        total = read_level(shared[0], message, 3, heads, n)
        total = total + read_level(shared[1], message, 4, heads, n)
        for bit in range(3):
            if j >> bit & 1:
                block = j >> (bit + 1) << (bit + 1)
                total = total + read_level(local[bit, block], message, bit, heads, n)
        out_ref[j] = total


def high_kernel(heads, where_ref, part_ref, plane_ref, message_ref, out_ref):
    n = plane_ref.shape[2]
    shared = [sibling_sum(plane_ref, where_ref[1], bit) for bit in range(2)]
    for j in range(part_ref.shape[0]):
        message = message_ref[j]
        total = part_ref[j] + read_level(shared[0], message, 5, heads, n)
        total = total + read_level(shared[1], message, 6, heads, n)
        out_ref[j] = total.astype(bf16)


def far_call(kernel, name, heads, where, first, states, message, dtype):
    group, _, tok = message.shape
    rows = states.shape[1]
    vmem = pl.BlockSpec(memory_space=pltpu.VMEM)
    return pl.pallas_call(
        functools.partial(kernel, heads),
        in_specs=[pl.BlockSpec(memory_space=pltpu.SMEM), vmem, vmem, vmem],
        out_specs=vmem,
        out_shape=jax.ShapeDtypeStruct((group, rows, tok), dtype),
        compiler_params=pltpu.CompilerParams(vmem_limit_bytes=24 * 2**20),
        cost_estimate=cost(8 * group * rows * tok * 128, 8 * group * rows * tok),
        name=name,
    )(where, first, states, message)


def project(where_ref, pieces, normed_ref, out_ref):
    mine = where_ref[1]
    half = normed_ref.shape[1]
    width = pieces[0].shape[1]
    for k in range(len(pieces) // 2):
        block = dot(pieces[2 * k][0], normed_ref[mine], NN)
        block = block + dot(pieces[2 * k + 1][0], normed_ref[1 - mine], NN)
        at = pl.multiple_of((where_ref[0] ^ k) * width, width)
        out_ref[:, pl.ds(at, width)] = block.T.astype(out_ref.dtype)


def finish_kernel(where_ref, *refs):
    pieces = refs[:8]
    acc_ref, silu_ref, far_ref, gain_ref, out_ref, normed_ref = refs[8:]

    @pl.when(pl.program_id(0) == 0)
    def _():
        rows = acc_ref.shape[0]
        gated = (acc_ref[...] + far_ref[...].astype(f32)) * silu_ref[...]
        squares = jnp.sum(gated * gated, axis=0, keepdims=True)
        scale = lax.rsqrt(squares / rows + epsilon)
        normed = (gated * scale * gain_ref[...]).astype(bf16)
        normed_ref[0] = normed[: rows // 2]
        normed_ref[1] = normed[rows // 2 :]

    project(where_ref, pieces, normed_ref, out_ref)


def keep_kernel(where_ref, *refs):
    project(where_ref, refs[:8], refs[8], refs[9])


def piece_specs(pieces, offset):
    _, cols, depth = pieces[0].shape
    return [
        pl.BlockSpec((1, cols, depth), lambda i, where: (where[offset] + i, 0, 0)) for _ in pieces
    ]


def finish(where, pieces, acc, silu, far, gain):
    rows, tok = acc.shape
    z_size, cols, depth = pieces[0].shape
    steps = z_size // 2
    wide = cols * len(pieces) // 2

    def whole(array):
        return pl.BlockSpec(array.shape, lambda i, where: (0,) * array.ndim)

    others = [acc, silu, far, gain]
    return pl.pallas_call(
        finish_kernel,
        grid_spec=pltpu.PrefetchScalarGridSpec(
            num_scalar_prefetch=1,
            grid=(steps,),
            in_specs=piece_specs(pieces, 2) + [whole(a) for a in others],
            out_specs=[
                pl.BlockSpec((tok, wide), lambda i, where: (0, i)),
                pl.BlockSpec((2, rows // 2, tok), lambda i, where: (0, 0, 0)),
            ],
        ),
        out_shape=[
            jax.ShapeDtypeStruct((tok, wide * steps), bf16),
            jax.ShapeDtypeStruct((2, rows // 2, tok), bf16),
        ],
        compiler_params=params(40),
        cost_estimate=cost(2 * tok * rows * wide * steps, 16 * 2**20),
        name="finish",
    )(where, *pieces, *others)


def keep(where, pieces, normed):
    _, rows, tok = normed.shape
    z_size, cols, depth = pieces[0].shape
    steps = z_size // 2
    wide = cols * len(pieces) // 2
    return pl.pallas_call(
        keep_kernel,
        grid_spec=pltpu.PrefetchScalarGridSpec(
            num_scalar_prefetch=1,
            grid=(steps,),
            in_specs=piece_specs(pieces, 3)
            + [pl.BlockSpec((2, rows, tok), lambda i, where: (0, 0, 0))],
            out_specs=pl.BlockSpec((tok, wide), lambda i, where: (0, i)),
        ),
        out_shape=jax.ShapeDtypeStruct((tok, wide * steps), f32),
        compiler_params=params(40),
        cost_estimate=cost(2 * tok * 2 * rows * wide * steps, 8 * 2**20),
        name="keep",
    )(where, *pieces, normed)


def shared_along(value, axis):
    spread = jnp.broadcast_to(value[None], (lax.axis_size(axis), *value.shape))
    return lax.all_to_all(spread, axis, 0, 0, tiled=True)


def gathered_weight(out_weight):
    rows, cols = out_weight.shape
    mine = lax.axis_index("rep")
    half = lax.dynamic_slice_in_dim(out_weight, mine * (rows // 2), rows // 2, 0).T
    line = shared_along(half, "y").reshape(-1, rows // 2)
    own = shared_along(line, "zl")
    pieces = []
    for k in range(lax.axis_size("x")):
        piece = own if k == 0 else swapped(own, "x", k)
        pieces += [piece, swapped(piece, "rep", 1)]
    return pieces


def on_device(
    seq_values, seq_gate, seq_keys, seq_queries, level_weights, skip_gain, norm_gain, out_weight
):
    tok, width = seq_values.shape
    n = seq_keys.shape[1]
    head_count = skip_gain.shape[0]
    head_size = width // head_count
    group = lax.axis_size("y")
    heads = head_count // group
    rows = width // group
    axes = [("y", b) for b in range(3)] + [("x", b) for b in range(2)] + [("zl", b) for b in range(2)]
    uppers = jnp.stack([(lax.axis_index(a) >> b) & 1 for a, b in axes])
    head = lax.axis_index("head")
    z_half = lax.axis_size("zl") // 2
    place = jnp.stack([lax.axis_index("x"), lax.axis_index("zl")]).astype(jnp.int32)
    where = jnp.stack(
        [lax.axis_index("x"), lax.axis_index("rep"), (1 - head) * z_half, head * z_half]
    ).astype(jnp.int32)

    vt, sent = own_state(seq_values, seq_keys)
    raw = lax.all_to_all(sent.reshape(group, rows, n), "y", 0, 0, tiled=True)
    pieces = gathered_weight(out_weight)

    far_weights = level_weights[LOCAL_LEVELS:] * uppers[:, None, None].astype(bf16)
    levels = len(axes)
    far_weights = far_weights.reshape(levels, group, heads, tok).swapaxes(0, 1)
    far_weights = far_weights.reshape(group, levels * heads, tok)
    far_weights = jnp.pad(far_weights, ((0, 0), (0, -levels * heads % 16), (0, 0)))
    message = jnp.concatenate(
        [jnp.broadcast_to(seq_queries.T[None], (group, n, tok)), far_weights], axis=1
    )
    message = lax.all_to_all(message, "y", 0, 0, tiled=True)

    def summed(blocks):
        return jnp.sum(blocks.astype(f32), axis=0).astype(bf16)

    line = shared_along(summed(raw), "x")
    plane = shared_along(summed(line), "zl")

    acc, silu = local_part(vt, seq_gate, seq_keys, seq_queries, level_weights, skip_gain, head_size)
    part = far_call(low_kernel, "low_levels", heads, place, raw, line, message, f32)
    far = far_call(high_kernel, "high_levels", heads, place, part, plane, message, bf16)
    far = lax.all_to_all(far, "y", 0, 0, tiled=True).reshape(width, tok)

    to_send, normed = finish(where, pieces, acc, silu, far, norm_gain[:, None])
    got = swapped(to_send, "head", 1)
    kept = keep(where, pieces, normed)
    return (kept + got.astype(f32)).astype(bf16)


def solution(mesh):
    grid = Mesh(mesh.devices.reshape(4, 4, 8, 2, 2), ("zl", "x", "y", "head", "rep"))
    ctx = ("zl", "x", "y")
    tokens = ("rep", *ctx)
    placed = (
        P(tokens, "head"),
        P(tokens, "head"),
        P(tokens, None),
        P(tokens, None),
        P(None, "head", tokens),
        P("head"),
        P("head"),
        P("head", ctx),
    )
    return jax.shard_map(
        on_device, mesh=grid, in_specs=placed, out_specs=P(tokens, "head"), check_vma=False
    )
```

time: 267 us -> 223 us (0.84)
  the two profiles are of different devices: /device:TPU:220 before, /device:TPU:64 now
where the time goes in v2:
time: 223 us; the launch traced here: 221 us
  waiting for transfers between devices  99.7 us (45%)
  starting transfers between devices  58.9 us (26%)
  blocking collectives  22.1 us (10%)
  Pallas kernels  19.1 us (9%)
  local copies, waits for them, and re-layouts  18.9 us (8%)
  other arithmetic  2.23 us (1%)
    ppermute x8, waiting for transfers between devices, swapped(): lax.ppermute(value, axis, [(i, i ^ mask) for i in range(lax.axis_size(axi...  45.7 us
    all_to_all x4, waiting for transfers between devices, shared_along(): return lax.all_to_all(spread, axis, 0, 0, tiled=True)  36.5 us
    ppermute x8, starting transfers between devices, swapped(): lax.ppermute(value, axis, [(i, i ^ mask) for i in range(lax.axis_size(axi...  26.2 us
    all_to_all x1, blocking collectives, on_device(): message = lax.all_to_all(message, 'y', 0, 0, tiled=True)  22.1 us
    all_to_all x4, starting transfers between devices, shared_along(): return lax.all_to_all(spread, axis, 0, 0, tiled=True)  21.9 us
    all_to_all x1, waiting for transfers between devices, on_device(): raw = lax.all_to_all(sent.reshape(group, rows, n), 'y', 0, 0, tiled=True)  17.5 us
    unnamed x38, local copies, waits for them, and re-layouts  14.9 us
    all_to_all x1, starting transfers between devices, on_device(): raw = lax.all_to_all(sent.reshape(group, rows, n), 'y', 0, 0, tiled=True)  7.1 us
  transfers between devices with their start and end apart: 14, of which 6 were waited for; matrix products, arithmetic and copies ran while one was open for 1% of the time, Pallas kernels for 5%

profile of v2, /device:TPU:64, one launch (start us, length us, event | category | flops | bytes accessed | tf_op | source)
XLA Modules:
  0.0 221.4 jit_solution(9340495108474055745)
XLA Ops:
  2.1 2.2 %own_state.1 = (bf16[2048,256]{1,0:T(8,128)(2,1)S(1)}, bf16[2048,128]{1,0:T(8,128)(2,1)}) custom-call(bf16[256,2048]{1,0:T(8,128)(2,1)S(1)} %copy-done.9, bf16[256,128]{1,0:T(8,128)(2,1)S(1)} %copy-done.10), custom_call_target="tpu_custom_call" | custom-call | flops 134217728 | bytes 2097152 | tf_op jit(solution)/shard_map/own_state/pallas_call | solution.py:46
  5.3 7.1 %all-to-all-start.2 = ((bf16[8,256,128]{2,1,0:T(8,128)(2,1)}), bf16[8,256,128]{2,1,0:T(8,128)(2,1)S(1)}, u32[]{:S(2)}, u32[]{:S(2)}) async-start(bf16[8,256,128]{2,1,0:T(8,128)(2,1)} %bitcast.7), calls=%async_computation.2 | async-start | bytes 1048576 | tf_op jit(solution)/shard_map/all_to_all | solution.py:331
  12.4 17.5 %all-to-all-done.2.raw_ref = bf16[8,256,128]{2,1,0:T(8,128)(2,1)S(1)} async-done(((bf16[8,256,128]{2,1,0:T(8,128)(2,1)}), bf16[8,256,128]{2,1,0:T(8,128)(2,1)S(1)}, u32[]{:S(2)}, u32[]{:S(2)}) %all-to-all-start.2) | async-done | bytes 524320 | tf_op jit(solution)/shard_map/all_to_all | solution.py:331
  30.7 3.4 %all-to-all-start = ((bf16[8,16,1024]{2,1,0:T(8,128)(2,1)}), bf16[8,16,1024]{2,1,0:T(8,128)(2,1)S(1)}, u32[]{:S(2)}, u32[]{:S(2)}) async-start(bf16[8,16,1024]{2,1,0:T(8,128)(2,1)} %broadcast_in_dim.14), calls=%async_computation | async-start | bytes 524288 | tf_op jit(solution)/shard_map/all_to_all | solution.py:295
  34.3 12.0 %all-to-all-done = bf16[8,16,1024]{2,1,0:T(8,128)(2,1)S(1)} async-done(((bf16[8,16,1024]{2,1,0:T(8,128)(2,1)}), bf16[8,16,1024]{2,1,0:T(8,128)(2,1)S(1)}, u32[]{:S(2)}, u32[]{:S(2)}) %all-to-all-start) | async-done | bytes 262176 | tf_op jit(solution)/shard_map/all_to_all | solution.py:295
  47.1 4.3 %all-to-all-start.3 = ((bf16[4,256,128]{2,1,0:T(8,128)(2,1)}), bf16[4,256,128]{2,1,0:T(8,128)(2,1)S(1)}, u32[]{:S(2)}, u32[]{:S(2)}) async-start(bf16[4,256,128]{2,1,0:T(8,128)(2,1)} %broadcast_in_dim.17), calls=%async_computation.3 | async-start | bytes 524288 | tf_op jit(solution)/shard_map/all_to_all | solution.py:295
  52.7 5.4 %all-to-all-done.3.line_ref = bf16[4,256,128]{2,1,0:T(8,128)(2,1)S(1)} async-done(((bf16[4,256,128]{2,1,0:T(8,128)(2,1)}), bf16[4,256,128]{2,1,0:T(8,128)(2,1)S(1)}, u32[]{:S(2)}, u32[]{:S(2)}) %all-to-all-start.3) | async-done | bytes 262176 | tf_op jit(solution)/shard_map/all_to_all | solution.py:295
  58.0 22.1 %all_to_all.35.message_ref = bf16[8,160,256]{2,1,0:T(8,128)(2,1)} all-to-all(bf16[8,160,256]{2,1,0:T(8,128)(2,1)S(1)} %fusion.1), channel_id=1, replica_groups=mesh['zl'=4,'x'=4,'y'=8,'head'=2,'rep'=2] {'y'}, dimensions={0} | all-to-all | bytes 1310720 | tf_op jit(solution)/shard_map/all_to_all | solution.py:342
  81.3 6.9 %all-to-all-start.1 = ((bf16[4,128,1024]{2,1,0:T(8,128)(2,1)}), bf16[4,128,1024]{2,1,0:T(8,128)(2,1)S(1)}, u32[]{:S(2)}, u32[]{:S(2)}) async-start(bf16[4,128,1024]{2,1,0:T(8,128)(2,1)} %broadcast_in_dim.16), calls=%async_computation.1 | async-start | bytes 2097152 | tf_op jit(solution)/shard_map/all_to_all | solution.py:295
  88.2 19.1 %all-to-all-done.1.refs_0_ = bf16[4,128,1024]{2,1,0:T(8,128)(2,1)S(1)} async-done(((bf16[4,128,1024]{2,1,0:T(8,128)(2,1)}), bf16[4,128,1024]{2,1,0:T(8,128)(2,1)S(1)}, u32[]{:S(2)}, u32[]{:S(2)}) %all-to-all-start.1) | async-done | bytes 1048608 | tf_op jit(solution)/shard_map/all_to_all | solution.py:295
  108.1 7.3 %all-to-all-start.5 = ((bf16[4,256,128]{2,1,0:T(8,128)(2,1)}), bf16[4,256,128]{2,1,0:T(8,128)(2,1)}, u32[]{:S(2)}, u32[]{:S(2)}) async-start(bf16[4,256,128]{2,1,0:T(8,128)(2,1)} %broadcast_in_dim.19), calls=%async_computation.5 | async-start | bytes 524288 | tf_op jit(solution)/shard_map/all_to_all | solution.py:295
  115.3 3.1 %collective-permute-start.5 = (bf16[4,128,1024]{2,1,0:T(8,128)(2,1)S(1)}, bf16[4,128,1024]{2,1,0:T(8,128)(2,1)}, u32[]{:S(2)}, u32[]{:S(2)}) collective-permute-start(bf16[4,128,1024]{2,1,0:T(8,128)(2,1)S(1)} %all-to-all-done.1.refs_0_), channel_id=1, source_target_pairs={{0,96},{32,64},{64,32},{96,0},{1,97},{33,65},{65,33},{97,1},{2,98}... | collective-permute-start | bytes 3145736 | tf_op jit(solution)/shard_map/ppermute | solution.py:29
  118.5 3.4 %collective-permute-start.3 = (bf16[4,128,1024]{2,1,0:T(8,128)(2,1)S(1)}, bf16[4,128,1024]{2,1,0:T(8,128)(2,1)}, u32[]{:S(2)}, u32[]{:S(2)}) collective-permute-start(bf16[4,128,1024]{2,1,0:T(8,128)(2,1)S(1)} %all-to-all-done.1.refs_0_), channel_id=1, source_target_pairs={{0,64},{32,96},{64,0},{96,32},{1,65},{33,97},{65,1},{97,33},{2,66}... | collective-permute-start | bytes 3145736 | tf_op jit(solution)/shard_map/ppermute | solution.py:29
  121.8 3.3 %collective-permute-start.1 = (bf16[4,128,1024]{2,1,0:T(8,128)(2,1)S(1)}, bf16[4,128,1024]{2,1,0:T(8,128)(2,1)}, u32[]{:S(2)}, u32[]{:S(2)}) collective-permute-start(bf16[4,128,1024]{2,1,0:T(8,128)(2,1)S(1)} %all-to-all-done.1.refs_0_), channel_id=1, source_target_pairs={{0,32},{32,0},{64,96},{96,64},{1,33},{33,1},{65,97},{97,65},{2,34}... | collective-permute-start | bytes 3145736 | tf_op jit(solution)/shard_map/ppermute | solution.py:29
  132.8 3.7 %all-to-all-start.6 = ((bf16[8,256,256]{2,1,0:T(8,128)(2,1)}), bf16[8,256,256]{2,1,0:T(8,128)(2,1)S(1)}, u32[]{:S(2)}, u32[]{:S(2)}) async-start(bf16[8,256,256]{2,1,0:T(8,128)(2,1)} %copy-done.5), calls=%async_computation.6 | async-start | bytes 2097152 | tf_op jit(solution)/shard_map/all_to_all | solution.py:353
  136.5 1.9 collective-permute-start
  138.4 25.5 %collective-permute-done.5.refs_6_ = bf16[4,128,1024]{2,1,0:T(8,128)(2,1)} collective-permute-done((bf16[4,128,1024]{2,1,0:T(8,128)(2,1)S(1)}, bf16[4,128,1024]{2,1,0:T(8,128)(2,1)}, u32[]{:S(2)}, u32[]{:S(2)}) %collective-permute-start.5) | collective-permute-done | bytes 1048608 | tf_op jit(solution)/shard_map/ppermute | solution.py:29
  165.9 2.4 %collective-permute-start.4 = (bf16[4,128,1024]{2,1,0:T(8,128)(2,1)}, bf16[4,128,1024]{2,1,0:T(8,128)(2,1)}, u32[]{:S(2)}, u32[]{:S(2)}) collective-permute-start(bf16[4,128,1024]{2,1,0:T(8,128)(2,1)} %collective-permute-done.3.refs_4_), channel_id=1, source_target_pairs={{0,1},{1,0},{2,3},{3,2},{4,5},{5,4},{6,7},{7,6},{8,9},{9,8},{10,11... | collective-permute-start | bytes 3145736 | tf_op jit(solution)/shard_map/ppermute | solution.py:29
  168.3 1.9 collective-permute-start.2
  174.0 4.2 %local_part.1 = (f32[2048,256]{1,0:T(8,128)S(1)}, f32[2048,256]{1,0:T(8,128)S(1)}) custom-call(f32[32]{0:T(128)S(1)} %copy-done.17, bf16[2048,256]{1,0:T(8,128)(2,1)S(1)} %copy-done.16, bf16[256,2048]{1,0:T(8,128)(2,1)S(1)} %copy-done.14, bf16[256,128]{1,0:T(8,128)(2,1)S(1)} %copy-done.11, bf16[256,128]{1,0:T(8,128)(2,1)S(1)} %copy-done.12, ...), custom_call_target="tpu_custom_call" | custom-call | flops 1073741824 | bytes 6291456 | tf_op jit(solution)/shard_map/local_part/pallas_call | solution.py:117
  182.6 5.5 %finish.1 = (bf16[256,1024]{1,0:T(8,128)(2,1)S(1)}, bf16[2,1024,256]{2,1,0:T(8,128)(2,1)S(1)}) custom-call(s32[4]{0:T(128)S(1)} %pad_add_fusion.where_ref, bf16[4,128,1024]{2,1,0:T(8,128)(2,1)S(1)} %all-to-all-done.1.refs_0_, bf16[4,128,1024]{2,1,0:T(8,128)(2,1)} %collective-permute-done.refs_1_, bf16[4,128,1024]{2,1,0:T(8,128)(2,1)} %collective-permute-done.1.refs_2_, ...), custom_call_target="tpu_custom_call" | custom-call | flops 1073741824 | bytes 16777216 | tf_op jit(solution)/shard_map/finish/pallas_call | solution.py:251
  188.1 8.2 %collective-permute-start.7 = (bf16[256,1024]{1,0:T(8,128)(2,1)S(1)}, bf16[256,1024]{1,0:T(8,128)(2,1)S(1)}, u32[]{:S(2)}, u32[]{:S(2)}) collective-permute-start(bf16[256,1024]{1,0:T(8,128)(2,1)S(1)} %get-tuple-element.16), channel_id=1, source_target_pairs={{0,2},{2,0},{1,3},{3,1},{4,6},{6,4},{5,7},{7,5},{8,10},{10,8},{9,1... | collective-permute-start | bytes 1572872 | tf_op jit(solution)/shard_map/ppermute | solution.py:29
  196.3 3.9 %keep.1 = f32[256,1024]{1,0:T(8,128)S(1)} custom-call(s32[4]{0:T(128)S(1)} %pad_add_fusion.where_ref, bf16[4,128,1024]{2,1,0:T(8,128)(2,1)S(1)} %all-to-all-done.1.refs_0_, bf16[4,128,1024]{2,1,0:T(8,128)(2,1)} %collective-permute-done.refs_1_, bf16[4,128,1024]{2,1,0:T(8,128)(2,1)} %collective-permute-done.1.refs_2_, ...), custom_call_target="tpu_custom_call" | custom-call | flops 1073741824 | bytes 8388608 | tf_op jit(solution)/shard_map/keep/pallas_call | solution.py:277
  200.3 20.2 %collective-permute-done.7 = bf16[256,1024]{1,0:T(8,128)(2,1)S(1)} collective-permute-done((bf16[256,1024]{1,0:T(8,128)(2,1)S(1)}, bf16[256,1024]{1,0:T(8,128)(2,1)S(1)}, u32[]{:S(2)}, u32[]{:S(2)}) %collective-permute-start.7) | collective-permute-done | bytes 524320 | tf_op jit(solution)/shard_map/ppermute | solution.py:29
  (68 shorter events, 26.4 us)
Async XLA Ops:
  0.0 12.4 %copy-start = (bf16[2048,16]{0,1:T(8,128)(2,1)S(1)}, bf16[2048,16]{0,1:T(8,128)(2,1)}, u32[]{:S(2)}) copy-start(bf16[2048,16]{0,1:T(8,128)(2,1)} %param.15) | copy-start | bytes 196612
  0.0 1.3 copy-start.9
  5.3 24.6 %all-to-all-start.2 = ((bf16[8,256,128]{2,1,0:T(8,128)(2,1)}), bf16[8,256,128]{2,1,0:T(8,128)(2,1)S(1)}, u32[]{:S(2)}, u32[]{:S(2)}) async-start(bf16[8,256,128]{2,1,0:T(8,128)(2,1)} %bitcast.7), calls=%async_computation.2 | async-start | bytes 1048576 | tf_op jit(solution)/shard_map/all_to_all | solution.py:331
  12.4 39.9 %copy-start.12 = (bf16[256,128]{1,0:T(8,128)(2,1)S(1)}, bf16[256,128]{1,0:T(8,128)(2,1)}, u32[]{:S(2)}) copy-start(bf16[256,128]{1,0:T(8,128)(2,1)} %query_ref.1) | copy-start | bytes 196612
  29.9 22.6 %copy-start.3 = (bf16[8,256,128]{2,1,0:T(8,128)(2,1)}, bf16[8,256,128]{2,1,0:T(8,128)(2,1)S(1)}, u32[]{:S(2)}) copy-start(bf16[8,256,128]{2,1,0:T(8,128)(2,1)S(1)} %all-to-all-done.2.raw_ref) | copy-start | bytes 1572868
  30.7 15.7 %all-to-all-start = ((bf16[8,16,1024]{2,1,0:T(8,128)(2,1)}), bf16[8,16,1024]{2,1,0:T(8,128)(2,1)S(1)}, u32[]{:S(2)}, u32[]{:S(2)}) async-start(bf16[8,16,1024]{2,1,0:T(8,128)(2,1)} %broadcast_in_dim.14), calls=%async_computation | async-start | bytes 524288 | tf_op jit(solution)/shard_map/all_to_all | solution.py:295
  47.1 11.0 %all-to-all-start.3 = ((bf16[4,256,128]{2,1,0:T(8,128)(2,1)}), bf16[4,256,128]{2,1,0:T(8,128)(2,1)S(1)}, u32[]{:S(2)}, u32[]{:S(2)}) async-start(bf16[4,256,128]{2,1,0:T(8,128)(2,1)} %broadcast_in_dim.17), calls=%async_computation.3 | async-start | bytes 524288 | tf_op jit(solution)/shard_map/all_to_all | solution.py:295
  81.3 26.1 %all-to-all-start.1 = ((bf16[4,128,1024]{2,1,0:T(8,128)(2,1)}), bf16[4,128,1024]{2,1,0:T(8,128)(2,1)S(1)}, u32[]{:S(2)}, u32[]{:S(2)}) async-start(bf16[4,128,1024]{2,1,0:T(8,128)(2,1)} %broadcast_in_dim.16), calls=%async_computation.1 | async-start | bytes 2097152 | tf_op jit(solution)/shard_map/all_to_all | solution.py:295
  108.1 21.0 %all-to-all-start.5 = ((bf16[4,256,128]{2,1,0:T(8,128)(2,1)}), bf16[4,256,128]{2,1,0:T(8,128)(2,1)}, u32[]{:S(2)}, u32[]{:S(2)}) async-start(bf16[4,256,128]{2,1,0:T(8,128)(2,1)} %broadcast_in_dim.19), calls=%async_computation.5 | async-start | bytes 524288 | tf_op jit(solution)/shard_map/all_to_all | solution.py:295
  115.3 48.6 %collective-permute-start.5 = (bf16[4,128,1024]{2,1,0:T(8,128)(2,1)S(1)}, bf16[4,128,1024]{2,1,0:T(8,128)(2,1)}, u32[]{:S(2)}, u32[]{:S(2)}) collective-permute-start(bf16[4,128,1024]{2,1,0:T(8,128)(2,1)S(1)} %all-to-all-done.1.refs_0_), channel_id=1, source_target_pairs={{0,96},{32,64},{64,32},{96,0},{1,97},{33,65},{65,33},{97,1},{2,98}... | collective-permute-start | bytes 3145736 | tf_op jit(solution)/shard_map/ppermute | solution.py:29
  118.5 47.4 %collective-permute-start.3 = (bf16[4,128,1024]{2,1,0:T(8,128)(2,1)S(1)}, bf16[4,128,1024]{2,1,0:T(8,128)(2,1)}, u32[]{:S(2)}, u32[]{:S(2)}) collective-permute-start(bf16[4,128,1024]{2,1,0:T(8,128)(2,1)S(1)} %all-to-all-done.1.refs_0_), channel_id=1, source_target_pairs={{0,64},{32,96},{64,0},{96,32},{1,65},{33,97},{65,1},{97,33},{2,66}... | collective-permute-start | bytes 3145736 | tf_op jit(solution)/shard_map/ppermute | solution.py:29
  121.8 46.5 %collective-permute-start.1 = (bf16[4,128,1024]{2,1,0:T(8,128)(2,1)S(1)}, bf16[4,128,1024]{2,1,0:T(8,128)(2,1)}, u32[]{:S(2)}, u32[]{:S(2)}) collective-permute-start(bf16[4,128,1024]{2,1,0:T(8,128)(2,1)S(1)} %all-to-all-done.1.refs_0_), channel_id=1, source_target_pairs={{0,32},{32,0},{64,96},{96,64},{1,33},{33,1},{65,97},{97,65},{2,34}... | collective-permute-start | bytes 3145736 | tf_op jit(solution)/shard_map/ppermute | solution.py:29
  132.8 37.5 %copy-start.18 = (f32[2048]{0:T(1024)S(1)}, f32[2048]{0:T(1024)}, u32[]{:S(2)}) copy-start(f32[2048]{0:T(1024)} %param.14) | copy-start | bytes 24580
  132.8 37.8 %copy-start.11 = (bf16[256,128]{1,0:T(8,128)(2,1)S(1)}, bf16[256,128]{1,0:T(8,128)(2,1)}, u32[]{:S(2)}) copy-start(bf16[256,128]{1,0:T(8,128)(2,1)} %keys_ref.3) | copy-start | bytes 196612
  132.8 37.8 %copy-start.17 = (f32[32]{0:T(128)S(1)}, f32[32]{0:T(128)}, u32[]{:S(2)}) copy-start(f32[32]{0:T(128)} %skip_ref.1) | copy-start | bytes 388
  132.8 48.2 %all-to-all-start.6 = ((bf16[8,256,256]{2,1,0:T(8,128)(2,1)}), bf16[8,256,256]{2,1,0:T(8,128)(2,1)S(1)}, u32[]{:S(2)}, u32[]{:S(2)}) async-start(bf16[8,256,256]{2,1,0:T(8,128)(2,1)} %copy-done.5), calls=%async_computation.6 | async-start | bytes 2097152 | tf_op jit(solution)/shard_map/all_to_all | solution.py:353
  136.5 44.5 %collective-permute-start = (bf16[4,128,1024]{2,1,0:T(8,128)(2,1)S(1)}, bf16[4,128,1024]{2,1,0:T(8,128)(2,1)}, u32[]{:S(2)}, u32[]{:S(2)}) collective-permute-start(bf16[4,128,1024]{2,1,0:T(8,128)(2,1)S(1)} %all-to-all-done.1.refs_0_), channel_id=1, source_target_pairs={{0,1},{1,0},{2,3},{3,2},{4,5},{5,4},{6,7},{7,6},{8,9},{9,8},{10,11... | collective-permute-start | bytes 3145736 | tf_op jit(solution)/shard_map/ppermute | solution.py:29
  164.0 17.0 %collective-permute-start.6 = (bf16[4,128,1024]{2,1,0:T(8,128)(2,1)}, bf16[4,128,1024]{2,1,0:T(8,128)(2,1)}, u32[]{:S(2)}, u32[]{:S(2)}) collective-permute-start(bf16[4,128,1024]{2,1,0:T(8,128)(2,1)} %collective-permute-done.5.refs_6_), channel_id=1, source_target_pairs={{0,1},{1,0},{2,3},{3,2},{4,5},{5,4},{6,7},{7,6},{8,9},{9,8},{10,11... | collective-permute-start | bytes 3145736 | tf_op jit(solution)/shard_map/ppermute | solution.py:29
  165.9 15.1 %collective-permute-start.4 = (bf16[4,128,1024]{2,1,0:T(8,128)(2,1)}, bf16[4,128,1024]{2,1,0:T(8,128)(2,1)}, u32[]{:S(2)}, u32[]{:S(2)}) collective-permute-start(bf16[4,128,1024]{2,1,0:T(8,128)(2,1)} %collective-permute-done.3.refs_4_), channel_id=1, source_target_pairs={{0,1},{1,0},{2,3},{3,2},{4,5},{5,4},{6,7},{7,6},{8,9},{9,8},{10,11... | collective-permute-start | bytes 3145736 | tf_op jit(solution)/shard_map/ppermute | solution.py:29
  168.3 12.7 %collective-permute-start.2 = (bf16[4,128,1024]{2,1,0:T(8,128)(2,1)}, bf16[4,128,1024]{2,1,0:T(8,128)(2,1)}, u32[]{:S(2)}, u32[]{:S(2)}) collective-permute-start(bf16[4,128,1024]{2,1,0:T(8,128)(2,1)} %collective-permute-done.1.refs_2_), channel_id=1, source_target_pairs={{0,1},{1,0},{2,3},{3,2},{4,5},{5,4},{6,7},{7,6},{8,9},{9,8},{10,11... | collective-permute-start | bytes 3145736 | tf_op jit(solution)/shard_map/ppermute | solution.py:29
  178.2 1.3 copy-start.6
  179.6 1.3 copy-start.8
  181.0 1.6 copy-start.7
  188.1 32.4 %collective-permute-start.7 = (bf16[256,1024]{1,0:T(8,128)(2,1)S(1)}, bf16[256,1024]{1,0:T(8,128)(2,1)S(1)}, u32[]{:S(2)}, u32[]{:S(2)}) collective-permute-start(bf16[256,1024]{1,0:T(8,128)(2,1)S(1)} %get-tuple-element.16), channel_id=1, source_target_pairs={{0,2},{2,0},{1,3},{3,1},{4,6},{6,4},{5,7},{7,5},{8,10},{10,8},{9,1... | collective-permute-start | bytes 1572872 | tf_op jit(solution)/shard_map/ppermute | solution.py:29
  (9 other events, 9.4 us)

commit v3 on v2

--- a/solution.py
+++ b/solution.py
@@ -137,11 +137,45 @@
     )(skip, vt, gate, keys, query, weights)
 
 
-def read_level(state, message, level, heads, n):
-    rows, tok = state.shape[0], message.shape[1]
-    part = dot(state, message[:n], NN).reshape(heads, rows // heads, tok)
-    first = n + level * heads
-    return (part * message[first : first + heads].astype(f32)[:, None, :]).reshape(rows, tok)
+def pack_kernel(heads, slot, upper_ref, query_ref, w_ref, out_ref):
+    n, tok = query_ref.shape[1], out_ref.shape[1]
+    out_ref[:n] = query_ref[...].T
+    count = upper_ref.shape[0]
+    for e in range(w_ref.shape[1] // heads):
+        rows = [
+            w_ref[LOCAL_LEVELS + level, e * heads : (e + 1) * heads, :].astype(f32) * upper_ref[level]
+            for level in range(count)
+        ]
+        rows.append(jnp.zeros((slot - count * heads, tok), f32))
+        first = n + e * slot
+        out_ref[first : first + slot] = jnp.concatenate(rows, axis=0).astype(bf16)
+
+
+def packed(uppers, query, weights, heads, slot):
+    tok, n = query.shape
+    total = n + weights.shape[1] // heads * slot
+    vmem = pl.BlockSpec(memory_space=pltpu.VMEM)
+    return pl.pallas_call(
+        functools.partial(pack_kernel, heads, slot),
+        in_specs=[pl.BlockSpec(memory_space=pltpu.SMEM), vmem, vmem],
+        out_specs=vmem,
+        out_shape=jax.ShapeDtypeStruct((total, tok), bf16),
+        compiler_params=pltpu.CompilerParams(vmem_limit_bytes=24 * 2**20),
+        cost_estimate=cost(total * tok, 4 * total * tok),
+        name="pack",
+    )(uppers, query, weights)
+
+
+def message_of(ref, j, share, n, slot):
+    first = pl.multiple_of(n + share * slot, slot)
+    return ref[j, :n, :], ref[j, pl.ds(first, slot), :].astype(f32)
+
+
+def read_level(state, message, level, heads):
+    query, weights = message
+    rows, tok = state.shape[0], query.shape[1]
+    part = dot(state, query, NN).reshape(heads, rows // heads, tok)
+    return (part * weights[level * heads : (level + 1) * heads][:, None, :]).reshape(rows, tok)
 
 
 def sibling_sum(ref, index, bit):
@@ -155,7 +189,7 @@
     return total.astype(bf16)
 
 
-def low_kernel(heads, where_ref, raw_ref, line_ref, message_ref, out_ref):
+def low_kernel(heads, slot, where_ref, raw_ref, line_ref, message_ref, out_ref):
     n = raw_ref.shape[2]
     group = raw_ref.shape[0]
     local = {}
@@ -164,32 +198,32 @@
             local[bit, block] = sibling_sum(raw_ref, block + (1 << bit), bit)
     shared = [sibling_sum(line_ref, where_ref[0], bit) for bit in range(2)]
     for j in range(group):
-        message = message_ref[j]
-        total = read_level(shared[0], message, 3, heads, n)
-        total = total + read_level(shared[1], message, 4, heads, n)
+        message = message_of(message_ref, j, where_ref[2], n, slot)
+        total = read_level(shared[0], message, 3, heads)
+        total = total + read_level(shared[1], message, 4, heads)
         for bit in range(3):
             if j >> bit & 1:
                 block = j >> (bit + 1) << (bit + 1)
-                total = total + read_level(local[bit, block], message, bit, heads, n)
+                total = total + read_level(local[bit, block], message, bit, heads)
         out_ref[j] = total
 
 
-def high_kernel(heads, where_ref, part_ref, plane_ref, message_ref, out_ref):
+def high_kernel(heads, slot, where_ref, part_ref, plane_ref, message_ref, out_ref):
     n = plane_ref.shape[2]
     shared = [sibling_sum(plane_ref, where_ref[1], bit) for bit in range(2)]
     for j in range(part_ref.shape[0]):
-        message = message_ref[j]
-        total = part_ref[j] + read_level(shared[0], message, 5, heads, n)
-        total = total + read_level(shared[1], message, 6, heads, n)
+        message = message_of(message_ref, j, where_ref[2], n, slot)
+        total = part_ref[j] + read_level(shared[0], message, 5, heads)
+        total = total + read_level(shared[1], message, 6, heads)
         out_ref[j] = total.astype(bf16)
 
 
-def far_call(kernel, name, heads, where, first, states, message, dtype):
+def far_call(kernel, name, heads, slot, where, first, states, message, dtype):
     group, _, tok = message.shape
     rows = states.shape[1]
     vmem = pl.BlockSpec(memory_space=pltpu.VMEM)
     return pl.pallas_call(
-        functools.partial(kernel, heads),
+        functools.partial(kernel, heads, slot),
         in_specs=[pl.BlockSpec(memory_space=pltpu.SMEM), vmem, vmem, vmem],
         out_specs=vmem,
         out_shape=jax.ShapeDtypeStruct((group, rows, tok), dtype),
@@ -234,7 +268,8 @@
 def piece_specs(pieces, offset):
     _, cols, depth = pieces[0].shape
     return [
-        pl.BlockSpec((1, cols, depth), lambda i, where: (where[offset] + i, 0, 0)) for _ in pieces
+        pl.BlockSpec((1, cols, depth), lambda i, where: ((where[offset] + i) ^ where[4], 0, 0))
+        for _ in pieces
     ]
 
 
@@ -295,12 +330,15 @@
     return lax.all_to_all(spread, axis, 0, 0, tiled=True)
 
 
-def gathered_weight(out_weight):
+def weight_line(out_weight):
     rows, cols = out_weight.shape
     mine = lax.axis_index("rep")
     half = lax.dynamic_slice_in_dim(out_weight, mine * (rows // 2), rows // 2, 0).T
-    line = shared_along(half, "y").reshape(-1, rows // 2)
-    own = shared_along(line, "zl")
+    return shared_along(half, "y").reshape(-1, rows // 2)
+
+
+def weight_pieces(line):
+    own = jnp.stack([line] + [swapped(line, "zl", d) for d in range(1, lax.axis_size("zl"))])
     pieces = []
     for k in range(lax.axis_size("x")):
         piece = own if k == 0 else swapped(own, "x", k)
@@ -318,38 +356,33 @@
     group = lax.axis_size("y")
     heads = head_count // group
     rows = width // group
+    slot = 32
     axes = [("y", b) for b in range(3)] + [("x", b) for b in range(2)] + [("zl", b) for b in range(2)]
-    uppers = jnp.stack([(lax.axis_index(a) >> b) & 1 for a, b in axes])
-    head = lax.axis_index("head")
+    uppers = jnp.stack([(lax.axis_index(a) >> b) & 1 for a, b in axes]).astype(f32)
+    x, y, z, head = (lax.axis_index(a) for a in ("x", "y", "zl", "head"))
     z_half = lax.axis_size("zl") // 2
-    place = jnp.stack([lax.axis_index("x"), lax.axis_index("zl")]).astype(jnp.int32)
+    place = jnp.stack([x, z, y]).astype(jnp.int32)
     where = jnp.stack(
-        [lax.axis_index("x"), lax.axis_index("rep"), (1 - head) * z_half, head * z_half]
+        [x, lax.axis_index("rep"), (1 - head) * z_half, head * z_half, z]
     ).astype(jnp.int32)
 
+    weight = weight_line(out_weight)
+    message = packed(uppers, seq_queries, level_weights, heads, slot)
+    message = lax.all_gather(message, "y", axis=0)
     vt, sent = own_state(seq_values, seq_keys)
+    sent, weight = lax.optimization_barrier((sent, weight))
     raw = lax.all_to_all(sent.reshape(group, rows, n), "y", 0, 0, tiled=True)
-    pieces = gathered_weight(out_weight)
-
-    far_weights = level_weights[LOCAL_LEVELS:] * uppers[:, None, None].astype(bf16)
-    levels = len(axes)
-    far_weights = far_weights.reshape(levels, group, heads, tok).swapaxes(0, 1)
-    far_weights = far_weights.reshape(group, levels * heads, tok)
-    far_weights = jnp.pad(far_weights, ((0, 0), (0, -levels * heads % 16), (0, 0)))
-    message = jnp.concatenate(
-        [jnp.broadcast_to(seq_queries.T[None], (group, n, tok)), far_weights], axis=1
-    )
-    message = lax.all_to_all(message, "y", 0, 0, tiled=True)
+    pieces = weight_pieces(weight)
+    acc, silu = local_part(vt, seq_gate, seq_keys, seq_queries, level_weights, skip_gain, head_size)
+    raw, acc, silu = lax.optimization_barrier((raw, acc, silu))
 
     def summed(blocks):
         return jnp.sum(blocks.astype(f32), axis=0).astype(bf16)
 
     line = shared_along(summed(raw), "x")
     plane = shared_along(summed(line), "zl")
-
-    acc, silu = local_part(vt, seq_gate, seq_keys, seq_queries, level_weights, skip_gain, head_size)
-    part = far_call(low_kernel, "low_levels", heads, place, raw, line, message, f32)
-    far = far_call(high_kernel, "high_levels", heads, place, part, plane, message, bf16)
+    part = far_call(low_kernel, "low_levels", heads, slot, place, raw, line, message, f32)
+    far = far_call(high_kernel, "high_levels", heads, slot, place, part, plane, message, bf16)
     far = lax.all_to_all(far, "y", 0, 0, tiled=True).reshape(width, tok)
 
     to_send, normed = finish(where, pieces, acc, silu, far, norm_gain[:, None])

time: 223 us -> 180 us (0.81)
  waiting for transfers between devices: 99.7 us -> 53.9 us
  between operations: 0.41 us -> 13.7 us
  blocking collectives: 22.1 us -> 10.7 us
  starting transfers between devices: 58.9 us -> 62.2 us
  local copies, waits for them, and re-layouts: 18.9 us -> 16.1 us
    all_to_all x4 -> x2, waiting for transfers between devices: 36.5 us -> 7.83 us  [shared_along(): return lax.all_to_all(spread, axis, 0, 0, tiled=True)]
    all_to_all x1, waiting for transfers between devices: 17.5 us -> 1.42 us  [on_device(): raw = lax.all_to_all(sent.reshape(group, rows, n), 'y', 0, 0, tiled=True)]
    ppermute x8 -> x11, starting transfers between devices: 26.2 us -> 40 us  [swapped(): lax.ppermute(value, axis, [(i, i ^ mask) for i in range(lax.axis_size(axi...]
    all_to_all x1, blocking collectives: 22.1 us -> 10.7 us  [shared_along(): return lax.all_to_all(spread, axis, 0, 0, tiled=True)]
    all_to_all x4 -> x2, starting transfers between devices: 21.9 us -> 14.5 us  [shared_along(): return lax.all_to_all(spread, axis, 0, 0, tiled=True)]
    all_to_all x1, starting transfers between devices: 7.1 us -> 3.49 us  [on_device(): raw = lax.all_to_all(sent.reshape(group, rows, n), 'y', 0, 0, tiled=True)]
    pallas_call x2 -> x3, Pallas kernels: 3.29 us -> 4.58 us  [the longest x2 3.29 us: far_call(): pl.pallas_call(functools.partial(kernel, heads, slot), in_specs=[pl.Block...]
    ppermute x8 -> x11, waiting for transfers between devices: 45.7 us -> 44.6 us  [swapped(): lax.ppermute(value, axis, [(i, i ^ mask) for i in range(lax.axis_size(axi...]
  transfers between devices with their start and end apart: 14 -> 16, of which waited for: 6 -> 7; matrix products, arithmetic and copies ran while one was open for 1% -> 2% of each run, Pallas kernels for 5% -> 8%
where the time goes in v3:
time: 180 us; the launch traced here: 179 us
  starting transfers between devices  62.2 us (35%)
  waiting for transfers between devices  53.9 us (30%)
  Pallas kernels  20.4 us (11%)
  local copies, waits for them, and re-layouts  16.1 us (9%)
  between operations  13.7 us (8%)
  blocking collectives  10.7 us (6%)
  other arithmetic  2.3 us (1%)
    ppermute x11, waiting for transfers between devices, swapped(): lax.ppermute(value, axis, [(i, i ^ mask) for i in range(lax.axis_size(axi...  44.6 us
    ppermute x11, starting transfers between devices, swapped(): lax.ppermute(value, axis, [(i, i ^ mask) for i in range(lax.axis_size(axi...  40 us
    all_to_all x2, starting transfers between devices, shared_along(): return lax.all_to_all(spread, axis, 0, 0, tiled=True)  14.5 us
    unnamed x42, local copies, waits for them, and re-layouts  14.1 us
    all_to_all x1, blocking collectives, shared_along(): return lax.all_to_all(spread, axis, 0, 0, tiled=True)  10.7 us
    all_to_all x2, waiting for transfers between devices, shared_along(): return lax.all_to_all(spread, axis, 0, 0, tiled=True)  7.83 us
    pallas_call x1, Pallas kernels, finish(): pl.pallas_call(finish_kernel, grid_spec=pltpu.PrefetchScalarGridSpec(num_...  5.5 us
    pallas_call x1, Pallas kernels, local_part(): pl.pallas_call(functools.partial(local_kernel, heads, tok // 2), grid=(st...  4.17 us
  transfers between devices with their start and end apart: 16, of which 7 were waited for; matrix products, arithmetic and copies ran while one was open for 2% of the time, Pallas kernels for 8%

profile of v3, /device:TPU:64, one launch (start us, length us, event | category | flops | bytes accessed | tf_op | source)
XLA Modules:
  0.0 179.3 jit_solution(3557427869932002939)
XLA Ops:
  10.6 7.1 %all-to-all-start = ((bf16[8,16,1024]{2,1,0:T(8,128)(2,1)}), bf16[8,16,1024]{2,1,0:T(8,128)(2,1)S(1)}, u32[]{:S(2)}, u32[]{:S(2)}) async-start(bf16[8,16,1024]{2,1,0:T(8,128)(2,1)} %broadcast_in_dim.8), calls=%async_computation | async-start | bytes 524288 | tf_op jit(solution)/shard_map/all_to_all | solution.py:330
  18.5 2.2 %own_state.1 = (bf16[2048,256]{1,0:T(8,128)(2,1)S(1)}, bf16[2048,128]{1,0:T(8,128)(2,1)}) custom-call(bf16[256,2048]{1,0:T(8,128)(2,1)S(1)} %copy-done.9, bf16[256,128]{1,0:T(8,128)(2,1)S(1)} %copy-done.12), custom_call_target="tpu_custom_call" | custom-call | flops 134217728 | bytes 2097152 | tf_op jit(solution)/shard_map/own_state/pallas_call | solution.py:46
  21.7 7.8 %all-to-all-done = bf16[8,16,1024]{2,1,0:T(8,128)(2,1)S(1)} async-done(((bf16[8,16,1024]{2,1,0:T(8,128)(2,1)}), bf16[8,16,1024]{2,1,0:T(8,128)(2,1)S(1)}, u32[]{:S(2)}, u32[]{:S(2)}) %all-to-all-start) | async-done | bytes 262176 | tf_op jit(solution)/shard_map/all_to_all | solution.py:330
  29.6 3.5 %all-to-all-start.1 = ((bf16[8,256,128]{2,1,0:T(8,128)(2,1)}), bf16[8,256,128]{2,1,0:T(8,128)(2,1)S(1)}, u32[]{:S(2)}, u32[]{:S(2)}) async-start(bf16[8,256,128]{2,1,0:T(8,128)(2,1)} %bitcast.11), calls=%async_computation.1 | async-start | bytes 1048576 | tf_op jit(solution)/shard_map/all_to_all | solution.py:374
  33.1 4.3 %collective-permute-start.2 = (bf16[128,1024]{1,0:T(8,128)(2,1)S(1)}, bf16[128,1024]{1,0:T(8,128)(2,1)S(1)}, u32[]{:S(2)}, u32[]{:S(2)}) collective-permute-start(bf16[128,1024]{1,0:T(8,128)(2,1)S(1)} %bitcast.27), channel_id=1, source_target_pairs={{0,384},{128,256},{256,128},{384,0},{1,385},{129,257},{257,129},{3... | collective-permute-start | bytes 786440 | tf_op jit(solution)/shard_map/ppermute | solution.py:29
  37.4 5.2 %collective-permute-start = (bf16[128,1024]{1,0:T(8,128)(2,1)S(1)}, bf16[128,1024]{1,0:T(8,128)(2,1)}, u32[]{:S(2)}, u32[]{:S(2)}) collective-permute-start(bf16[128,1024]{1,0:T(8,128)(2,1)S(1)} %bitcast.28), channel_id=1, source_target_pairs={{0,128},{128,0},{256,384},{384,256},{1,129},{129,1},{257,385},{385... | collective-permute-start | bytes 786440 | tf_op jit(solution)/shard_map/ppermute | solution.py:29
  42.6 1.9 %collective-permute-start.1 = (bf16[128,1024]{1,0:T(8,128)(2,1)S(1)}, bf16[128,1024]{1,0:T(8,128)(2,1)}, u32[]{:S(2)}, u32[]{:S(2)}) collective-permute-start(bf16[128,1024]{1,0:T(8,128)(2,1)S(1)} %bitcast.29), channel_id=1, source_target_pairs={{0,256},{128,384},{256,0},{384,128},{1,257},{129,385},{257,1},{385... | collective-permute-start | bytes 786440 | tf_op jit(solution)/shard_map/ppermute | solution.py:29
  45.8 4.2 %local_part.1 = (f32[2048,256]{1,0:T(8,128)S(1)}, f32[2048,256]{1,0:T(8,128)S(1)}) custom-call(f32[32]{0:T(128)S(1)} %copy-done.19, bf16[2048,256]{1,0:T(8,128)(2,1)S(1)} %copy-done.18, bf16[256,2048]{1,0:T(8,128)(2,1)S(1)} %copy-done.16, bf16[256,128]{1,0:T(8,128)(2,1)S(1)} %copy-done.13, bf16[256,128]{1,0:T(8,128)(2,1)S(1)} %copy-done.15, ...), custom_call_target="tpu_custom_call" | custom-call | flops 1073741824 | bytes 6291456 | tf_op jit(solution)/shard_map/local_part/pallas_call | solution.py:117
  54.2 10.7 %all_to_all.25.line_ref = bf16[4,256,128]{2,1,0:T(8,128)(2,1)S(1)} all-to-all(bf16[4,256,128]{2,1,0:T(8,128)(2,1)S(1)} %broadcast_in_dim.9), channel_id=1, replica_groups=mesh['zl'=4,'x'=4,'y'=8,'head'=2,'rep'=2] {'x'}, dimensions={0} | all-to-all | bytes 524288 | tf_op jit(solution)/shard_map/all_to_all | solution.py:330
  65.6 7.4 %all-to-all-start.3 = ((bf16[4,256,128]{2,1,0:T(8,128)(2,1)}), bf16[4,256,128]{2,1,0:T(8,128)(2,1)}, u32[]{:S(2)}, u32[]{:S(2)}) async-start(bf16[4,256,128]{2,1,0:T(8,128)(2,1)} %broadcast_in_dim.10), calls=%async_computation.3 | async-start | bytes 524288 | tf_op jit(solution)/shard_map/all_to_all | solution.py:330
  74.2 2.5 %collective-permute-start.4 = (bf16[4,128,1024]{2,1,0:T(8,128)(2,1)S(1)}, bf16[4,128,1024]{2,1,0:T(8,128)(2,1)}, u32[]{:S(2)}, u32[]{:S(2)}) collective-permute-start(bf16[4,128,1024]{2,1,0:T(8,128)(2,1)S(1)} %pad_maximum_fusion.refs_0_), channel_id=1, source_target_pairs={{0,32},{32,0},{64,96},{96,64},{1,33},{33,1},{65,97},{97,65},{2,34}... | collective-permute-start | bytes 3145736 | tf_op jit(solution)/shard_map/ppermute | solution.py:29
  76.7 4.0 %collective-permute-start.6 = (bf16[4,128,1024]{2,1,0:T(8,128)(2,1)S(1)}, bf16[4,128,1024]{2,1,0:T(8,128)(2,1)}, u32[]{:S(2)}, u32[]{:S(2)}) collective-permute-start(bf16[4,128,1024]{2,1,0:T(8,128)(2,1)S(1)} %pad_maximum_fusion.refs_0_), channel_id=1, source_target_pairs={{0,64},{32,96},{64,0},{96,32},{1,65},{33,97},{65,1},{97,33},{2,66}... | collective-permute-start | bytes 3145736 | tf_op jit(solution)/shard_map/ppermute | solution.py:29
  80.7 4.0 %collective-permute-start.8 = (bf16[4,128,1024]{2,1,0:T(8,128)(2,1)S(1)}, bf16[4,128,1024]{2,1,0:T(8,128)(2,1)}, u32[]{:S(2)}, u32[]{:S(2)}) collective-permute-start(bf16[4,128,1024]{2,1,0:T(8,128)(2,1)S(1)} %pad_maximum_fusion.refs_0_), channel_id=1, source_target_pairs={{0,96},{32,64},{64,32},{96,0},{1,97},{33,65},{65,33},{97,1},{2,98}... | collective-permute-start | bytes 3145736 | tf_op jit(solution)/shard_map/ppermute | solution.py:29
  93.0 4.1 %all-to-all-start.4 = ((bf16[8,256,256]{2,1,0:T(8,128)(2,1)}), bf16[8,256,256]{2,1,0:T(8,128)(2,1)S(1)}, u32[]{:S(2)}, u32[]{:S(2)}) async-start(bf16[8,256,256]{2,1,0:T(8,128)(2,1)} %copy-done.5), calls=%async_computation.4 | async-start | bytes 2097152 | tf_op jit(solution)/shard_map/all_to_all | solution.py:386
  99.0 3.3 %collective-permute-done.4.refs_2_ = bf16[4,128,1024]{2,1,0:T(8,128)(2,1)} collective-permute-done((bf16[4,128,1024]{2,1,0:T(8,128)(2,1)S(1)}, bf16[4,128,1024]{2,1,0:T(8,128)(2,1)}, u32[]{:S(2)}, u32[]{:S(2)}) %collective-permute-start.4) | collective-permute-done | bytes 1048608 | tf_op jit(solution)/shard_map/ppermute | solution.py:29
  102.3 1.9 %collective-permute-start.5 = (bf16[4,128,1024]{2,1,0:T(8,128)(2,1)}, bf16[4,128,1024]{2,1,0:T(8,128)(2,1)}, u32[]{:S(2)}, u32[]{:S(2)}) collective-permute-start(bf16[4,128,1024]{2,1,0:T(8,128)(2,1)} %collective-permute-done.4.refs_2_), channel_id=1, source_target_pairs={{0,1},{1,0},{2,3},{3,2},{4,5},{5,4},{6,7},{7,6},{8,9},{9,8},{10,11... | collective-permute-start | bytes 3145736 | tf_op jit(solution)/shard_map/ppermute | solution.py:29
  104.3 14.5 %collective-permute-done.6.refs_4_ = bf16[4,128,1024]{2,1,0:T(8,128)(2,1)} collective-permute-done((bf16[4,128,1024]{2,1,0:T(8,128)(2,1)S(1)}, bf16[4,128,1024]{2,1,0:T(8,128)(2,1)}, u32[]{:S(2)}, u32[]{:S(2)}) %collective-permute-start.6) | collective-permute-done | bytes 1048608 | tf_op jit(solution)/shard_map/ppermute | solution.py:29
  118.7 1.9 %collective-permute-start.7 = (bf16[4,128,1024]{2,1,0:T(8,128)(2,1)}, bf16[4,128,1024]{2,1,0:T(8,128)(2,1)}, u32[]{:S(2)}, u32[]{:S(2)}) collective-permute-start(bf16[4,128,1024]{2,1,0:T(8,128)(2,1)} %collective-permute-done.6.refs_4_), channel_id=1, source_target_pairs={{0,1},{1,0},{2,3},{3,2},{4,5},{5,4},{6,7},{7,6},{8,9},{9,8},{10,11... | collective-permute-start | bytes 3145736 | tf_op jit(solution)/shard_map/ppermute | solution.py:29
  120.6 4.5 %collective-permute-done.8.refs_6_ = bf16[4,128,1024]{2,1,0:T(8,128)(2,1)} collective-permute-done((bf16[4,128,1024]{2,1,0:T(8,128)(2,1)S(1)}, bf16[4,128,1024]{2,1,0:T(8,128)(2,1)}, u32[]{:S(2)}, u32[]{:S(2)}) %collective-permute-start.8) | collective-permute-done | bytes 1048608 | tf_op jit(solution)/shard_map/ppermute | solution.py:29
  127.5 2.5 %collective-permute-done.9.refs_7_ = bf16[4,128,1024]{2,1,0:T(8,128)(2,1)} collective-permute-done((bf16[4,128,1024]{2,1,0:T(8,128)(2,1)}, bf16[4,128,1024]{2,1,0:T(8,128)(2,1)}, u32[]{:S(2)}, u32[]{:S(2)}) %collective-permute-start.9) | collective-permute-done | bytes 1048608 | tf_op jit(solution)/shard_map/ppermute | solution.py:29
  131.6 5.5 %finish.1 = (bf16[256,1024]{1,0:T(8,128)(2,1)S(1)}, bf16[2,1024,256]{2,1,0:T(8,128)(2,1)S(1)}) custom-call(s32[5]{0:T(128)S(1)} %stack.70.where_ref, bf16[4,128,1024]{2,1,0:T(8,128)(2,1)S(1)} %pad_maximum_fusion.refs_0_, bf16[4,128,1024]{2,1,0:T(8,128)(2,1)} %collective-permute-done.3.refs_1_, bf16[4,128,1024]{2,1,0:T(8,128)(2,1)} %collective-permute-done.4.refs_2_, ...), custom_call_target="tpu_custom_call" | custom-call | flops 1073741824 | bytes 16777216 | tf_op jit(solution)/shard_map/finish/pallas_call | solution.py:286
  137.1 10.6 %collective-permute-start.10 = (bf16[256,1024]{1,0:T(8,128)(2,1)S(1)}, bf16[256,1024]{1,0:T(8,128)(2,1)S(1)}, u32[]{:S(2)}, u32[]{:S(2)}) collective-permute-start(bf16[256,1024]{1,0:T(8,128)(2,1)S(1)} %get-tuple-element.26), channel_id=1, source_target_pairs={{0,2},{2,0},{1,3},{3,1},{4,6},{6,4},{5,7},{7,5},{8,10},{10,8},{9,1... | collective-permute-start | bytes 1572872 | tf_op jit(solution)/shard_map/ppermute | solution.py:29
  147.7 3.9 %keep.1 = f32[256,1024]{1,0:T(8,128)S(1)} custom-call(s32[5]{0:T(128)S(1)} %stack.70.where_ref, bf16[4,128,1024]{2,1,0:T(8,128)(2,1)S(1)} %pad_maximum_fusion.refs_0_, bf16[4,128,1024]{2,1,0:T(8,128)(2,1)} %collective-permute-done.3.refs_1_, bf16[4,128,1024]{2,1,0:T(8,128)(2,1)} %collective-permute-done.4.refs_2_, ...), custom_call_target="tpu_custom_call" | custom-call | flops 1073741824 | bytes 8388608 | tf_op jit(solution)/shard_map/keep/pallas_call | solution.py:312
  151.7 19.8 %collective-permute-done.10 = bf16[256,1024]{1,0:T(8,128)(2,1)S(1)} collective-permute-done((bf16[256,1024]{1,0:T(8,128)(2,1)S(1)}, bf16[256,1024]{1,0:T(8,128)(2,1)S(1)}, u32[]{:S(2)}, u32[]{:S(2)}) %collective-permute-start.10) | collective-permute-done | bytes 524320 | tf_op jit(solution)/shard_map/ppermute | solution.py:29
  (72 shorter events, 28.3 us)
Async XLA Ops:
  6.5 11.2 %copy-start.9 = (bf16[256,2048]{1,0:T(8,128)(2,1)S(1)}, bf16[256,2048]{1,0:T(8,128)(2,1)}, u32[]{:S(2)}) copy-start(bf16[256,2048]{1,0:T(8,128)(2,1)} %values_ref.1) | copy-start | bytes 3145732
  6.5 78.2 %all-gather.3.cloned.1.call-start = ((), (), s32[]{:S(2)}) async-start(), calls=%async_computation.5 | async-start | bytes 1769472 | tf_op jit(solution)/shard_map/all_gather | solution.py:371
  8.5 36.0 %copy-start.11 = (bf16[16,32,256]{2,1,0:T(8,128)(2,1)S(1)}, bf16[16,32,256]{2,1,0:T(8,128)(2,1)}, u32[]{:S(2)}) copy-start(bf16[16,32,256]{2,1,0:T(8,128)(2,1)} %w_ref.3) | copy-start | bytes 786436
  8.5 36.0 %copy-start.13 = (bf16[256,128]{1,0:T(8,128)(2,1)S(1)}, bf16[256,128]{1,0:T(8,128)(2,1)}, u32[]{:S(2)}) copy-start(bf16[256,128]{1,0:T(8,128)(2,1)} %keys_ref.3) | copy-start | bytes 196612
  8.5 36.0 %copy-start.15 = (bf16[256,128]{1,0:T(8,128)(2,1)S(1)}, bf16[256,128]{1,0:T(8,128)(2,1)}, u32[]{:S(2)}) copy-start(bf16[256,128]{1,0:T(8,128)(2,1)} %query_ref.3) | copy-start | bytes 196612
  8.5 36.0 %copy-start.19 = (f32[32]{0:T(128)S(1)}, f32[32]{0:T(128)}, u32[]{:S(2)}) copy-start(f32[32]{0:T(128)} %skip_ref.1) | copy-start | bytes 388
  10.6 19.0 %all-to-all-start = ((bf16[8,16,1024]{2,1,0:T(8,128)(2,1)}), bf16[8,16,1024]{2,1,0:T(8,128)(2,1)S(1)}, u32[]{:S(2)}, u32[]{:S(2)}) async-start(bf16[8,16,1024]{2,1,0:T(8,128)(2,1)} %broadcast_in_dim.8), calls=%async_computation | async-start | bytes 524288 | tf_op jit(solution)/shard_map/all_to_all | solution.py:330
  18.5 26.0 %copy-start.16 = (bf16[256,2048]{1,0:T(8,128)(2,1)S(1)}, bf16[256,2048]{1,0:T(8,128)(2,1)}, u32[]{:S(2)}) copy-start(bf16[256,2048]{1,0:T(8,128)(2,1)} %gate_ref.1) | copy-start | bytes 3145732
  29.6 24.5 %all-to-all-start.1 = ((bf16[8,256,128]{2,1,0:T(8,128)(2,1)}), bf16[8,256,128]{2,1,0:T(8,128)(2,1)S(1)}, u32[]{:S(2)}, u32[]{:S(2)}) async-start(bf16[8,256,128]{2,1,0:T(8,128)(2,1)} %bitcast.11), calls=%async_computation.1 | async-start | bytes 1048576 | tf_op jit(solution)/shard_map/all_to_all | solution.py:374
  33.1 40.0 %collective-permute-start.2 = (bf16[128,1024]{1,0:T(8,128)(2,1)S(1)}, bf16[128,1024]{1,0:T(8,128)(2,1)S(1)}, u32[]{:S(2)}, u32[]{:S(2)}) collective-permute-start(bf16[128,1024]{1,0:T(8,128)(2,1)S(1)} %bitcast.27), channel_id=1, source_target_pairs={{0,384},{128,256},{256,128},{384,0},{1,385},{129,257},{257,129},{3... | collective-permute-start | bytes 786440 | tf_op jit(solution)/shard_map/ppermute | solution.py:29
  37.4 35.7 %collective-permute-start = (bf16[128,1024]{1,0:T(8,128)(2,1)S(1)}, bf16[128,1024]{1,0:T(8,128)(2,1)}, u32[]{:S(2)}, u32[]{:S(2)}) collective-permute-start(bf16[128,1024]{1,0:T(8,128)(2,1)S(1)} %bitcast.28), channel_id=1, source_target_pairs={{0,128},{128,0},{256,384},{384,256},{1,129},{129,1},{257,385},{385... | collective-permute-start | bytes 786440 | tf_op jit(solution)/shard_map/ppermute | solution.py:29
  42.6 30.5 %collective-permute-start.1 = (bf16[128,1024]{1,0:T(8,128)(2,1)S(1)}, bf16[128,1024]{1,0:T(8,128)(2,1)}, u32[]{:S(2)}, u32[]{:S(2)}) collective-permute-start(bf16[128,1024]{1,0:T(8,128)(2,1)S(1)} %bitcast.29), channel_id=1, source_target_pairs={{0,256},{128,384},{256,0},{384,128},{1,257},{129,385},{257,1},{385... | collective-permute-start | bytes 786440 | tf_op jit(solution)/shard_map/ppermute | solution.py:29
  54.0 19.0 %copy-start.3 = (bf16[8,256,128]{2,1,0:T(8,128)(2,1)}, bf16[8,256,128]{2,1,0:T(8,128)(2,1)S(1)}, u32[]{:S(2)}) copy-start(bf16[8,256,128]{2,1,0:T(8,128)(2,1)S(1)} %all-to-all-done.1.raw_ref) | copy-start | bytes 1572868
  65.6 23.2 %all-to-all-start.3 = ((bf16[4,256,128]{2,1,0:T(8,128)(2,1)}), bf16[4,256,128]{2,1,0:T(8,128)(2,1)}, u32[]{:S(2)}, u32[]{:S(2)}) async-start(bf16[4,256,128]{2,1,0:T(8,128)(2,1)} %broadcast_in_dim.10), calls=%async_computation.3 | async-start | bytes 524288 | tf_op jit(solution)/shard_map/all_to_all | solution.py:330
  74.2 28.1 %collective-permute-start.4 = (bf16[4,128,1024]{2,1,0:T(8,128)(2,1)S(1)}, bf16[4,128,1024]{2,1,0:T(8,128)(2,1)}, u32[]{:S(2)}, u32[]{:S(2)}) collective-permute-start(bf16[4,128,1024]{2,1,0:T(8,128)(2,1)S(1)} %pad_maximum_fusion.refs_0_), channel_id=1, source_target_pairs={{0,32},{32,0},{64,96},{96,64},{1,33},{33,1},{65,97},{97,65},{2,34}... | collective-permute-start | bytes 3145736 | tf_op jit(solution)/shard_map/ppermute | solution.py:29
  76.7 42.0 %collective-permute-start.6 = (bf16[4,128,1024]{2,1,0:T(8,128)(2,1)S(1)}, bf16[4,128,1024]{2,1,0:T(8,128)(2,1)}, u32[]{:S(2)}, u32[]{:S(2)}) collective-permute-start(bf16[4,128,1024]{2,1,0:T(8,128)(2,1)S(1)} %pad_maximum_fusion.refs_0_), channel_id=1, source_target_pairs={{0,64},{32,96},{64,0},{96,32},{1,65},{33,97},{65,1},{97,33},{2,66}... | collective-permute-start | bytes 3145736 | tf_op jit(solution)/shard_map/ppermute | solution.py:29
  80.7 44.4 %collective-permute-start.8 = (bf16[4,128,1024]{2,1,0:T(8,128)(2,1)S(1)}, bf16[4,128,1024]{2,1,0:T(8,128)(2,1)}, u32[]{:S(2)}, u32[]{:S(2)}) collective-permute-start(bf16[4,128,1024]{2,1,0:T(8,128)(2,1)S(1)} %pad_maximum_fusion.refs_0_), channel_id=1, source_target_pairs={{0,96},{32,64},{64,32},{96,0},{1,97},{33,65},{65,33},{97,1},{2,98}... | collective-permute-start | bytes 3145736 | tf_op jit(solution)/shard_map/ppermute | solution.py:29
  93.0 34.1 %copy-start.20 = (f32[2048]{0:T(1024)S(1)}, f32[2048]{0:T(1024)}, u32[]{:S(2)}) copy-start(f32[2048]{0:T(1024)} %param.14) | copy-start | bytes 24580
  93.0 37.0 %all-to-all-start.4 = ((bf16[8,256,256]{2,1,0:T(8,128)(2,1)}), bf16[8,256,256]{2,1,0:T(8,128)(2,1)S(1)}, u32[]{:S(2)}, u32[]{:S(2)}) async-start(bf16[8,256,256]{2,1,0:T(8,128)(2,1)} %copy-done.5), calls=%async_computation.4 | async-start | bytes 2097152 | tf_op jit(solution)/shard_map/all_to_all | solution.py:386
  97.1 30.4 %collective-permute-start.3 = (bf16[4,128,1024]{2,1,0:T(8,128)(2,1)S(1)}, bf16[4,128,1024]{2,1,0:T(8,128)(2,1)}, u32[]{:S(2)}, u32[]{:S(2)}) collective-permute-start(bf16[4,128,1024]{2,1,0:T(8,128)(2,1)S(1)} %pad_maximum_fusion.refs_0_), channel_id=1, source_target_pairs={{0,1},{1,0},{2,3},{3,2},{4,5},{5,4},{6,7},{7,6},{8,9},{9,8},{10,11... | collective-permute-start | bytes 3145736 | tf_op jit(solution)/shard_map/ppermute | solution.py:29
  102.3 25.2 %collective-permute-start.5 = (bf16[4,128,1024]{2,1,0:T(8,128)(2,1)}, bf16[4,128,1024]{2,1,0:T(8,128)(2,1)}, u32[]{:S(2)}, u32[]{:S(2)}) collective-permute-start(bf16[4,128,1024]{2,1,0:T(8,128)(2,1)} %collective-permute-done.4.refs_2_), channel_id=1, source_target_pairs={{0,1},{1,0},{2,3},{3,2},{4,5},{5,4},{6,7},{7,6},{8,9},{9,8},{10,11... | collective-permute-start | bytes 3145736 | tf_op jit(solution)/shard_map/ppermute | solution.py:29
  118.7 8.8 %collective-permute-start.7 = (bf16[4,128,1024]{2,1,0:T(8,128)(2,1)}, bf16[4,128,1024]{2,1,0:T(8,128)(2,1)}, u32[]{:S(2)}, u32[]{:S(2)}) collective-permute-start(bf16[4,128,1024]{2,1,0:T(8,128)(2,1)} %collective-permute-done.6.refs_4_), channel_id=1, source_target_pairs={{0,1},{1,0},{2,3},{3,2},{4,5},{5,4},{6,7},{7,6},{8,9},{9,8},{10,11... | collective-permute-start | bytes 3145736 | tf_op jit(solution)/shard_map/ppermute | solution.py:29
  125.1 4.9 %collective-permute-start.9 = (bf16[4,128,1024]{2,1,0:T(8,128)(2,1)}, bf16[4,128,1024]{2,1,0:T(8,128)(2,1)}, u32[]{:S(2)}, u32[]{:S(2)}) collective-permute-start(bf16[4,128,1024]{2,1,0:T(8,128)(2,1)} %collective-permute-done.8.refs_6_), channel_id=1, source_target_pairs={{0,1},{1,0},{2,3},{3,2},{4,5},{5,4},{6,7},{7,6},{8,9},{9,8},{10,11... | collective-permute-start | bytes 3145736 | tf_op jit(solution)/shard_map/ppermute | solution.py:29
  137.1 34.4 %collective-permute-start.10 = (bf16[256,1024]{1,0:T(8,128)(2,1)S(1)}, bf16[256,1024]{1,0:T(8,128)(2,1)S(1)}, u32[]{:S(2)}, u32[]{:S(2)}) collective-permute-start(bf16[256,1024]{1,0:T(8,128)(2,1)S(1)} %get-tuple-element.26), channel_id=1, source_target_pairs={{0,2},{2,0},{1,3},{3,1},{4,6},{6,4},{5,7},{7,5},{8,10},{10,8},{9,1... | collective-permute-start | bytes 1572872 | tf_op jit(solution)/shard_map/ppermute | solution.py:29
  (13 other events, 17.4 us)
Sparse Core Ops, SparseCore 0:
  9.9 52.9 all-gather.2

commit v4 on v2

--- a/solution.py
+++ b/solution.py
@@ -9,6 +9,7 @@
 
 epsilon = 1e-05
 LOCAL_LEVELS = 9
+VMEM_MIB = 56
 NN = (((1,), (0,)), ((), ()))
 NT = (((1,), (1,)), ((), ()))
 f32 = jnp.float32
@@ -33,35 +34,57 @@
     return lax.dot_general(a, b, dims, preferred_element_type=f32)
 
 
-def state_kernel(values_ref, keys_ref, vt_ref, sent_ref):
+def send_kernel(heads, slot, upper_ref, values_ref, keys_ref, query_ref, w_ref, vt_ref, sent_ref):
     vt = values_ref[...].T
     vt_ref[...] = vt
-    sent_ref[...] = dot(vt, keys_ref[...], NN).astype(bf16)
-
-
-def own_state(values, keys):
+    state = dot(vt, keys_ref[...], NN).astype(bf16)
+    tok, n = query_ref.shape
+    count = upper_ref.shape[0]
+    shares = sent_ref.shape[0]
+    rows = state.shape[0] // shares
+    for e in range(shares):
+        w = [
+            w_ref[LOCAL_LEVELS + level, e * heads : (e + 1) * heads, :].astype(f32) * upper_ref[level]
+            for level in range(count)
+        ]
+        w.append(jnp.zeros((slot - count * heads, tok), f32))
+        w = jnp.concatenate(w, axis=0).astype(bf16)
+        sent_ref[e, :rows] = state[e * rows : (e + 1) * rows]
+        sent_ref[e, rows : rows + tok] = query_ref[...]
+        for k in range(tok // n):
+            first = rows + tok + k * slot
+            sent_ref[e, first : first + slot] = w[:, k * n : (k + 1) * n]
+
+
+def to_group(uppers, values, keys, query, weights, group, slot):
     tok, width = values.shape
-    cols = width // 4
     n = keys.shape[1]
-    return pl.pallas_call(
-        state_kernel,
-        grid=(4,),
+    steps = 4
+    cols = width // steps
+    heads = weights.shape[1] // group
+    rows = width // group + tok + tok // n * slot
+    return pl.pallas_call(
+        functools.partial(send_kernel, heads, slot),
+        grid=(steps,),
         in_specs=[
+            pl.BlockSpec(memory_space=pltpu.SMEM),
             pl.BlockSpec((tok, cols), lambda i: (0, i)),
             pl.BlockSpec((tok, n), lambda i: (0, 0)),
+            pl.BlockSpec((tok, n), lambda i: (0, 0)),
+            pl.BlockSpec((16, group // steps * heads, tok), lambda i: (0, i, 0)),
         ],
         out_specs=[
             pl.BlockSpec((cols, tok), lambda i: (i, 0)),
-            pl.BlockSpec((cols, n), lambda i: (i, 0)),
+            pl.BlockSpec((group // steps, rows, n), lambda i: (i, 0, 0)),
         ],
         out_shape=[
             jax.ShapeDtypeStruct((width, tok), bf16),
-            jax.ShapeDtypeStruct((width, n), bf16),
-        ],
-        compiler_params=params(24),
+            jax.ShapeDtypeStruct((group, rows, n), bf16),
+        ],
+        compiler_params=params(VMEM_MIB),
         cost_estimate=cost(2 * tok * width * n, 4 * tok * width),
-        name="own_state",
-    )(values, keys)
+        name="to_group",
+    )(uppers, values, keys, query, weights)
 
 
 def local_kernel(heads, half, skip_ref, vt_ref, gate_ref, keys_ref, query_ref, w_ref, acc_ref, silu_ref, score_ref):
@@ -131,72 +154,70 @@
         ],
         out_shape=[jax.ShapeDtypeStruct((cols, tok), f32)] * 2,
         scratch_shapes=[pltpu.VMEM((tok, tok), f32)],
-        compiler_params=params(24),
+        compiler_params=params(VMEM_MIB),
         cost_estimate=cost(8 * tok * tok * cols, 12 * tok * cols),
         name="local_part",
     )(skip, vt, gate, keys, query, weights)
 
 
-def read_level(state, message, level, heads, n):
-    rows, tok = state.shape[0], message.shape[1]
-    part = dot(state, message[:n], NN).reshape(heads, rows // heads, tok)
-    first = n + level * heads
-    return (part * message[first : first + heads].astype(f32)[:, None, :]).reshape(rows, tok)
-
-
-def sibling_sum(ref, index, bit):
+def read_level(state, query, weights, level, heads):
+    rows, tok = state.shape[0], query.shape[0]
+    part = dot(state, query, NT).reshape(heads, rows // heads, tok)
+    return (part * weights[level * heads : (level + 1) * heads][:, None, :]).reshape(rows, tok)
+
+
+def sibling_sum(ref, index, bit, rows):
     count = 1 << bit
     first = ((index >> bit) ^ 1) << bit
     if count == 1:
-        return ref[first]
-    total = ref[first].astype(f32)
+        return ref[first, :rows]
+    total = ref[first, :rows].astype(f32)
     for k in range(1, count):
-        total = total + ref[first + k].astype(f32)
+        total = total + ref[first + k, :rows].astype(f32)
     return total.astype(bf16)
 
 
-def low_kernel(heads, where_ref, raw_ref, line_ref, message_ref, out_ref):
-    n = raw_ref.shape[2]
-    group = raw_ref.shape[0]
+def far_kernel(heads, slot, where_ref, got_ref, line_ref, plane_ref, out_ref):
+    group, rows, tok = out_ref.shape
+    n = got_ref.shape[2]
     local = {}
     for bit in range(3):
         for block in range(0, group, 2 << bit):
-            local[bit, block] = sibling_sum(raw_ref, block + (1 << bit), bit)
-    shared = [sibling_sum(line_ref, where_ref[0], bit) for bit in range(2)]
+            local[bit, block] = sibling_sum(got_ref, block + (1 << bit), bit, rows)
+    shared = [sibling_sum(line_ref, where_ref[0], bit, rows) for bit in range(2)]
+    shared += [sibling_sum(plane_ref, where_ref[1], bit, rows) for bit in range(2)]
     for j in range(group):
-        message = message_ref[j]
-        total = read_level(shared[0], message, 3, heads, n)
-        total = total + read_level(shared[1], message, 4, heads, n)
+        query = got_ref[j, rows : rows + tok]
+        weights = jnp.concatenate(
+            [
+                got_ref[j, rows + tok + k * slot : rows + tok + (k + 1) * slot]
+                for k in range(tok // n)
+            ],
+            axis=1,
+        ).astype(f32)
+        total = read_level(shared[0], query, weights, 3, heads)
+        for level in range(1, 4):
+            total = total + read_level(shared[level], query, weights, 3 + level, heads)
         for bit in range(3):
             if j >> bit & 1:
                 block = j >> (bit + 1) << (bit + 1)
-                total = total + read_level(local[bit, block], message, bit, heads, n)
-        out_ref[j] = total
-
-
-def high_kernel(heads, where_ref, part_ref, plane_ref, message_ref, out_ref):
-    n = plane_ref.shape[2]
-    shared = [sibling_sum(plane_ref, where_ref[1], bit) for bit in range(2)]
-    for j in range(part_ref.shape[0]):
-        message = message_ref[j]
-        total = part_ref[j] + read_level(shared[0], message, 5, heads, n)
-        total = total + read_level(shared[1], message, 6, heads, n)
+                total = total + read_level(local[bit, block], query, weights, bit, heads)
         out_ref[j] = total.astype(bf16)
 
 
-def far_call(kernel, name, heads, where, first, states, message, dtype):
-    group, _, tok = message.shape
-    rows = states.shape[1]
+def far_levels(where, got, line, plane, heads, slot, tok):
+    group = got.shape[0]
+    rows = line.shape[1]
     vmem = pl.BlockSpec(memory_space=pltpu.VMEM)
     return pl.pallas_call(
-        functools.partial(kernel, heads),
+        functools.partial(far_kernel, heads, slot),
         in_specs=[pl.BlockSpec(memory_space=pltpu.SMEM), vmem, vmem, vmem],
         out_specs=vmem,
-        out_shape=jax.ShapeDtypeStruct((group, rows, tok), dtype),
-        compiler_params=pltpu.CompilerParams(vmem_limit_bytes=24 * 2**20),
-        cost_estimate=cost(8 * group * rows * tok * 128, 8 * group * rows * tok),
-        name=name,
-    )(where, first, states, message)
+        out_shape=jax.ShapeDtypeStruct((group, rows, tok), bf16),
+        compiler_params=pltpu.CompilerParams(vmem_limit_bytes=VMEM_MIB * 2**20),
+        cost_estimate=cost(12 * group * rows * tok * 128, 8 * group * rows * tok),
+        name="far_levels",
+    )(where, got, line, plane)
 
 
 def project(where_ref, pieces, normed_ref, out_ref):
@@ -234,7 +255,8 @@
 def piece_specs(pieces, offset):
     _, cols, depth = pieces[0].shape
     return [
-        pl.BlockSpec((1, cols, depth), lambda i, where: (where[offset] + i, 0, 0)) for _ in pieces
+        pl.BlockSpec((1, cols, depth), lambda i, where: ((where[offset] + i) ^ where[4], 0, 0))
+        for _ in pieces
     ]
 
 
@@ -263,7 +285,7 @@
             jax.ShapeDtypeStruct((tok, wide * steps), bf16),
             jax.ShapeDtypeStruct((2, rows // 2, tok), bf16),
         ],
-        compiler_params=params(40),
+        compiler_params=params(max(VMEM_MIB, 40)),
         cost_estimate=cost(2 * tok * rows * wide * steps, 16 * 2**20),
         name="finish",
     )(where, *pieces, *others)
@@ -284,7 +306,7 @@
             out_specs=pl.BlockSpec((tok, wide), lambda i, where: (0, i)),
         ),
         out_shape=jax.ShapeDtypeStruct((tok, wide * steps), f32),
-        compiler_params=params(40),
+        compiler_params=params(max(VMEM_MIB, 40)),
         cost_estimate=cost(2 * tok * 2 * rows * wide * steps, 8 * 2**20),
         name="keep",
     )(where, *pieces, normed)
@@ -295,12 +317,18 @@
     return lax.all_to_all(spread, axis, 0, 0, tiled=True)
 
 
-def gathered_weight(out_weight):
+def weight_line(out_weight):
     rows, cols = out_weight.shape
     mine = lax.axis_index("rep")
     half = lax.dynamic_slice_in_dim(out_weight, mine * (rows // 2), rows // 2, 0).T
-    line = shared_along(half, "y").reshape(-1, rows // 2)
-    own = shared_along(line, "zl")
+    return shared_along(half, "y").reshape(-1, rows // 2)
+
+
+def weight_plane(line):
+    return jnp.stack([line] + [swapped(line, "zl", d) for d in range(1, lax.axis_size("zl"))])
+
+
+def weight_pieces(own):
     pieces = []
     for k in range(lax.axis_size("x")):
         piece = own if k == 0 else swapped(own, "x", k)
@@ -318,38 +346,31 @@
     group = lax.axis_size("y")
     heads = head_count // group
     rows = width // group
+    slot = 32
     axes = [("y", b) for b in range(3)] + [("x", b) for b in range(2)] + [("zl", b) for b in range(2)]
-    uppers = jnp.stack([(lax.axis_index(a) >> b) & 1 for a, b in axes])
-    head = lax.axis_index("head")
+    uppers = jnp.stack([(lax.axis_index(a) >> b) & 1 for a, b in axes]).astype(f32)
+    x, y, z, head = (lax.axis_index(a) for a in ("x", "y", "zl", "head"))
     z_half = lax.axis_size("zl") // 2
-    place = jnp.stack([lax.axis_index("x"), lax.axis_index("zl")]).astype(jnp.int32)
+    place = jnp.stack([x, z]).astype(jnp.int32)
     where = jnp.stack(
-        [lax.axis_index("x"), lax.axis_index("rep"), (1 - head) * z_half, head * z_half]
+        [x, lax.axis_index("rep"), (1 - head) * z_half, head * z_half, z]
     ).astype(jnp.int32)
 
-    vt, sent = own_state(seq_values, seq_keys)
-    raw = lax.all_to_all(sent.reshape(group, rows, n), "y", 0, 0, tiled=True)
-    pieces = gathered_weight(out_weight)
-
-    far_weights = level_weights[LOCAL_LEVELS:] * uppers[:, None, None].astype(bf16)
-    levels = len(axes)
-    far_weights = far_weights.reshape(levels, group, heads, tok).swapaxes(0, 1)
-    far_weights = far_weights.reshape(group, levels * heads, tok)
-    far_weights = jnp.pad(far_weights, ((0, 0), (0, -levels * heads % 16), (0, 0)))
-    message = jnp.concatenate(
-        [jnp.broadcast_to(seq_queries.T[None], (group, n, tok)), far_weights], axis=1
-    )
-    message = lax.all_to_all(message, "y", 0, 0, tiled=True)
+    weight = weight_line(out_weight)
+    vt, sent = to_group(uppers, seq_values, seq_keys, seq_queries, level_weights, group, slot)
+    sent, weight = lax.optimization_barrier((sent, weight))
+    raw = lax.all_to_all(sent, "y", 0, 0, tiled=True)
+    weight = weight_plane(weight)
+    acc, silu = local_part(vt, seq_gate, seq_keys, seq_queries, level_weights, skip_gain, head_size)
+    raw, acc, silu, weight = lax.optimization_barrier((raw, acc, silu, weight))
+    pieces = weight_pieces(weight)
 
     def summed(blocks):
         return jnp.sum(blocks.astype(f32), axis=0).astype(bf16)
 
-    line = shared_along(summed(raw), "x")
+    line = shared_along(summed(raw[:, :rows]), "x")
     plane = shared_along(summed(line), "zl")
-
-    acc, silu = local_part(vt, seq_gate, seq_keys, seq_queries, level_weights, skip_gain, head_size)
-    part = far_call(low_kernel, "low_levels", heads, place, raw, line, message, f32)
-    far = far_call(high_kernel, "high_levels", heads, place, part, plane, message, bf16)
+    far = far_levels(place, raw, line, plane, heads, slot, tok)
     far = lax.all_to_all(far, "y", 0, 0, tiled=True).reshape(width, tok)
 
     to_send, normed = finish(where, pieces, acc, silu, far, norm_gain[:, None])

time: 223 us -> 175 us (0.78)
  waiting for transfers between devices: 99.7 us -> 66.7 us
  local copies, waits for them, and re-layouts: 18.9 us -> 6.16 us
  blocking collectives: 22.1 us -> 10.9 us
  Pallas kernels: 19.1 us -> 27.2 us
    all_to_all x4 -> x2, waiting for transfers between devices: 36.5 us -> 7.23 us  [shared_along(): return lax.all_to_all(spread, axis, 0, 0, tiled=True)]
    all_to_all x1, waiting for transfers between devices: 17.5 us -> 4.9 us  [on_device(): raw = lax.all_to_all(sent, 'y', 0, 0, tiled=True)]
    unnamed x38 -> x16, local copies, waits for them, and re-layouts: 14.9 us -> 2.59 us
    ppermute x8 -> x11, starting transfers between devices: 26.2 us -> 37.6 us  [swapped(): lax.ppermute(value, axis, [(i, i ^ mask) for i in range(lax.axis_size(axi...]
    all_to_all x1, blocking collectives: 22.1 us -> 10.9 us  [shared_along(): return lax.all_to_all(spread, axis, 0, 0, tiled=True)]
    ppermute x8 -> x11, waiting for transfers between devices: 45.7 us -> 54.5 us  [swapped(): lax.ppermute(value, axis, [(i, i ^ mask) for i in range(lax.axis_size(axi...]
    all_to_all x4 -> x2, starting transfers between devices: 21.9 us -> 14 us  [shared_along(): return lax.all_to_all(spread, axis, 0, 0, tiled=True)]
    all_to_all x1, starting transfers between devices: 7.1 us -> 3.56 us  [on_device(): raw = lax.all_to_all(sent, 'y', 0, 0, tiled=True)]
  transfers between devices with their start and end apart: 14 -> 15, of which waited for: 6 -> 7; matrix products, arithmetic and copies ran while one was open for 1% -> 2% of each run, Pallas kernels for 5% -> 11%
where the time goes in v4:
time: 175 us; the launch traced here: 174 us
  waiting for transfers between devices  66.7 us (38%)
  starting transfers between devices  58.8 us (34%)
  Pallas kernels  27.2 us (16%)
  blocking collectives  10.9 us (6%)
  local copies, waits for them, and re-layouts  6.16 us (4%)
  other arithmetic  3.59 us (2%)
    ppermute x11, waiting for transfers between devices, swapped(): lax.ppermute(value, axis, [(i, i ^ mask) for i in range(lax.axis_size(axi...  54.5 us
    ppermute x11, starting transfers between devices, swapped(): lax.ppermute(value, axis, [(i, i ^ mask) for i in range(lax.axis_size(axi...  37.6 us
    all_to_all x2, starting transfers between devices, shared_along(): return lax.all_to_all(spread, axis, 0, 0, tiled=True)  14 us
    all_to_all x1, blocking collectives, shared_along(): return lax.all_to_all(spread, axis, 0, 0, tiled=True)  10.9 us
    pallas_call x1, Pallas kernels, finish(): pl.pallas_call(finish_kernel, grid_spec=pltpu.PrefetchScalarGridSpec(num_...  7.43 us
    all_to_all x2, waiting for transfers between devices, shared_along(): return lax.all_to_all(spread, axis, 0, 0, tiled=True)  7.23 us
    pallas_call x1, Pallas kernels, local_part(): pl.pallas_call(functools.partial(local_kernel, heads, tok // 2), grid=(st...  6.23 us
    pallas_call x1, Pallas kernels, keep(): pl.pallas_call(keep_kernel, grid_spec=pltpu.PrefetchScalarGridSpec(num_sc...  5.43 us
  transfers between devices with their start and end apart: 15, of which 7 were waited for; matrix products, arithmetic and copies ran while one was open for 2% of the time, Pallas kernels for 11%

profile of v4, /device:TPU:64, one launch (start us, length us, event | category | flops | bytes accessed | tf_op | source)
XLA Modules:
  0.0 173.6 jit_solution(2353389605010757327)
XLA Ops:
  1.6 7.1 %all-to-all-start = ((bf16[8,16,1024]{2,1,0:T(8,128)(2,1)}), bf16[8,16,1024]{2,1,0:T(8,128)(2,1)S(1)}, u32[]{:S(2)}, u32[]{:S(2)}) async-start(bf16[8,16,1024]{2,1,0:T(8,128)(2,1)} %broadcast_in_dim.8), calls=%async_computation | async-start | bytes 524288 | tf_op jit(solution)/shard_map/all_to_all | solution.py:317
  9.3 4.0 %to_group.1 = (bf16[2048,256]{1,0:T(8,128)(2,1)}, bf16[8,576,128]{2,1,0:T(8,128)(2,1)}) custom-call(f32[7]{0:T(128)} %convert_element_type.6.upper_ref, bf16[256,2048]{1,0:T(8,128)(2,1)} %values_ref.1, bf16[256,128]{1,0:T(8,128)(2,1)} %keys_ref.3, bf16[256,128]{1,0:T(8,128)(2,1)} %query_ref.3, bf16[16,32,256]{2,1,0:T(8,128)(2,1)} %w_ref.3), custom_call_target="tpu_custom_call" | custom-call | flops 134217728 | bytes 2097152 | tf_op jit(solution)/shard_map/to_group/pallas_call | solution.py:66
  13.3 7.2 %all-to-all-done = bf16[8,16,1024]{2,1,0:T(8,128)(2,1)S(1)} async-done(((bf16[8,16,1024]{2,1,0:T(8,128)(2,1)}), bf16[8,16,1024]{2,1,0:T(8,128)(2,1)S(1)}, u32[]{:S(2)}, u32[]{:S(2)}) %all-to-all-start) | async-done | bytes 262176 | tf_op jit(solution)/shard_map/all_to_all | solution.py:317
  20.6 3.6 %all-to-all-start.1 = ((bf16[8,576,128]{2,1,0:T(8,128)(2,1)}), bf16[8,576,128]{2,1,0:T(8,128)(2,1)S(1)}, u32[]{:S(2)}, u32[]{:S(2)}) async-start(bf16[8,576,128]{2,1,0:T(8,128)(2,1)} %get-tuple-element.18), calls=%async_computation.1 | async-start | bytes 2359296 | tf_op jit(solution)/shard_map/all_to_all | solution.py:362
  24.1 4.3 %collective-permute-start.2 = (bf16[128,1024]{1,0:T(8,128)(2,1)S(1)}, bf16[128,1024]{1,0:T(8,128)(2,1)S(1)}, u32[]{:S(2)}, u32[]{:S(2)}) collective-permute-start(bf16[128,1024]{1,0:T(8,128)(2,1)S(1)} %bitcast.22), channel_id=1, source_target_pairs={{0,384},{128,256},{256,128},{384,0},{1,385},{129,257},{257,129},{3... | collective-permute-start | bytes 786440 | tf_op jit(solution)/shard_map/ppermute | solution.py:30
  28.4 3.7 %collective-permute-start.1 = (bf16[128,1024]{1,0:T(8,128)(2,1)S(1)}, bf16[128,1024]{1,0:T(8,128)(2,1)S(1)}, u32[]{:S(2)}, u32[]{:S(2)}) collective-permute-start(bf16[128,1024]{1,0:T(8,128)(2,1)S(1)} %bitcast.23), channel_id=1, source_target_pairs={{0,256},{128,384},{256,0},{384,128},{1,257},{129,385},{257,1},{385... | collective-permute-start | bytes 786440 | tf_op jit(solution)/shard_map/ppermute | solution.py:30
  32.2 3.4 %collective-permute-start = (bf16[128,1024]{1,0:T(8,128)(2,1)S(1)}, bf16[128,1024]{1,0:T(8,128)(2,1)S(1)}, u32[]{:S(2)}, u32[]{:S(2)}) collective-permute-start(bf16[128,1024]{1,0:T(8,128)(2,1)S(1)} %bitcast.24), channel_id=1, source_target_pairs={{0,128},{128,0},{256,384},{384,256},{1,129},{129,1},{257,385},{385... | collective-permute-start | bytes 786440 | tf_op jit(solution)/shard_map/ppermute | solution.py:30
  35.5 6.2 %local_part.1 = (f32[2048,256]{1,0:T(8,128)}, f32[2048,256]{1,0:T(8,128)}) custom-call(f32[32]{0:T(128)} %skip_ref.1, bf16[2048,256]{1,0:T(8,128)(2,1)} %get-tuple-element.19.vt_ref, bf16[256,2048]{1,0:T(8,128)(2,1)} %gate_ref.1, bf16[256,128]{1,0:T(8,128)(2,1)} %keys_ref.3, bf16[256,128]{1,0:T(8,128)(2,1)} %query_ref.3, bf16[16,32,256]{2,1,0:T(8,128)(2,1)} %w_ref.3), custom_call_target="tpu_custom_call" | custom-call | flops 1073741824 | bytes 6291456 | tf_op jit(solution)/shard_map/local_part/pallas_call | solution.py:140
  41.8 4.5 %collective-permute-done.2 = bf16[128,1024]{1,0:T(8,128)(2,1)S(1)} collective-permute-done((bf16[128,1024]{1,0:T(8,128)(2,1)S(1)}, bf16[128,1024]{1,0:T(8,128)(2,1)S(1)}, u32[]{:S(2)}, u32[]{:S(2)}) %collective-permute-start.2) | collective-permute-done | bytes 262176 | tf_op jit(solution)/shard_map/ppermute | solution.py:30
  46.2 2.8 %collective-permute-done.1 = bf16[128,1024]{1,0:T(8,128)(2,1)S(1)} collective-permute-done((bf16[128,1024]{1,0:T(8,128)(2,1)S(1)}, bf16[128,1024]{1,0:T(8,128)(2,1)S(1)}, u32[]{:S(2)}, u32[]{:S(2)}) %collective-permute-start.1) | collective-permute-done | bytes 262176 | tf_op jit(solution)/shard_map/ppermute | solution.py:30
  49.2 4.9 %all-to-all-done.1.got_ref = bf16[8,576,128]{2,1,0:T(8,128)(2,1)S(1)} async-done(((bf16[8,576,128]{2,1,0:T(8,128)(2,1)}), bf16[8,576,128]{2,1,0:T(8,128)(2,1)S(1)}, u32[]{:S(2)}, u32[]{:S(2)}) %all-to-all-start.1) | async-done | bytes 1179680 | tf_op jit(solution)/shard_map/all_to_all | solution.py:362
  54.2 10.9 %all_to_all.25.line_ref = bf16[4,256,128]{2,1,0:T(8,128)(2,1)S(1)} all-to-all(bf16[4,256,128]{2,1,0:T(8,128)(2,1)S(1)} %broadcast_in_dim.9), channel_id=1, replica_groups=mesh['zl'=4,'x'=4,'y'=8,'head'=2,'rep'=2] {'x'}, dimensions={0} | all-to-all | bytes 524288 | tf_op jit(solution)/shard_map/all_to_all | solution.py:317
  65.9 6.9 %all-to-all-start.3 = ((bf16[4,256,128]{2,1,0:T(8,128)(2,1)}), bf16[4,256,128]{2,1,0:T(8,128)(2,1)S(1)}, u32[]{:S(2)}, u32[]{:S(2)}) async-start(bf16[4,256,128]{2,1,0:T(8,128)(2,1)} %broadcast_in_dim.10), calls=%async_computation.3 | async-start | bytes 524288 | tf_op jit(solution)/shard_map/all_to_all | solution.py:317
  72.9 3.1 %collective-permute-start.8 = (bf16[4,128,1024]{2,1,0:T(8,128)(2,1)S(1)}, bf16[4,128,1024]{2,1,0:T(8,128)(2,1)S(1)}, u32[]{:S(2)}, u32[]{:S(2)}) collective-permute-start(bf16[4,128,1024]{2,1,0:T(8,128)(2,1)S(1)} %pad_maximum_fusion.refs_0_), channel_id=1, source_target_pairs={{0,96},{32,64},{64,32},{96,0},{1,97},{33,65},{65,33},{97,1},{2,98}... | collective-permute-start | bytes 3145736 | tf_op jit(solution)/shard_map/ppermute | solution.py:30
  75.9 3.4 %collective-permute-start.6 = (bf16[4,128,1024]{2,1,0:T(8,128)(2,1)S(1)}, bf16[4,128,1024]{2,1,0:T(8,128)(2,1)}, u32[]{:S(2)}, u32[]{:S(2)}) collective-permute-start(bf16[4,128,1024]{2,1,0:T(8,128)(2,1)S(1)} %pad_maximum_fusion.refs_0_), channel_id=1, source_target_pairs={{0,64},{32,96},{64,0},{96,32},{1,65},{33,97},{65,1},{97,33},{2,66}... | collective-permute-start | bytes 3145736 | tf_op jit(solution)/shard_map/ppermute | solution.py:30
  79.3 3.4 %collective-permute-start.4 = (bf16[4,128,1024]{2,1,0:T(8,128)(2,1)S(1)}, bf16[4,128,1024]{2,1,0:T(8,128)(2,1)}, u32[]{:S(2)}, u32[]{:S(2)}) collective-permute-start(bf16[4,128,1024]{2,1,0:T(8,128)(2,1)S(1)} %pad_maximum_fusion.refs_0_), channel_id=1, source_target_pairs={{0,32},{32,0},{64,96},{96,64},{1,33},{33,1},{65,97},{97,65},{2,34}... | collective-permute-start | bytes 3145736 | tf_op jit(solution)/shard_map/ppermute | solution.py:30
  84.0 4.1 %far_levels.1 = bf16[8,256,256]{2,1,0:T(8,128)(2,1)} custom-call(s32[2]{0:T(128)} %pad_add_fusion.where_ref, bf16[8,576,128]{2,1,0:T(8,128)(2,1)} %copy-done.4, bf16[4,256,128]{2,1,0:T(8,128)(2,1)} %copy-done.5, bf16[4,256,128]{2,1,0:T(8,128)(2,1)} %copy-done.6), custom_call_target="tpu_custom_call" | custom-call | flops 805306368 | bytes 4194304 | tf_op jit(solution)/shard_map/far_levels/pallas_call | solution.py:212
  88.1 3.7 %all-to-all-start.4 = ((bf16[8,256,256]{2,1,0:T(8,128)(2,1)}), bf16[8,256,256]{2,1,0:T(8,128)(2,1)S(1)}, u32[]{:S(2)}, u32[]{:S(2)}) async-start(bf16[8,256,256]{2,1,0:T(8,128)(2,1)} %far_levels.1), calls=%async_computation.4 | async-start | bytes 2097152 | tf_op jit(solution)/shard_map/all_to_all | solution.py:374
  93.8 27.7 %collective-permute-done.8.refs_6_ = bf16[4,128,1024]{2,1,0:T(8,128)(2,1)S(1)} collective-permute-done((bf16[4,128,1024]{2,1,0:T(8,128)(2,1)S(1)}, bf16[4,128,1024]{2,1,0:T(8,128)(2,1)S(1)}, u32[]{:S(2)}, u32[]{:S(2)}) %collective-permute-start.8) | collective-permute-done | bytes 1048608 | tf_op jit(solution)/shard_map/ppermute | solution.py:30
  123.4 2.4 %collective-permute-start.7 = (bf16[4,128,1024]{2,1,0:T(8,128)(2,1)}, bf16[4,128,1024]{2,1,0:T(8,128)(2,1)}, u32[]{:S(2)}, u32[]{:S(2)}) collective-permute-start(bf16[4,128,1024]{2,1,0:T(8,128)(2,1)} %collective-permute-done.6.refs_4_), channel_id=1, source_target_pairs={{0,1},{1,0},{2,3},{3,2},{4,5},{5,4},{6,7},{7,6},{8,9},{9,8},{10,11... | collective-permute-start | bytes 3145736 | tf_op jit(solution)/shard_map/ppermute | solution.py:30
  131.8 7.4 %finish.1 = (bf16[256,1024]{1,0:T(8,128)(2,1)}, bf16[2,1024,256]{2,1,0:T(8,128)(2,1)}) custom-call(s32[5]{0:T(128)} %stack.67.where_ref, bf16[4,128,1024]{2,1,0:T(8,128)(2,1)} %copy-done.1, bf16[4,128,1024]{2,1,0:T(8,128)(2,1)} %collective-permute-done.3.refs_1_, bf16[4,128,1024]{2,1,0:T(8,128)(2,1)} %collective-permute-done.4.refs_2_, ...), custom_call_target="tpu_custom_call" | custom-call | flops 1073741824 | bytes 16777216 | tf_op jit(solution)/shard_map/finish/pallas_call | solution.py:273
  139.2 8.2 %collective-permute-start.10 = (bf16[256,1024]{1,0:T(8,128)(2,1)}, bf16[256,1024]{1,0:T(8,128)(2,1)S(1)}, u32[]{:S(2)}, u32[]{:S(2)}) collective-permute-start(bf16[256,1024]{1,0:T(8,128)(2,1)} %get-tuple-element.28), channel_id=1, source_target_pairs={{0,2},{2,0},{1,3},{3,1},{4,6},{6,4},{5,7},{7,5},{8,10},{10,8},{9,1... | collective-permute-start | bytes 1572872 | tf_op jit(solution)/shard_map/ppermute | solution.py:30
  147.4 5.4 %keep.1 = f32[256,1024]{1,0:T(8,128)} custom-call(s32[5]{0:T(128)} %stack.67.where_ref, bf16[4,128,1024]{2,1,0:T(8,128)(2,1)} %copy-done.1, bf16[4,128,1024]{2,1,0:T(8,128)(2,1)} %collective-permute-done.3.refs_1_, bf16[4,128,1024]{2,1,0:T(8,128)(2,1)} %collective-permute-done.4.refs_2_, bf16[4,128,1024]{2,1,0:T(8,128)(2,1)} %collective-permute-done.5.refs_3_, ...), custom_call_target="tpu_custom_call" | custom-call | flops 1073741824 | bytes 8388608 | tf_op jit(solution)/shard_map/keep/pallas_call | solution.py:299
  152.8 18.5 %collective-permute-done.10 = bf16[256,1024]{1,0:T(8,128)(2,1)S(1)} collective-permute-done((bf16[256,1024]{1,0:T(8,128)(2,1)}, bf16[256,1024]{1,0:T(8,128)(2,1)S(1)}, u32[]{:S(2)}, u32[]{:S(2)}) %collective-permute-start.10) | collective-permute-done | bytes 524320 | tf_op jit(solution)/shard_map/ppermute | solution.py:30
  (41 shorter events, 16.5 us)
Async XLA Ops:
  0.0 0.8 copy-start
  1.6 19.0 %all-to-all-start = ((bf16[8,16,1024]{2,1,0:T(8,128)(2,1)}), bf16[8,16,1024]{2,1,0:T(8,128)(2,1)S(1)}, u32[]{:S(2)}, u32[]{:S(2)}) async-start(bf16[8,16,1024]{2,1,0:T(8,128)(2,1)} %broadcast_in_dim.8), calls=%async_computation | async-start | bytes 524288 | tf_op jit(solution)/shard_map/all_to_all | solution.py:317
  20.6 33.5 %all-to-all-start.1 = ((bf16[8,576,128]{2,1,0:T(8,128)(2,1)}), bf16[8,576,128]{2,1,0:T(8,128)(2,1)S(1)}, u32[]{:S(2)}, u32[]{:S(2)}) async-start(bf16[8,576,128]{2,1,0:T(8,128)(2,1)} %get-tuple-element.18), calls=%async_computation.1 | async-start | bytes 2359296 | tf_op jit(solution)/shard_map/all_to_all | solution.py:362
  24.1 22.1 %collective-permute-start.2 = (bf16[128,1024]{1,0:T(8,128)(2,1)S(1)}, bf16[128,1024]{1,0:T(8,128)(2,1)S(1)}, u32[]{:S(2)}, u32[]{:S(2)}) collective-permute-start(bf16[128,1024]{1,0:T(8,128)(2,1)S(1)} %bitcast.22), channel_id=1, source_target_pairs={{0,384},{128,256},{256,128},{384,0},{1,385},{129,257},{257,129},{3... | collective-permute-start | bytes 786440 | tf_op jit(solution)/shard_map/ppermute | solution.py:30
  28.4 20.6 %collective-permute-start.1 = (bf16[128,1024]{1,0:T(8,128)(2,1)S(1)}, bf16[128,1024]{1,0:T(8,128)(2,1)S(1)}, u32[]{:S(2)}, u32[]{:S(2)}) collective-permute-start(bf16[128,1024]{1,0:T(8,128)(2,1)S(1)} %bitcast.23), channel_id=1, source_target_pairs={{0,256},{128,384},{256,0},{384,128},{1,257},{129,385},{257,1},{385... | collective-permute-start | bytes 786440 | tf_op jit(solution)/shard_map/ppermute | solution.py:30
  32.2 16.9 %collective-permute-start = (bf16[128,1024]{1,0:T(8,128)(2,1)S(1)}, bf16[128,1024]{1,0:T(8,128)(2,1)S(1)}, u32[]{:S(2)}, u32[]{:S(2)}) collective-permute-start(bf16[128,1024]{1,0:T(8,128)(2,1)S(1)} %bitcast.24), channel_id=1, source_target_pairs={{0,128},{128,0},{256,384},{384,256},{1,129},{129,1},{257,385},{385... | collective-permute-start | bytes 786440 | tf_op jit(solution)/shard_map/ppermute | solution.py:30
  49.2 42.7 %copy-start.1 = (bf16[4,128,1024]{2,1,0:T(8,128)(2,1)}, bf16[4,128,1024]{2,1,0:T(8,128)(2,1)S(1)}, u32[]{:S(2)}) copy-start(bf16[4,128,1024]{2,1,0:T(8,128)(2,1)S(1)} %pad_maximum_fusion.refs_0_) | copy-start | bytes 3145732
  54.1 11.9 %copy-start.4 = (bf16[8,576,128]{2,1,0:T(8,128)(2,1)}, bf16[8,576,128]{2,1,0:T(8,128)(2,1)S(1)}, u32[]{:S(2)}) copy-start(bf16[8,576,128]{2,1,0:T(8,128)(2,1)S(1)} %all-to-all-done.1.got_ref) | copy-start | bytes 3538948
  65.1 18.2 %copy-start.5 = (bf16[4,256,128]{2,1,0:T(8,128)(2,1)}, bf16[4,256,128]{2,1,0:T(8,128)(2,1)S(1)}, u32[]{:S(2)}) copy-start(bf16[4,256,128]{2,1,0:T(8,128)(2,1)S(1)} %all_to_all.25.line_ref) | copy-start | bytes 786436
  65.9 17.4 %all-to-all-start.3 = ((bf16[4,256,128]{2,1,0:T(8,128)(2,1)}), bf16[4,256,128]{2,1,0:T(8,128)(2,1)S(1)}, u32[]{:S(2)}, u32[]{:S(2)}) async-start(bf16[4,256,128]{2,1,0:T(8,128)(2,1)} %broadcast_in_dim.10), calls=%async_computation.3 | async-start | bytes 524288 | tf_op jit(solution)/shard_map/all_to_all | solution.py:317
  72.9 48.6 %collective-permute-start.8 = (bf16[4,128,1024]{2,1,0:T(8,128)(2,1)S(1)}, bf16[4,128,1024]{2,1,0:T(8,128)(2,1)S(1)}, u32[]{:S(2)}, u32[]{:S(2)}) collective-permute-start(bf16[4,128,1024]{2,1,0:T(8,128)(2,1)S(1)} %pad_maximum_fusion.refs_0_), channel_id=1, source_target_pairs={{0,96},{32,64},{64,32},{96,0},{1,97},{33,65},{65,33},{97,1},{2,98}... | collective-permute-start | bytes 3145736 | tf_op jit(solution)/shard_map/ppermute | solution.py:30
  75.9 47.5 %collective-permute-start.6 = (bf16[4,128,1024]{2,1,0:T(8,128)(2,1)S(1)}, bf16[4,128,1024]{2,1,0:T(8,128)(2,1)}, u32[]{:S(2)}, u32[]{:S(2)}) collective-permute-start(bf16[4,128,1024]{2,1,0:T(8,128)(2,1)S(1)} %pad_maximum_fusion.refs_0_), channel_id=1, source_target_pairs={{0,64},{32,96},{64,0},{96,32},{1,65},{33,97},{65,1},{97,33},{2,66}... | collective-permute-start | bytes 3145736 | tf_op jit(solution)/shard_map/ppermute | solution.py:30
  79.3 46.5 %collective-permute-start.4 = (bf16[4,128,1024]{2,1,0:T(8,128)(2,1)S(1)}, bf16[4,128,1024]{2,1,0:T(8,128)(2,1)}, u32[]{:S(2)}, u32[]{:S(2)}) collective-permute-start(bf16[4,128,1024]{2,1,0:T(8,128)(2,1)S(1)} %pad_maximum_fusion.refs_0_), channel_id=1, source_target_pairs={{0,32},{32,0},{64,96},{96,64},{1,33},{33,1},{65,97},{97,65},{2,34}... | collective-permute-start | bytes 3145736 | tf_op jit(solution)/shard_map/ppermute | solution.py:30
  83.3 0.7 copy-start.6
  88.1 39.7 %copy-start.7 = (f32[2048]{0:T(1024)S(1)}, f32[2048]{0:T(1024)}, u32[]{:S(2)}) copy-start(f32[2048]{0:T(1024)} %param.14) | copy-start | bytes 24580
  88.1 42.6 %all-to-all-start.4 = ((bf16[8,256,256]{2,1,0:T(8,128)(2,1)}), bf16[8,256,256]{2,1,0:T(8,128)(2,1)S(1)}, u32[]{:S(2)}, u32[]{:S(2)}) async-start(bf16[8,256,256]{2,1,0:T(8,128)(2,1)} %far_levels.1), calls=%async_computation.4 | async-start | bytes 2097152 | tf_op jit(solution)/shard_map/all_to_all | solution.py:374
  91.8 37.9 %collective-permute-start.3 = (bf16[4,128,1024]{2,1,0:T(8,128)(2,1)S(1)}, bf16[4,128,1024]{2,1,0:T(8,128)(2,1)}, u32[]{:S(2)}, u32[]{:S(2)}) collective-permute-start(bf16[4,128,1024]{2,1,0:T(8,128)(2,1)S(1)} %pad_maximum_fusion.refs_0_), channel_id=1, source_target_pairs={{0,1},{1,0},{2,3},{3,2},{4,5},{5,4},{6,7},{7,6},{8,9},{9,8},{10,11... | collective-permute-start | bytes 3145736 | tf_op jit(solution)/shard_map/ppermute | solution.py:30
  121.5 9.3 %copy-start.3 = (bf16[4,128,1024]{2,1,0:T(8,128)(2,1)}, bf16[4,128,1024]{2,1,0:T(8,128)(2,1)S(1)}, u32[]{:S(2)}) copy-start(bf16[4,128,1024]{2,1,0:T(8,128)(2,1)S(1)} %collective-permute-done.8.refs_6_) | copy-start | bytes 3145732
  121.5 8.3 %collective-permute-start.9 = (bf16[4,128,1024]{2,1,0:T(8,128)(2,1)S(1)}, bf16[4,128,1024]{2,1,0:T(8,128)(2,1)}, u32[]{:S(2)}, u32[]{:S(2)}) collective-permute-start(bf16[4,128,1024]{2,1,0:T(8,128)(2,1)S(1)} %collective-permute-done.8.refs_6_), channel_id=1, source_target_pairs={{0,1},{1,0},{2,3},{3,2},{4,5},{5,4},{6,7},{7,6},{8,9},{9,8},{10,11... | collective-permute-start | bytes 3145736 | tf_op jit(solution)/shard_map/ppermute | solution.py:30
  123.4 6.3 %collective-permute-start.7 = (bf16[4,128,1024]{2,1,0:T(8,128)(2,1)}, bf16[4,128,1024]{2,1,0:T(8,128)(2,1)}, u32[]{:S(2)}, u32[]{:S(2)}) collective-permute-start(bf16[4,128,1024]{2,1,0:T(8,128)(2,1)} %collective-permute-done.6.refs_4_), channel_id=1, source_target_pairs={{0,1},{1,0},{2,3},{3,2},{4,5},{5,4},{6,7},{7,6},{8,9},{9,8},{10,11... | collective-permute-start | bytes 3145736 | tf_op jit(solution)/shard_map/ppermute | solution.py:30
  125.8 4.9 %collective-permute-start.5 = (bf16[4,128,1024]{2,1,0:T(8,128)(2,1)}, bf16[4,128,1024]{2,1,0:T(8,128)(2,1)}, u32[]{:S(2)}, u32[]{:S(2)}) collective-permute-start(bf16[4,128,1024]{2,1,0:T(8,128)(2,1)} %collective-permute-done.4.refs_2_), channel_id=1, source_target_pairs={{0,1},{1,0},{2,3},{3,2},{4,5},{5,4},{6,7},{7,6},{8,9},{9,8},{10,11... | collective-permute-start | bytes 3145736 | tf_op jit(solution)/shard_map/ppermute | solution.py:30
  130.7 1.0 copy-start.2
  139.2 32.2 %collective-permute-start.10 = (bf16[256,1024]{1,0:T(8,128)(2,1)}, bf16[256,1024]{1,0:T(8,128)(2,1)S(1)}, u32[]{:S(2)}, u32[]{:S(2)}) collective-permute-start(bf16[256,1024]{1,0:T(8,128)(2,1)} %get-tuple-element.28), channel_id=1, source_target_pairs={{0,2},{2,0},{1,3},{3,1},{4,6},{6,4},{5,7},{7,5},{8,10},{10,8},{9,1... | collective-permute-start | bytes 1572872 | tf_op jit(solution)/shard_map/ppermute | solution.py:30

commit v5 on v4

--- a/solution.py
+++ b/solution.py
@@ -328,10 +328,9 @@
     return jnp.stack([line] + [swapped(line, "zl", d) for d in range(1, lax.axis_size("zl"))])
 
 
-def weight_pieces(own):
+def weight_pieces(halves):
     pieces = []
-    for k in range(lax.axis_size("x")):
-        piece = own if k == 0 else swapped(own, "x", k)
+    for piece in halves:
         pieces += [piece, swapped(piece, "rep", 1)]
     return pieces
 
@@ -362,14 +361,16 @@
     raw = lax.all_to_all(sent, "y", 0, 0, tiled=True)
     weight = weight_plane(weight)
     acc, silu = local_part(vt, seq_gate, seq_keys, seq_queries, level_weights, skip_gain, head_size)
-    raw, acc, silu, weight = lax.optimization_barrier((raw, acc, silu, weight))
-    pieces = weight_pieces(weight)
+    raw, acc, silu, own = lax.optimization_barrier((raw, acc, silu, weight))
+    near, middle, last = [swapped(weight, "x", k) for k in range(1, lax.axis_size("x"))]
 
     def summed(blocks):
         return jnp.sum(blocks.astype(f32), axis=0).astype(bf16)
 
     line = shared_along(summed(raw[:, :rows]), "x")
     plane = shared_along(summed(line), "zl")
+    plane, own, near, last = lax.optimization_barrier((plane, own, near, last))
+    pieces = weight_pieces([own, near, middle, last])
     far = far_levels(place, raw, line, plane, heads, slot, tok)
     far = lax.all_to_all(far, "y", 0, 0, tiled=True).reshape(width, tok)
 

time: 175 us -> 174 us (level)
  waiting for transfers between devices: 66.7 us -> 51.2 us
  starting transfers between devices: 58.8 us -> 67.4 us
  blocking collectives: 10.9 us -> 17.2 us
    ppermute x11, waiting for transfers between devices: 54.5 us -> 36.5 us  [swapped(): lax.ppermute(value, axis, [(i, i ^ mask) for i in range(lax.axis_size(axi...]
    all_to_all x1, blocking collectives: 10.9 us -> 17.2 us  [shared_along(): return lax.all_to_all(spread, axis, 0, 0, tiled=True)]
    all_to_all x1, waiting for transfers between devices: 0.01 us -> 5.58 us  [on_device(): far = lax.all_to_all(far, 'y', 0, 0, tiled=True).reshape(width, tok)]
    all_to_all x1, waiting for transfers between devices: 4.9 us -> 0.01 us  [on_device(): raw = lax.all_to_all(sent, 'y', 0, 0, tiled=True)]
    ppermute x11, starting transfers between devices: 37.6 us -> 42 us  [swapped(): lax.ppermute(value, axis, [(i, i ^ mask) for i in range(lax.axis_size(axi...]
    all_to_all x1, starting transfers between devices: 3.69 us -> 6.84 us  [on_device(): far = lax.all_to_all(far, 'y', 0, 0, tiled=True).reshape(width, tok)]
    all_to_all x2, waiting for transfers between devices: 7.23 us -> 9.13 us  [shared_along(): return lax.all_to_all(spread, axis, 0, 0, tiled=True)]
  transfers between devices with their start and end apart: 15 -> 15, of which waited for: 7 -> 8; matrix products, arithmetic and copies ran while one was open for 2% -> 3% of each run, Pallas kernels for 11% -> 11%
where the time goes in v5:
time: 174 us; the launch traced here: 173 us
  starting transfers between devices  67.4 us (39%)
  waiting for transfers between devices  51.2 us (29%)
  Pallas kernels  27.2 us (16%)
  blocking collectives  17.2 us (10%)
  local copies, waits for them, and re-layouts  5.44 us (3%)
  other arithmetic  4.64 us (3%)
    ppermute x11, starting transfers between devices, swapped(): lax.ppermute(value, axis, [(i, i ^ mask) for i in range(lax.axis_size(axi...  42 us
    ppermute x11, waiting for transfers between devices, swapped(): lax.ppermute(value, axis, [(i, i ^ mask) for i in range(lax.axis_size(axi...  36.5 us
    all_to_all x1, blocking collectives, shared_along(): return lax.all_to_all(spread, axis, 0, 0, tiled=True)  17.2 us
    all_to_all x2, starting transfers between devices, shared_along(): return lax.all_to_all(spread, axis, 0, 0, tiled=True)  14.2 us
    all_to_all x2, waiting for transfers between devices, shared_along(): return lax.all_to_all(spread, axis, 0, 0, tiled=True)  9.13 us
    pallas_call x1, Pallas kernels, finish(): pl.pallas_call(finish_kernel, grid_spec=pltpu.PrefetchScalarGridSpec(num_...  7.44 us
    all_to_all x1, starting transfers between devices, on_device(): far = lax.all_to_all(far, 'y', 0, 0, tiled=True).reshape(width, tok)  6.84 us
    pallas_call x1, Pallas kernels, local_part(): pl.pallas_call(functools.partial(local_kernel, heads, tok // 2), grid=(st...  6.24 us
  transfers between devices with their start and end apart: 15, of which 8 were waited for; matrix products, arithmetic and copies ran while one was open for 3% of the time, Pallas kernels for 11%

profile of v5, /device:TPU:64, one launch (start us, length us, event | category | flops | bytes accessed | tf_op | source)
XLA Modules:
  0.0 173.1 jit_solution(6676160938420133732)
XLA Ops:
  1.6 7.1 %all-to-all-start = ((bf16[8,16,1024]{2,1,0:T(8,128)(2,1)}), bf16[8,16,1024]{2,1,0:T(8,128)(2,1)S(1)}, u32[]{:S(2)}, u32[]{:S(2)}) async-start(bf16[8,16,1024]{2,1,0:T(8,128)(2,1)} %broadcast_in_dim.8), calls=%async_computation | async-start | bytes 524288 | tf_op jit(solution)/shard_map/all_to_all | solution.py:317
  9.3 4.0 %to_group.1 = (bf16[2048,256]{1,0:T(8,128)(2,1)}, bf16[8,576,128]{2,1,0:T(8,128)(2,1)}) custom-call(f32[7]{0:T(128)} %convert_element_type.6.upper_ref, bf16[256,2048]{1,0:T(8,128)(2,1)} %values_ref.1, bf16[256,128]{1,0:T(8,128)(2,1)} %keys_ref.3, bf16[256,128]{1,0:T(8,128)(2,1)} %query_ref.3, bf16[16,32,256]{2,1,0:T(8,128)(2,1)} %w_ref.3), custom_call_target="tpu_custom_call" | custom-call | flops 134217728 | bytes 2097152 | tf_op jit(solution)/shard_map/to_group/pallas_call | solution.py:66
  13.3 7.3 %all-to-all-done = bf16[8,16,1024]{2,1,0:T(8,128)(2,1)S(1)} async-done(((bf16[8,16,1024]{2,1,0:T(8,128)(2,1)}), bf16[8,16,1024]{2,1,0:T(8,128)(2,1)S(1)}, u32[]{:S(2)}, u32[]{:S(2)}) %all-to-all-start) | async-done | bytes 262176 | tf_op jit(solution)/shard_map/all_to_all | solution.py:317
  20.6 4.3 %all-to-all-start.1 = ((bf16[8,576,128]{2,1,0:T(8,128)(2,1)}), bf16[8,576,128]{2,1,0:T(8,128)(2,1)}, u32[]{:S(2)}, u32[]{:S(2)}) async-start(bf16[8,576,128]{2,1,0:T(8,128)(2,1)} %get-tuple-element.22), calls=%async_computation.1 | async-start | bytes 2359296 | tf_op jit(solution)/shard_map/all_to_all | solution.py:361
  24.8 4.3 %collective-permute-start.2 = (bf16[128,1024]{1,0:T(8,128)(2,1)S(1)}, bf16[128,1024]{1,0:T(8,128)(2,1)S(1)}, u32[]{:S(2)}, u32[]{:S(2)}) collective-permute-start(bf16[128,1024]{1,0:T(8,128)(2,1)S(1)} %bitcast.22), channel_id=1, source_target_pairs={{0,384},{128,256},{256,128},{384,0},{1,385},{129,257},{257,129},{3... | collective-permute-start | bytes 786440 | tf_op jit(solution)/shard_map/ppermute | solution.py:30
  29.1 3.7 %collective-permute-start.1 = (bf16[128,1024]{1,0:T(8,128)(2,1)S(1)}, bf16[128,1024]{1,0:T(8,128)(2,1)S(1)}, u32[]{:S(2)}, u32[]{:S(2)}) collective-permute-start(bf16[128,1024]{1,0:T(8,128)(2,1)S(1)} %bitcast.23), channel_id=1, source_target_pairs={{0,256},{128,384},{256,0},{384,128},{1,257},{129,385},{257,1},{385... | collective-permute-start | bytes 786440 | tf_op jit(solution)/shard_map/ppermute | solution.py:30
  32.8 3.4 %collective-permute-start = (bf16[128,1024]{1,0:T(8,128)(2,1)S(1)}, bf16[128,1024]{1,0:T(8,128)(2,1)S(1)}, u32[]{:S(2)}, u32[]{:S(2)}) collective-permute-start(bf16[128,1024]{1,0:T(8,128)(2,1)S(1)} %bitcast.24), channel_id=1, source_target_pairs={{0,128},{128,0},{256,384},{384,256},{1,129},{129,1},{257,385},{385... | collective-permute-start | bytes 786440 | tf_op jit(solution)/shard_map/ppermute | solution.py:30
  36.2 10.7 %collective-permute-done.2 = bf16[128,1024]{1,0:T(8,128)(2,1)S(1)} collective-permute-done((bf16[128,1024]{1,0:T(8,128)(2,1)S(1)}, bf16[128,1024]{1,0:T(8,128)(2,1)S(1)}, u32[]{:S(2)}, u32[]{:S(2)}) %collective-permute-start.2) | collective-permute-done | bytes 262176 | tf_op jit(solution)/shard_map/ppermute | solution.py:30
  46.9 2.8 %collective-permute-done.1 = bf16[128,1024]{1,0:T(8,128)(2,1)S(1)} collective-permute-done((bf16[128,1024]{1,0:T(8,128)(2,1)S(1)}, bf16[128,1024]{1,0:T(8,128)(2,1)S(1)}, u32[]{:S(2)}, u32[]{:S(2)}) %collective-permute-start.1) | collective-permute-done | bytes 262176 | tf_op jit(solution)/shard_map/ppermute | solution.py:30
  49.9 4.7 %collective-permute-start.4 = (bf16[4,128,1024]{2,1,0:T(8,128)(2,1)S(1)}, bf16[4,128,1024]{2,1,0:T(8,128)(2,1)S(1)}, u32[]{:S(2)}, u32[]{:S(2)}) collective-permute-start(bf16[4,128,1024]{2,1,0:T(8,128)(2,1)S(1)} %pad_maximum_fusion.refs_0_), channel_id=1, source_target_pairs={{0,96},{32,64},{64,32},{96,0},{1,97},{33,65},{65,33},{97,1},{2,98}... | collective-permute-start | bytes 3145736 | tf_op jit(solution)/shard_map/ppermute | solution.py:30
  56.7 6.2 %local_part.1 = (f32[2048,256]{1,0:T(8,128)}, f32[2048,256]{1,0:T(8,128)}) custom-call(f32[32]{0:T(128)} %skip_ref.1, bf16[2048,256]{1,0:T(8,128)(2,1)} %get-tuple-element.23.vt_ref, bf16[256,2048]{1,0:T(8,128)(2,1)} %gate_ref.1, bf16[256,128]{1,0:T(8,128)(2,1)} %keys_ref.3, bf16[256,128]{1,0:T(8,128)(2,1)} %query_ref.3, bf16[16,32,256]{2,1,0:T(8,128)(2,1)} %w_ref.3), custom_call_target="tpu_custom_call" | custom-call | flops 1073741824 | bytes 6291456 | tf_op jit(solution)/shard_map/local_part/pallas_call | solution.py:140
  64.1 17.2 %all_to_all.25.line_ref = bf16[4,256,128]{2,1,0:T(8,128)(2,1)S(1)} all-to-all(bf16[4,256,128]{2,1,0:T(8,128)(2,1)S(1)} %broadcast_in_dim.9), channel_id=1, replica_groups=mesh['zl'=4,'x'=4,'y'=8,'head'=2,'rep'=2] {'x'}, dimensions={0} | all-to-all | bytes 524288 | tf_op jit(solution)/shard_map/all_to_all | solution.py:317
  82.0 7.1 %all-to-all-start.3 = ((bf16[4,256,128]{2,1,0:T(8,128)(2,1)}), bf16[4,256,128]{2,1,0:T(8,128)(2,1)}, u32[]{:S(2)}, u32[]{:S(2)}) async-start(bf16[4,256,128]{2,1,0:T(8,128)(2,1)} %broadcast_in_dim.10), calls=%async_computation.3 | async-start | bytes 524288 | tf_op jit(solution)/shard_map/all_to_all | solution.py:317
  89.2 3.8 %collective-permute-start.7 = (bf16[4,128,1024]{2,1,0:T(8,128)(2,1)S(1)}, bf16[4,128,1024]{2,1,0:T(8,128)(2,1)}, u32[]{:S(2)}, u32[]{:S(2)}) collective-permute-start(bf16[4,128,1024]{2,1,0:T(8,128)(2,1)S(1)} %pad_maximum_fusion.refs_0_), channel_id=1, source_target_pairs={{0,64},{32,96},{64,0},{96,32},{1,65},{33,97},{65,1},{97,33},{2,66}... | collective-permute-start | bytes 3145736 | tf_op jit(solution)/shard_map/ppermute | solution.py:30
  95.5 4.1 %far_levels.1 = bf16[8,256,256]{2,1,0:T(8,128)(2,1)} custom-call(s32[2]{0:T(128)} %pad_add_fusion.where_ref, bf16[8,576,128]{2,1,0:T(8,128)(2,1)} %all-to-all-done.1.got_ref, bf16[4,256,128]{2,1,0:T(8,128)(2,1)} %copy-done.5, bf16[4,256,128]{2,1,0:T(8,128)(2,1)} %all-to-all-done.3.plane_ref), custom_call_target="tpu_custom_call" | custom-call | flops 805306368 | bytes 4194304 | tf_op jit(solution)/shard_map/far_levels/pallas_call | solution.py:212
  99.6 6.8 %all-to-all-start.4 = ((bf16[8,256,256]{2,1,0:T(8,128)(2,1)}), bf16[8,256,256]{2,1,0:T(8,128)(2,1)S(1)}, u32[]{:S(2)}, u32[]{:S(2)}) async-start(bf16[8,256,256]{2,1,0:T(8,128)(2,1)} %far_levels.1), calls=%async_computation.4 | async-start | bytes 2097152 | tf_op jit(solution)/shard_map/all_to_all | solution.py:375
  106.4 7.8 %collective-permute-done.7.refs_4_ = bf16[4,128,1024]{2,1,0:T(8,128)(2,1)} collective-permute-done((bf16[4,128,1024]{2,1,0:T(8,128)(2,1)S(1)}, bf16[4,128,1024]{2,1,0:T(8,128)(2,1)}, u32[]{:S(2)}, u32[]{:S(2)}) %collective-permute-start.7) | collective-permute-done | bytes 1048608 | tf_op jit(solution)/shard_map/ppermute | solution.py:30
  116.1 2.4 %collective-permute-start.5 = (bf16[4,128,1024]{2,1,0:T(8,128)(2,1)S(1)}, bf16[4,128,1024]{2,1,0:T(8,128)(2,1)}, u32[]{:S(2)}, u32[]{:S(2)}) collective-permute-start(bf16[4,128,1024]{2,1,0:T(8,128)(2,1)S(1)} %pad_maximum_fusion.refs_0_), channel_id=1, source_target_pairs={{0,1},{1,0},{2,3},{3,2},{4,5},{5,4},{6,7},{7,6},{8,9},{9,8},{10,11... | collective-permute-start | bytes 3145736 | tf_op jit(solution)/shard_map/ppermute | solution.py:30
  120.5 2.4 %collective-permute-start.9 = (bf16[4,128,1024]{2,1,0:T(8,128)(2,1)S(1)}, bf16[4,128,1024]{2,1,0:T(8,128)(2,1)}, u32[]{:S(2)}, u32[]{:S(2)}) collective-permute-start(bf16[4,128,1024]{2,1,0:T(8,128)(2,1)S(1)} %collective-permute-done.4.refs_6_), channel_id=1, source_target_pairs={{0,1},{1,0},{2,3},{3,2},{4,5},{5,4},{6,7},{7,6},{8,9},{9,8},{10,11... | collective-permute-start | bytes 3145736 | tf_op jit(solution)/shard_map/ppermute | solution.py:30
  125.3 5.6 %all-to-all-done.4 = bf16[8,256,256]{2,1,0:T(8,128)(2,1)S(1)} async-done(((bf16[8,256,256]{2,1,0:T(8,128)(2,1)}), bf16[8,256,256]{2,1,0:T(8,128)(2,1)S(1)}, u32[]{:S(2)}, u32[]{:S(2)}) %all-to-all-start.4) | async-done | bytes 1048608 | tf_op jit(solution)/shard_map/all_to_all | solution.py:375
  131.9 7.4 %finish.1 = (bf16[256,1024]{1,0:T(8,128)(2,1)}, bf16[2,1024,256]{2,1,0:T(8,128)(2,1)}) custom-call(s32[5]{0:T(128)} %stack.67.where_ref, bf16[4,128,1024]{2,1,0:T(8,128)(2,1)} %copy-done.1, bf16[4,128,1024]{2,1,0:T(8,128)(2,1)} %collective-permute-done.5.refs_1_, bf16[4,128,1024]{2,1,0:T(8,128)(2,1)} %copy-done.4, ...), custom_call_target="tpu_custom_call" | custom-call | flops 1073741824 | bytes 16777216 | tf_op jit(solution)/shard_map/finish/pallas_call | solution.py:273
  139.3 11.4 %collective-permute-start.10 = (bf16[256,1024]{1,0:T(8,128)(2,1)}, bf16[256,1024]{1,0:T(8,128)(2,1)S(1)}, u32[]{:S(2)}, u32[]{:S(2)}) collective-permute-start(bf16[256,1024]{1,0:T(8,128)(2,1)} %get-tuple-element.36), channel_id=1, source_target_pairs={{0,2},{2,0},{1,3},{3,1},{4,6},{6,4},{5,7},{7,5},{8,10},{10,8},{9,1... | collective-permute-start | bytes 1572872 | tf_op jit(solution)/shard_map/ppermute | solution.py:30
  150.8 5.4 %keep.1 = f32[256,1024]{1,0:T(8,128)} custom-call(s32[5]{0:T(128)} %stack.67.where_ref, bf16[4,128,1024]{2,1,0:T(8,128)(2,1)} %copy-done.1, bf16[4,128,1024]{2,1,0:T(8,128)(2,1)} %collective-permute-done.5.refs_1_, bf16[4,128,1024]{2,1,0:T(8,128)(2,1)} %copy-done.4, bf16[4,128,1024]{2,1,0:T(8,128)(2,1)} %collective-permute-done.6.refs_3_, ...), custom_call_target="tpu_custom_call" | custom-call | flops 1073741824 | bytes 8388608 | tf_op jit(solution)/shard_map/keep/pallas_call | solution.py:299
  156.2 14.8 %collective-permute-done.10 = bf16[256,1024]{1,0:T(8,128)(2,1)S(1)} collective-permute-done((bf16[256,1024]{1,0:T(8,128)(2,1)}, bf16[256,1024]{1,0:T(8,128)(2,1)S(1)}, u32[]{:S(2)}, u32[]{:S(2)}) %collective-permute-start.10) | collective-permute-done | bytes 524320 | tf_op jit(solution)/shard_map/ppermute | solution.py:30
  (39 shorter events, 18.3 us)
Async XLA Ops:
  0.0 0.8 copy-start
  1.6 19.0 %all-to-all-start = ((bf16[8,16,1024]{2,1,0:T(8,128)(2,1)}), bf16[8,16,1024]{2,1,0:T(8,128)(2,1)S(1)}, u32[]{:S(2)}, u32[]{:S(2)}) async-start(bf16[8,16,1024]{2,1,0:T(8,128)(2,1)} %broadcast_in_dim.8), calls=%async_computation | async-start | bytes 524288 | tf_op jit(solution)/shard_map/all_to_all | solution.py:317
  20.6 42.4 %all-to-all-start.1 = ((bf16[8,576,128]{2,1,0:T(8,128)(2,1)}), bf16[8,576,128]{2,1,0:T(8,128)(2,1)}, u32[]{:S(2)}, u32[]{:S(2)}) async-start(bf16[8,576,128]{2,1,0:T(8,128)(2,1)} %get-tuple-element.22), calls=%async_computation.1 | async-start | bytes 2359296 | tf_op jit(solution)/shard_map/all_to_all | solution.py:361
  24.8 22.1 %collective-permute-start.2 = (bf16[128,1024]{1,0:T(8,128)(2,1)S(1)}, bf16[128,1024]{1,0:T(8,128)(2,1)S(1)}, u32[]{:S(2)}, u32[]{:S(2)}) collective-permute-start(bf16[128,1024]{1,0:T(8,128)(2,1)S(1)} %bitcast.22), channel_id=1, source_target_pairs={{0,384},{128,256},{256,128},{384,0},{1,385},{129,257},{257,129},{3... | collective-permute-start | bytes 786440 | tf_op jit(solution)/shard_map/ppermute | solution.py:30
  29.1 20.6 %collective-permute-start.1 = (bf16[128,1024]{1,0:T(8,128)(2,1)S(1)}, bf16[128,1024]{1,0:T(8,128)(2,1)S(1)}, u32[]{:S(2)}, u32[]{:S(2)}) collective-permute-start(bf16[128,1024]{1,0:T(8,128)(2,1)S(1)} %bitcast.23), channel_id=1, source_target_pairs={{0,256},{128,384},{256,0},{384,128},{1,257},{129,385},{257,1},{385... | collective-permute-start | bytes 786440 | tf_op jit(solution)/shard_map/ppermute | solution.py:30
  32.8 16.9 %collective-permute-start = (bf16[128,1024]{1,0:T(8,128)(2,1)S(1)}, bf16[128,1024]{1,0:T(8,128)(2,1)S(1)}, u32[]{:S(2)}, u32[]{:S(2)}) collective-permute-start(bf16[128,1024]{1,0:T(8,128)(2,1)S(1)} %bitcast.24), channel_id=1, source_target_pairs={{0,128},{128,0},{256,384},{384,256},{1,129},{129,1},{257,385},{385... | collective-permute-start | bytes 786440 | tf_op jit(solution)/shard_map/ppermute | solution.py:30
  49.9 66.3 %copy-start.1 = (bf16[4,128,1024]{2,1,0:T(8,128)(2,1)}, bf16[4,128,1024]{2,1,0:T(8,128)(2,1)S(1)}, u32[]{:S(2)}) copy-start(bf16[4,128,1024]{2,1,0:T(8,128)(2,1)S(1)} %pad_maximum_fusion.refs_0_) | copy-start | bytes 3145732
  49.9 43.8 %collective-permute-start.4 = (bf16[4,128,1024]{2,1,0:T(8,128)(2,1)S(1)}, bf16[4,128,1024]{2,1,0:T(8,128)(2,1)S(1)}, u32[]{:S(2)}, u32[]{:S(2)}) collective-permute-start(bf16[4,128,1024]{2,1,0:T(8,128)(2,1)S(1)} %pad_maximum_fusion.refs_0_), channel_id=1, source_target_pairs={{0,96},{32,64},{64,32},{96,0},{1,97},{33,65},{65,33},{97,1},{2,98}... | collective-permute-start | bytes 3145736 | tf_op jit(solution)/shard_map/ppermute | solution.py:30
  54.5 39.1 %collective-permute-start.3 = (bf16[4,128,1024]{2,1,0:T(8,128)(2,1)S(1)}, bf16[4,128,1024]{2,1,0:T(8,128)(2,1)S(1)}, u32[]{:S(2)}, u32[]{:S(2)}) collective-permute-start(bf16[4,128,1024]{2,1,0:T(8,128)(2,1)S(1)} %pad_maximum_fusion.refs_0_), channel_id=1, source_target_pairs={{0,32},{32,0},{64,96},{96,64},{1,33},{33,1},{65,97},{97,65},{2,34}... | collective-permute-start | bytes 3145736 | tf_op jit(solution)/shard_map/ppermute | solution.py:30
  81.2 14.3 %copy-start.5 = (bf16[4,256,128]{2,1,0:T(8,128)(2,1)}, bf16[4,256,128]{2,1,0:T(8,128)(2,1)S(1)}, u32[]{:S(2)}) copy-start(bf16[4,256,128]{2,1,0:T(8,128)(2,1)S(1)} %all_to_all.25.line_ref) | copy-start | bytes 786436
  82.0 13.5 %all-to-all-start.3 = ((bf16[4,256,128]{2,1,0:T(8,128)(2,1)}), bf16[4,256,128]{2,1,0:T(8,128)(2,1)}, u32[]{:S(2)}, u32[]{:S(2)}) async-start(bf16[4,256,128]{2,1,0:T(8,128)(2,1)} %broadcast_in_dim.10), calls=%async_computation.3 | async-start | bytes 524288 | tf_op jit(solution)/shard_map/all_to_all | solution.py:317
  89.2 25.0 %collective-permute-start.7 = (bf16[4,128,1024]{2,1,0:T(8,128)(2,1)S(1)}, bf16[4,128,1024]{2,1,0:T(8,128)(2,1)}, u32[]{:S(2)}, u32[]{:S(2)}) collective-permute-start(bf16[4,128,1024]{2,1,0:T(8,128)(2,1)S(1)} %pad_maximum_fusion.refs_0_), channel_id=1, source_target_pairs={{0,64},{32,96},{64,0},{96,32},{1,65},{33,97},{65,1},{97,33},{2,66}... | collective-permute-start | bytes 3145736 | tf_op jit(solution)/shard_map/ppermute | solution.py:30
  93.6 26.8 %copy-start.3 = (bf16[4,128,1024]{2,1,0:T(8,128)(2,1)}, bf16[4,128,1024]{2,1,0:T(8,128)(2,1)S(1)}, u32[]{:S(2)}) copy-start(bf16[4,128,1024]{2,1,0:T(8,128)(2,1)S(1)} %collective-permute-done.4.refs_6_) | copy-start | bytes 3145732
  93.6 6.0 %copy-start.4 = (bf16[4,128,1024]{2,1,0:T(8,128)(2,1)}, bf16[4,128,1024]{2,1,0:T(8,128)(2,1)S(1)}, u32[]{:S(2)}) copy-start(bf16[4,128,1024]{2,1,0:T(8,128)(2,1)S(1)} %collective-permute-done.3.refs_2_) | copy-start | bytes 3145732
  99.6 23.3 %copy-start.6 = (f32[2048]{0:T(1024)S(1)}, f32[2048]{0:T(1024)}, u32[]{:S(2)}) copy-start(f32[2048]{0:T(1024)} %param.14) | copy-start | bytes 24580
  99.6 31.3 %all-to-all-start.4 = ((bf16[8,256,256]{2,1,0:T(8,128)(2,1)}), bf16[8,256,256]{2,1,0:T(8,128)(2,1)S(1)}, u32[]{:S(2)}, u32[]{:S(2)}) async-start(bf16[8,256,256]{2,1,0:T(8,128)(2,1)} %far_levels.1), calls=%async_computation.4 | async-start | bytes 2097152 | tf_op jit(solution)/shard_map/all_to_all | solution.py:375
  114.2 10.7 %collective-permute-start.8 = (bf16[4,128,1024]{2,1,0:T(8,128)(2,1)}, bf16[4,128,1024]{2,1,0:T(8,128)(2,1)}, u32[]{:S(2)}, u32[]{:S(2)}) collective-permute-start(bf16[4,128,1024]{2,1,0:T(8,128)(2,1)} %collective-permute-done.7.refs_4_), channel_id=1, source_target_pairs={{0,1},{1,0},{2,3},{3,2},{4,5},{5,4},{6,7},{7,6},{8,9},{9,8},{10,11... | collective-permute-start | bytes 3145736 | tf_op jit(solution)/shard_map/ppermute | solution.py:30
  116.1 8.8 %collective-permute-start.5 = (bf16[4,128,1024]{2,1,0:T(8,128)(2,1)S(1)}, bf16[4,128,1024]{2,1,0:T(8,128)(2,1)}, u32[]{:S(2)}, u32[]{:S(2)}) collective-permute-start(bf16[4,128,1024]{2,1,0:T(8,128)(2,1)S(1)} %pad_maximum_fusion.refs_0_), channel_id=1, source_target_pairs={{0,1},{1,0},{2,3},{3,2},{4,5},{5,4},{6,7},{7,6},{8,9},{9,8},{10,11... | collective-permute-start | bytes 3145736 | tf_op jit(solution)/shard_map/ppermute | solution.py:30
  118.5 6.4 %collective-permute-start.6 = (bf16[4,128,1024]{2,1,0:T(8,128)(2,1)}, bf16[4,128,1024]{2,1,0:T(8,128)(2,1)}, u32[]{:S(2)}, u32[]{:S(2)}) collective-permute-start(bf16[4,128,1024]{2,1,0:T(8,128)(2,1)} %copy-done.4), channel_id=1, source_target_pairs={{0,1},{1,0},{2,3},{3,2},{4,5},{5,4},{6,7},{7,6},{8,9},{9,8},{10,11... | collective-permute-start | bytes 3145736 | tf_op jit(solution)/shard_map/ppermute | solution.py:30
  120.5 4.8 %collective-permute-start.9 = (bf16[4,128,1024]{2,1,0:T(8,128)(2,1)S(1)}, bf16[4,128,1024]{2,1,0:T(8,128)(2,1)}, u32[]{:S(2)}, u32[]{:S(2)}) collective-permute-start(bf16[4,128,1024]{2,1,0:T(8,128)(2,1)S(1)} %collective-permute-done.4.refs_6_), channel_id=1, source_target_pairs={{0,1},{1,0},{2,3},{3,2},{4,5},{5,4},{6,7},{7,6},{8,9},{9,8},{10,11... | collective-permute-start | bytes 3145736 | tf_op jit(solution)/shard_map/ppermute | solution.py:30
  130.9 1.0 copy-start.2
  139.3 31.6 %collective-permute-start.10 = (bf16[256,1024]{1,0:T(8,128)(2,1)}, bf16[256,1024]{1,0:T(8,128)(2,1)S(1)}, u32[]{:S(2)}, u32[]{:S(2)}) collective-permute-start(bf16[256,1024]{1,0:T(8,128)(2,1)} %get-tuple-element.36), channel_id=1, source_target_pairs={{0,2},{2,0},{1,3},{3,1},{4,6},{6,4},{5,7},{7,5},{8,10},{10,8},{9,1... | collective-permute-start | bytes 1572872 | tf_op jit(solution)/shard_map/ppermute | solution.py:30

commit v6 on v5

--- a/solution.py
+++ b/solution.py
@@ -285,7 +285,7 @@
             jax.ShapeDtypeStruct((tok, wide * steps), bf16),
             jax.ShapeDtypeStruct((2, rows // 2, tok), bf16),
         ],
-        compiler_params=params(max(VMEM_MIB, 40)),
+        compiler_params=params(40),
         cost_estimate=cost(2 * tok * rows * wide * steps, 16 * 2**20),
         name="finish",
     )(where, *pieces, *others)
@@ -306,7 +306,7 @@
             out_specs=pl.BlockSpec((tok, wide), lambda i, where: (0, i)),
         ),
         out_shape=jax.ShapeDtypeStruct((tok, wide * steps), f32),
-        compiler_params=params(max(VMEM_MIB, 40)),
+        compiler_params=params(40),
         cost_estimate=cost(2 * tok * 2 * rows * wide * steps, 8 * 2**20),
         name="keep",
     )(where, *pieces, normed)
@@ -322,10 +322,6 @@
     mine = lax.axis_index("rep")
     half = lax.dynamic_slice_in_dim(out_weight, mine * (rows // 2), rows // 2, 0).T
     return shared_along(half, "y").reshape(-1, rows // 2)
-
-
-def weight_plane(line):
-    return jnp.stack([line] + [swapped(line, "zl", d) for d in range(1, lax.axis_size("zl"))])
 
 
 def weight_pieces(halves):
@@ -359,10 +355,12 @@
     vt, sent = to_group(uppers, seq_values, seq_keys, seq_queries, level_weights, group, slot)
     sent, weight = lax.optimization_barrier((sent, weight))
     raw = lax.all_to_all(sent, "y", 0, 0, tiled=True)
-    weight = weight_plane(weight)
+    planes = [swapped(weight, "zl", d) for d in range(1, lax.axis_size("zl"))]
     acc, silu = local_part(vt, seq_gate, seq_keys, seq_queries, level_weights, skip_gain, head_size)
-    raw, acc, silu, own = lax.optimization_barrier((raw, acc, silu, weight))
-    near, middle, last = [swapped(weight, "x", k) for k in range(1, lax.axis_size("x"))]
+    planes, acc, silu = lax.optimization_barrier((planes, acc, silu))
+    own = jnp.stack([weight, *planes])
+    near, middle, last = [swapped(own, "x", k) for k in range(1, lax.axis_size("x"))]
+    raw, own = lax.optimization_barrier((raw, own))
 
     def summed(blocks):
         return jnp.sum(blocks.astype(f32), axis=0).astype(bf16)

time: 174 us -> 170 us (0.977)
  blocking collectives: 17.2 us -> 24.4 us
  waiting for transfers between devices: 51.2 us -> 47.5 us
  Pallas kernels: 27.2 us -> 23.6 us
  other arithmetic: 4.64 us -> 2.36 us
    all_to_all x1, blocking collectives: 17.2 us -> 24.4 us  [shared_along(): return lax.all_to_all(spread, axis, 0, 0, tiled=True)]
    ppermute x11, waiting for transfers between devices: 36.5 us -> 32.2 us  [swapped(): lax.ppermute(value, axis, [(i, i ^ mask) for i in range(lax.axis_size(axi...]
    pallas_call x1, Pallas kernels: 7.44 us -> 5.44 us  [finish(): pl.pallas_call(finish_kernel, grid_spec=pltpu.PrefetchScalarGridSpec(num_...]
  transfers between devices with their start and end apart: 15 -> 15, of which waited for: 8 -> 9; matrix products, arithmetic and copies ran while one was open for 3% -> 2% of each run, Pallas kernels for 11% -> 11%
where the time goes in v6:
time: 170 us; the launch traced here: 169 us
  starting transfers between devices  65.9 us (39%)
  waiting for transfers between devices  47.5 us (28%)
  blocking collectives  24.4 us (14%)
  Pallas kernels  23.6 us (14%)
  local copies, waits for them, and re-layouts  5.22 us (3%)
  other arithmetic  2.36 us (1%)
    ppermute x11, starting transfers between devices, swapped(): lax.ppermute(value, axis, [(i, i ^ mask) for i in range(lax.axis_size(axi...  41.8 us
    ppermute x11, waiting for transfers between devices, swapped(): lax.ppermute(value, axis, [(i, i ^ mask) for i in range(lax.axis_size(axi...  32.2 us
    all_to_all x1, blocking collectives, shared_along(): return lax.all_to_all(spread, axis, 0, 0, tiled=True)  24.4 us
    all_to_all x2, starting transfers between devices, shared_along(): return lax.all_to_all(spread, axis, 0, 0, tiled=True)  13.5 us
    all_to_all x2, waiting for transfers between devices, shared_along(): return lax.all_to_all(spread, axis, 0, 0, tiled=True)  9.08 us
    all_to_all x1, starting transfers between devices, on_device(): far = lax.all_to_all(far, 'y', 0, 0, tiled=True).reshape(width, tok)  6.97 us
    all_to_all x1, waiting for transfers between devices, on_device(): far = lax.all_to_all(far, 'y', 0, 0, tiled=True).reshape(width, tok)  6.23 us
    pallas_call x1, Pallas kernels, local_part(): pl.pallas_call(functools.partial(local_kernel, heads, tok // 2), grid=(st...  6.2 us
  transfers between devices with their start and end apart: 15, of which 9 were waited for; matrix products, arithmetic and copies ran while one was open for 2% of the time, Pallas kernels for 11%

profile of v6, /device:TPU:64, one launch (start us, length us, event | category | flops | bytes accessed | tf_op | source)
XLA Modules:
  0.0 169.1 jit_solution(2242300621786300812)
XLA Ops:
  1.6 7.1 %all-to-all-start = ((bf16[8,16,1024]{2,1,0:T(8,128)(2,1)}), bf16[8,16,1024]{2,1,0:T(8,128)(2,1)S(1)}, u32[]{:S(2)}, u32[]{:S(2)}) async-start(bf16[8,16,1024]{2,1,0:T(8,128)(2,1)} %broadcast_in_dim.8), calls=%async_computation | async-start | bytes 524288 | tf_op jit(solution)/shard_map/all_to_all | solution.py:317
  9.4 4.0 %to_group.1 = (bf16[2048,256]{1,0:T(8,128)(2,1)}, bf16[8,576,128]{2,1,0:T(8,128)(2,1)}) custom-call(f32[7]{0:T(128)} %convert_element_type.6.upper_ref, bf16[256,2048]{1,0:T(8,128)(2,1)} %values_ref.1, bf16[256,128]{1,0:T(8,128)(2,1)} %keys_ref.3, bf16[256,128]{1,0:T(8,128)(2,1)} %query_ref.3, bf16[16,32,256]{2,1,0:T(8,128)(2,1)} %w_ref.3), custom_call_target="tpu_custom_call" | custom-call | flops 134217728 | bytes 2097152 | tf_op jit(solution)/shard_map/to_group/pallas_call | solution.py:66
  13.3 7.2 %all-to-all-done = bf16[8,16,1024]{2,1,0:T(8,128)(2,1)S(1)} async-done(((bf16[8,16,1024]{2,1,0:T(8,128)(2,1)}), bf16[8,16,1024]{2,1,0:T(8,128)(2,1)S(1)}, u32[]{:S(2)}, u32[]{:S(2)}) %all-to-all-start) | async-done | bytes 262176 | tf_op jit(solution)/shard_map/all_to_all | solution.py:317
  20.6 3.6 %all-to-all-start.1 = ((bf16[8,576,128]{2,1,0:T(8,128)(2,1)}), bf16[8,576,128]{2,1,0:T(8,128)(2,1)S(1)}, u32[]{:S(2)}, u32[]{:S(2)}) async-start(bf16[8,576,128]{2,1,0:T(8,128)(2,1)} %get-tuple-element.25), calls=%async_computation.1 | async-start | bytes 2359296 | tf_op jit(solution)/shard_map/all_to_all | solution.py:357
  24.1 4.3 %collective-permute-start.2 = (bf16[128,1024]{1,0:T(8,128)(2,1)S(1)}, bf16[128,1024]{1,0:T(8,128)(2,1)S(1)}, u32[]{:S(2)}, u32[]{:S(2)}) collective-permute-start(bf16[128,1024]{1,0:T(8,128)(2,1)S(1)} %bitcast.22), channel_id=1, source_target_pairs={{0,384},{128,256},{256,128},{384,0},{1,385},{129,257},{257,129},{3... | collective-permute-start | bytes 786440 | tf_op jit(solution)/shard_map/ppermute | solution.py:30
  28.4 3.7 %collective-permute-start.1 = (bf16[128,1024]{1,0:T(8,128)(2,1)S(1)}, bf16[128,1024]{1,0:T(8,128)(2,1)S(1)}, u32[]{:S(2)}, u32[]{:S(2)}) collective-permute-start(bf16[128,1024]{1,0:T(8,128)(2,1)S(1)} %bitcast.23), channel_id=1, source_target_pairs={{0,256},{128,384},{256,0},{384,128},{1,257},{129,385},{257,1},{385... | collective-permute-start | bytes 786440 | tf_op jit(solution)/shard_map/ppermute | solution.py:30
  32.2 3.4 %collective-permute-start = (bf16[128,1024]{1,0:T(8,128)(2,1)S(1)}, bf16[128,1024]{1,0:T(8,128)(2,1)S(1)}, u32[]{:S(2)}, u32[]{:S(2)}) collective-permute-start(bf16[128,1024]{1,0:T(8,128)(2,1)S(1)} %bitcast.24), channel_id=1, source_target_pairs={{0,128},{128,0},{256,384},{384,256},{1,129},{129,1},{257,385},{385... | collective-permute-start | bytes 786440 | tf_op jit(solution)/shard_map/ppermute | solution.py:30
  35.5 6.2 %local_part.1 = (f32[2048,256]{1,0:T(8,128)}, f32[2048,256]{1,0:T(8,128)}) custom-call(f32[32]{0:T(128)} %skip_ref.1, bf16[2048,256]{1,0:T(8,128)(2,1)} %get-tuple-element.27.vt_ref, bf16[256,2048]{1,0:T(8,128)(2,1)} %gate_ref.1, bf16[256,128]{1,0:T(8,128)(2,1)} %keys_ref.3, bf16[256,128]{1,0:T(8,128)(2,1)} %query_ref.3, bf16[16,32,256]{2,1,0:T(8,128)(2,1)} %w_ref.3), custom_call_target="tpu_custom_call" | custom-call | flops 1073741824 | bytes 6291456 | tf_op jit(solution)/shard_map/local_part/pallas_call | solution.py:140
  41.7 4.5 %collective-permute-done.2 = bf16[128,1024]{1,0:T(8,128)(2,1)S(1)} collective-permute-done((bf16[128,1024]{1,0:T(8,128)(2,1)S(1)}, bf16[128,1024]{1,0:T(8,128)(2,1)S(1)}, u32[]{:S(2)}, u32[]{:S(2)}) %collective-permute-start.2) | collective-permute-done | bytes 262176 | tf_op jit(solution)/shard_map/ppermute | solution.py:30
  46.2 2.8 %collective-permute-done.1 = bf16[128,1024]{1,0:T(8,128)(2,1)S(1)} collective-permute-done((bf16[128,1024]{1,0:T(8,128)(2,1)S(1)}, bf16[128,1024]{1,0:T(8,128)(2,1)S(1)}, u32[]{:S(2)}, u32[]{:S(2)}) %collective-permute-start.1) | collective-permute-done | bytes 262176 | tf_op jit(solution)/shard_map/ppermute | solution.py:30
  49.2 4.7 %collective-permute-start.4 = (bf16[4,128,1024]{2,1,0:T(8,128)(2,1)S(1)}, bf16[4,128,1024]{2,1,0:T(8,128)(2,1)}, u32[]{:S(2)}, u32[]{:S(2)}) collective-permute-start(bf16[4,128,1024]{2,1,0:T(8,128)(2,1)S(1)} %pad_maximum_fusion.refs_0_), channel_id=1, source_target_pairs={{0,96},{32,64},{64,32},{96,0},{1,97},{33,65},{65,33},{97,1},{2,98}... | collective-permute-start | bytes 3145736 | tf_op jit(solution)/shard_map/ppermute | solution.py:30
  56.1 24.4 %all_to_all.25.line_ref = bf16[4,256,128]{2,1,0:T(8,128)(2,1)S(1)} all-to-all(bf16[4,256,128]{2,1,0:T(8,128)(2,1)S(1)} %broadcast_in_dim.9), channel_id=1, replica_groups=mesh['zl'=4,'x'=4,'y'=8,'head'=2,'rep'=2] {'x'}, dimensions={0} | all-to-all | bytes 524288 | tf_op jit(solution)/shard_map/all_to_all | solution.py:317
  81.4 6.4 %all-to-all-start.3 = ((bf16[4,256,128]{2,1,0:T(8,128)(2,1)}), bf16[4,256,128]{2,1,0:T(8,128)(2,1)S(1)}, u32[]{:S(2)}, u32[]{:S(2)}) async-start(bf16[4,256,128]{2,1,0:T(8,128)(2,1)} %broadcast_in_dim.10), calls=%async_computation.3 | async-start | bytes 524288 | tf_op jit(solution)/shard_map/all_to_all | solution.py:317
  87.8 3.8 %collective-permute-start.7 = (bf16[4,128,1024]{2,1,0:T(8,128)(2,1)S(1)}, bf16[4,128,1024]{2,1,0:T(8,128)(2,1)}, u32[]{:S(2)}, u32[]{:S(2)}) collective-permute-start(bf16[4,128,1024]{2,1,0:T(8,128)(2,1)S(1)} %pad_maximum_fusion.refs_0_), channel_id=1, source_target_pairs={{0,64},{32,96},{64,0},{96,32},{1,65},{33,97},{65,1},{97,33},{2,66}... | collective-permute-start | bytes 3145736 | tf_op jit(solution)/shard_map/ppermute | solution.py:30
  94.7 4.1 %far_levels.1 = bf16[8,256,256]{2,1,0:T(8,128)(2,1)} custom-call(s32[2]{0:T(128)} %pad_add_fusion.where_ref, bf16[8,576,128]{2,1,0:T(8,128)(2,1)} %copy-done.2, bf16[4,256,128]{2,1,0:T(8,128)(2,1)} %copy-done.3, bf16[4,256,128]{2,1,0:T(8,128)(2,1)} %copy-done.4), custom_call_target="tpu_custom_call" | custom-call | flops 805306368 | bytes 4194304 | tf_op jit(solution)/shard_map/far_levels/pallas_call | solution.py:212
  98.8 7.0 %all-to-all-start.4 = ((bf16[8,256,256]{2,1,0:T(8,128)(2,1)}), bf16[8,256,256]{2,1,0:T(8,128)(2,1)S(1)}, u32[]{:S(2)}, u32[]{:S(2)}) async-start(bf16[8,256,256]{2,1,0:T(8,128)(2,1)} %far_levels.1), calls=%async_computation.4 | async-start | bytes 2097152 | tf_op jit(solution)/shard_map/all_to_all | solution.py:373
  105.7 6.9 %collective-permute-done.7.refs_4_ = bf16[4,128,1024]{2,1,0:T(8,128)(2,1)} collective-permute-done((bf16[4,128,1024]{2,1,0:T(8,128)(2,1)S(1)}, bf16[4,128,1024]{2,1,0:T(8,128)(2,1)}, u32[]{:S(2)}, u32[]{:S(2)}) %collective-permute-start.7) | collective-permute-done | bytes 1048608 | tf_op jit(solution)/shard_map/ppermute | solution.py:30
  114.6 2.4 %collective-permute-start.5 = (bf16[4,128,1024]{2,1,0:T(8,128)(2,1)S(1)}, bf16[4,128,1024]{2,1,0:T(8,128)(2,1)}, u32[]{:S(2)}, u32[]{:S(2)}) collective-permute-start(bf16[4,128,1024]{2,1,0:T(8,128)(2,1)S(1)} %pad_maximum_fusion.refs_0_), channel_id=1, source_target_pairs={{0,1},{1,0},{2,3},{3,2},{4,5},{5,4},{6,7},{7,6},{8,9},{9,8},{10,11... | collective-permute-start | bytes 3145736 | tf_op jit(solution)/shard_map/ppermute | solution.py:30
  119.0 2.4 %collective-permute-start.9 = (bf16[4,128,1024]{2,1,0:T(8,128)(2,1)}, bf16[4,128,1024]{2,1,0:T(8,128)(2,1)}, u32[]{:S(2)}, u32[]{:S(2)}) collective-permute-start(bf16[4,128,1024]{2,1,0:T(8,128)(2,1)} %collective-permute-done.4.refs_6_), channel_id=1, source_target_pairs={{0,1},{1,0},{2,3},{3,2},{4,5},{5,4},{6,7},{7,6},{8,9},{9,8},{10,11... | collective-permute-start | bytes 3145736 | tf_op jit(solution)/shard_map/ppermute | solution.py:30
  124.0 6.2 %all-to-all-done.4 = bf16[8,256,256]{2,1,0:T(8,128)(2,1)S(1)} async-done(((bf16[8,256,256]{2,1,0:T(8,128)(2,1)}), bf16[8,256,256]{2,1,0:T(8,128)(2,1)S(1)}, u32[]{:S(2)}, u32[]{:S(2)}) %all-to-all-start.4) | async-done | bytes 1048608 | tf_op jit(solution)/shard_map/all_to_all | solution.py:373
  131.8 5.4 %finish.1 = (bf16[256,1024]{1,0:T(8,128)(2,1)S(1)}, bf16[2,1024,256]{2,1,0:T(8,128)(2,1)S(1)}) custom-call(s32[5]{0:T(128)S(1)} %stack.67.where_ref, bf16[4,128,1024]{2,1,0:T(8,128)(2,1)S(1)} %pad_maximum_fusion.refs_0_, bf16[4,128,1024]{2,1,0:T(8,128)(2,1)} %collective-permute-done.5.refs_1_, bf16[4,128,1024]{2,1,0:T(8,128)(2,1)} %collective-permute-done.3.refs_2_, ...), custom_call_target="tpu_custom_call" | custom-call | flops 1073741824 | bytes 16777216 | tf_op jit(solution)/shard_map/finish/pallas_call | solution.py:273
  137.2 11.2 %collective-permute-start.10 = (bf16[256,1024]{1,0:T(8,128)(2,1)S(1)}, bf16[256,1024]{1,0:T(8,128)(2,1)S(1)}, u32[]{:S(2)}, u32[]{:S(2)}) collective-permute-start(bf16[256,1024]{1,0:T(8,128)(2,1)S(1)} %get-tuple-element.42), channel_id=1, source_target_pairs={{0,2},{2,0},{1,3},{3,1},{4,6},{6,4},{5,7},{7,5},{8,10},{10,8},{9,1... | collective-permute-start | bytes 1572872 | tf_op jit(solution)/shard_map/ppermute | solution.py:30
  148.5 3.9 %keep.1 = f32[256,1024]{1,0:T(8,128)S(1)} custom-call(s32[5]{0:T(128)S(1)} %stack.67.where_ref, bf16[4,128,1024]{2,1,0:T(8,128)(2,1)S(1)} %pad_maximum_fusion.refs_0_, bf16[4,128,1024]{2,1,0:T(8,128)(2,1)} %collective-permute-done.5.refs_1_, bf16[4,128,1024]{2,1,0:T(8,128)(2,1)} %collective-permute-done.3.refs_2_, ...), custom_call_target="tpu_custom_call" | custom-call | flops 1073741824 | bytes 8388608 | tf_op jit(solution)/shard_map/keep/pallas_call | solution.py:299
  152.4 15.8 %collective-permute-done.10 = bf16[256,1024]{1,0:T(8,128)(2,1)S(1)} collective-permute-done((bf16[256,1024]{1,0:T(8,128)(2,1)S(1)}, bf16[256,1024]{1,0:T(8,128)(2,1)S(1)}, u32[]{:S(2)}, u32[]{:S(2)}) %collective-permute-start.10) | collective-permute-done | bytes 524320 | tf_op jit(solution)/shard_map/ppermute | solution.py:30
  (37 shorter events, 17.5 us)
Async XLA Ops:
  0.0 0.8 copy-start
  1.6 19.0 %all-to-all-start = ((bf16[8,16,1024]{2,1,0:T(8,128)(2,1)}), bf16[8,16,1024]{2,1,0:T(8,128)(2,1)S(1)}, u32[]{:S(2)}, u32[]{:S(2)}) async-start(bf16[8,16,1024]{2,1,0:T(8,128)(2,1)} %broadcast_in_dim.8), calls=%async_computation | async-start | bytes 524288 | tf_op jit(solution)/shard_map/all_to_all | solution.py:317
  20.6 35.4 %all-to-all-start.1 = ((bf16[8,576,128]{2,1,0:T(8,128)(2,1)}), bf16[8,576,128]{2,1,0:T(8,128)(2,1)S(1)}, u32[]{:S(2)}, u32[]{:S(2)}) async-start(bf16[8,576,128]{2,1,0:T(8,128)(2,1)} %get-tuple-element.25), calls=%async_computation.1 | async-start | bytes 2359296 | tf_op jit(solution)/shard_map/all_to_all | solution.py:357
  24.1 22.1 %collective-permute-start.2 = (bf16[128,1024]{1,0:T(8,128)(2,1)S(1)}, bf16[128,1024]{1,0:T(8,128)(2,1)S(1)}, u32[]{:S(2)}, u32[]{:S(2)}) collective-permute-start(bf16[128,1024]{1,0:T(8,128)(2,1)S(1)} %bitcast.22), channel_id=1, source_target_pairs={{0,384},{128,256},{256,128},{384,0},{1,385},{129,257},{257,129},{3... | collective-permute-start | bytes 786440 | tf_op jit(solution)/shard_map/ppermute | solution.py:30
  28.4 20.6 %collective-permute-start.1 = (bf16[128,1024]{1,0:T(8,128)(2,1)S(1)}, bf16[128,1024]{1,0:T(8,128)(2,1)S(1)}, u32[]{:S(2)}, u32[]{:S(2)}) collective-permute-start(bf16[128,1024]{1,0:T(8,128)(2,1)S(1)} %bitcast.23), channel_id=1, source_target_pairs={{0,256},{128,384},{256,0},{384,128},{1,257},{129,385},{257,1},{385... | collective-permute-start | bytes 786440 | tf_op jit(solution)/shard_map/ppermute | solution.py:30
  32.2 16.9 %collective-permute-start = (bf16[128,1024]{1,0:T(8,128)(2,1)S(1)}, bf16[128,1024]{1,0:T(8,128)(2,1)S(1)}, u32[]{:S(2)}, u32[]{:S(2)}) collective-permute-start(bf16[128,1024]{1,0:T(8,128)(2,1)S(1)} %bitcast.24), channel_id=1, source_target_pairs={{0,128},{128,0},{256,384},{384,256},{1,129},{129,1},{257,385},{385... | collective-permute-start | bytes 786440 | tf_op jit(solution)/shard_map/ppermute | solution.py:30
  49.2 43.0 %collective-permute-start.4 = (bf16[4,128,1024]{2,1,0:T(8,128)(2,1)S(1)}, bf16[4,128,1024]{2,1,0:T(8,128)(2,1)}, u32[]{:S(2)}, u32[]{:S(2)}) collective-permute-start(bf16[4,128,1024]{2,1,0:T(8,128)(2,1)S(1)} %pad_maximum_fusion.refs_0_), channel_id=1, source_target_pairs={{0,96},{32,64},{64,32},{96,0},{1,97},{33,65},{65,33},{97,1},{2,98}... | collective-permute-start | bytes 3145736 | tf_op jit(solution)/shard_map/ppermute | solution.py:30
  53.8 38.3 %collective-permute-start.3 = (bf16[4,128,1024]{2,1,0:T(8,128)(2,1)S(1)}, bf16[4,128,1024]{2,1,0:T(8,128)(2,1)}, u32[]{:S(2)}, u32[]{:S(2)}) collective-permute-start(bf16[4,128,1024]{2,1,0:T(8,128)(2,1)S(1)} %pad_maximum_fusion.refs_0_), channel_id=1, source_target_pairs={{0,32},{32,0},{64,96},{96,64},{1,33},{33,1},{65,97},{97,65},{2,34}... | collective-permute-start | bytes 3145736 | tf_op jit(solution)/shard_map/ppermute | solution.py:30
  56.0 25.4 %copy-start.2 = (bf16[8,576,128]{2,1,0:T(8,128)(2,1)}, bf16[8,576,128]{2,1,0:T(8,128)(2,1)S(1)}, u32[]{:S(2)}) copy-start(bf16[8,576,128]{2,1,0:T(8,128)(2,1)S(1)} %all-to-all-done.1.got_ref) | copy-start | bytes 3538948
  80.5 13.4 %copy-start.3 = (bf16[4,256,128]{2,1,0:T(8,128)(2,1)}, bf16[4,256,128]{2,1,0:T(8,128)(2,1)S(1)}, u32[]{:S(2)}) copy-start(bf16[4,256,128]{2,1,0:T(8,128)(2,1)S(1)} %all_to_all.25.line_ref) | copy-start | bytes 786436
  81.4 12.6 %all-to-all-start.3 = ((bf16[4,256,128]{2,1,0:T(8,128)(2,1)}), bf16[4,256,128]{2,1,0:T(8,128)(2,1)S(1)}, u32[]{:S(2)}, u32[]{:S(2)}) async-start(bf16[4,256,128]{2,1,0:T(8,128)(2,1)} %broadcast_in_dim.10), calls=%async_computation.3 | async-start | bytes 524288 | tf_op jit(solution)/shard_map/all_to_all | solution.py:317
  87.8 24.9 %collective-permute-start.7 = (bf16[4,128,1024]{2,1,0:T(8,128)(2,1)S(1)}, bf16[4,128,1024]{2,1,0:T(8,128)(2,1)}, u32[]{:S(2)}, u32[]{:S(2)}) collective-permute-start(bf16[4,128,1024]{2,1,0:T(8,128)(2,1)S(1)} %pad_maximum_fusion.refs_0_), channel_id=1, source_target_pairs={{0,64},{32,96},{64,0},{96,32},{1,65},{33,97},{65,1},{97,33},{2,66}... | collective-permute-start | bytes 3145736 | tf_op jit(solution)/shard_map/ppermute | solution.py:30
  94.0 0.7 copy-start.4
  98.8 22.6 %copy-start.5 = (f32[2048]{0:T(1024)S(1)}, f32[2048]{0:T(1024)}, u32[]{:S(2)}) copy-start(f32[2048]{0:T(1024)} %param.14) | copy-start | bytes 24580
  98.8 31.4 %all-to-all-start.4 = ((bf16[8,256,256]{2,1,0:T(8,128)(2,1)}), bf16[8,256,256]{2,1,0:T(8,128)(2,1)S(1)}, u32[]{:S(2)}, u32[]{:S(2)}) async-start(bf16[8,256,256]{2,1,0:T(8,128)(2,1)} %far_levels.1), calls=%async_computation.4 | async-start | bytes 2097152 | tf_op jit(solution)/shard_map/all_to_all | solution.py:373
  112.7 9.2 %collective-permute-start.8 = (bf16[4,128,1024]{2,1,0:T(8,128)(2,1)}, bf16[4,128,1024]{2,1,0:T(8,128)(2,1)}, u32[]{:S(2)}, u32[]{:S(2)}) collective-permute-start(bf16[4,128,1024]{2,1,0:T(8,128)(2,1)} %collective-permute-done.7.refs_4_), channel_id=1, source_target_pairs={{0,1},{1,0},{2,3},{3,2},{4,5},{5,4},{6,7},{7,6},{8,9},{9,8},{10,11... | collective-permute-start | bytes 3145736 | tf_op jit(solution)/shard_map/ppermute | solution.py:30
  114.6 7.2 %collective-permute-start.5 = (bf16[4,128,1024]{2,1,0:T(8,128)(2,1)S(1)}, bf16[4,128,1024]{2,1,0:T(8,128)(2,1)}, u32[]{:S(2)}, u32[]{:S(2)}) collective-permute-start(bf16[4,128,1024]{2,1,0:T(8,128)(2,1)S(1)} %pad_maximum_fusion.refs_0_), channel_id=1, source_target_pairs={{0,1},{1,0},{2,3},{3,2},{4,5},{5,4},{6,7},{7,6},{8,9},{9,8},{10,11... | collective-permute-start | bytes 3145736 | tf_op jit(solution)/shard_map/ppermute | solution.py:30
  117.0 4.9 %collective-permute-start.6 = (bf16[4,128,1024]{2,1,0:T(8,128)(2,1)}, bf16[4,128,1024]{2,1,0:T(8,128)(2,1)}, u32[]{:S(2)}, u32[]{:S(2)}) collective-permute-start(bf16[4,128,1024]{2,1,0:T(8,128)(2,1)} %collective-permute-done.3.refs_2_), channel_id=1, source_target_pairs={{0,1},{1,0},{2,3},{3,2},{4,5},{5,4},{6,7},{7,6},{8,9},{9,8},{10,11... | collective-permute-start | bytes 3145736 | tf_op jit(solution)/shard_map/ppermute | solution.py:30
  119.0 5.0 %collective-permute-start.9 = (bf16[4,128,1024]{2,1,0:T(8,128)(2,1)}, bf16[4,128,1024]{2,1,0:T(8,128)(2,1)}, u32[]{:S(2)}, u32[]{:S(2)}) collective-permute-start(bf16[4,128,1024]{2,1,0:T(8,128)(2,1)} %collective-permute-done.4.refs_6_), channel_id=1, source_target_pairs={{0,1},{1,0},{2,3},{3,2},{4,5},{5,4},{6,7},{7,6},{8,9},{9,8},{10,11... | collective-permute-start | bytes 3145736 | tf_op jit(solution)/shard_map/ppermute | solution.py:30
  130.2 1.6 copy-start.1
  137.2 31.0 %collective-permute-start.10 = (bf16[256,1024]{1,0:T(8,128)(2,1)S(1)}, bf16[256,1024]{1,0:T(8,128)(2,1)S(1)}, u32[]{:S(2)}, u32[]{:S(2)}) collective-permute-start(bf16[256,1024]{1,0:T(8,128)(2,1)S(1)} %get-tuple-element.42), channel_id=1, source_target_pairs={{0,2},{2,0},{1,3},{3,1},{4,6},{6,4},{5,7},{7,5},{8,10},{10,8},{9,1... | collective-permute-start | bytes 1572872 | tf_op jit(solution)/shard_map/ppermute | solution.py:30

commit v7 on v6

--- a/solution.py
+++ b/solution.py
@@ -166,26 +166,73 @@
     return (part * weights[level * heads : (level + 1) * heads][:, None, :]).reshape(rows, tok)
 
 
-def sibling_sum(ref, index, bit, rows):
-    count = 1 << bit
+def total_of(parts):
+    total = parts[0].astype(f32)
+    for part in parts[1:]:
+        total = total + part.astype(f32)
+    return total.astype(bf16)
+
+
+def siblings(index, bit):
     first = ((index >> bit) ^ 1) << bit
-    if count == 1:
-        return ref[first, :rows]
-    total = ref[first, :rows].astype(f32)
-    for k in range(1, count):
-        total = total + ref[first + k, :rows].astype(f32)
-    return total.astype(bf16)
-
-
-def far_kernel(heads, slot, where_ref, got_ref, line_ref, plane_ref, out_ref):
+    return [first + k for k in range(1 << bit)]
+
+
+def group_kernel(got_ref, out_ref):
+    total = total_of([got_ref[j] for j in range(got_ref.shape[0])])
+    for k in range(out_ref.shape[0]):
+        out_ref[k] = total
+
+
+def group_sum(got, rows, copies):
+    group, _, n = got.shape
+    return pl.pallas_call(
+        group_kernel,
+        grid=(1,),
+        in_specs=[pl.BlockSpec((group, rows, n), lambda i: (0, 0, 0))],
+        out_specs=pl.BlockSpec((copies, rows, n), lambda i: (0, 0, 0)),
+        out_shape=jax.ShapeDtypeStruct((copies, rows, n), bf16),
+        compiler_params=params(8),
+        cost_estimate=cost(group * rows * n, 2 * (group + copies) * rows * n),
+        name="group_sum",
+    )(got)
+
+
+def column_kernel(where_ref, line_ref, out_ref):
+    z = where_ref[1]
+    sums = [line_ref[z]]
+    sums += [total_of([line_ref[i] for i in siblings(z, bit)]) for bit in range(2)]
+    for k in range(out_ref.shape[0]):
+        for i, value in enumerate(sums):
+            out_ref[k, i] = value
+
+
+def column_sums(where, line, copies):
+    _, rows, n = line.shape
+    vmem = pl.BlockSpec(memory_space=pltpu.VMEM)
+    return pl.pallas_call(
+        column_kernel,
+        in_specs=[pl.BlockSpec(memory_space=pltpu.SMEM), vmem],
+        out_specs=vmem,
+        out_shape=jax.ShapeDtypeStruct((copies, 3, rows, n), bf16),
+        compiler_params=pltpu.CompilerParams(vmem_limit_bytes=8 * 2**20),
+        cost_estimate=cost(4 * rows * n, 2 * (4 + 3 * copies) * rows * n),
+        name="column_sums",
+    )(where, line)
+
+
+def far_kernel(heads, slot, where_ref, got_ref, plane_ref, out_ref):
     group, rows, tok = out_ref.shape
     n = got_ref.shape[2]
+    x = where_ref[0]
     local = {}
     for bit in range(3):
         for block in range(0, group, 2 << bit):
-            local[bit, block] = sibling_sum(got_ref, block + (1 << bit), bit, rows)
-    shared = [sibling_sum(line_ref, where_ref[0], bit, rows) for bit in range(2)]
-    shared += [sibling_sum(plane_ref, where_ref[1], bit, rows) for bit in range(2)]
+            parts = [got_ref[i, :rows] for i in siblings(block + (1 << bit), bit)]
+            local[bit, block] = total_of(parts)
+    shared = [total_of([plane_ref[i, 0] for i in siblings(x, bit)]) for bit in range(2)]
+    for kind in (1, 2):
+        shared.append(total_of([plane_ref[i, kind] for i in range(plane_ref.shape[0])]))
     for j in range(group):
         query = got_ref[j, rows : rows + tok]
         weights = jnp.concatenate(
@@ -205,19 +252,19 @@
         out_ref[j] = total.astype(bf16)
 
 
-def far_levels(where, got, line, plane, heads, slot, tok):
+def far_levels(where, got, plane, heads, slot, tok):
     group = got.shape[0]
-    rows = line.shape[1]
+    rows = plane.shape[2]
     vmem = pl.BlockSpec(memory_space=pltpu.VMEM)
     return pl.pallas_call(
         functools.partial(far_kernel, heads, slot),
-        in_specs=[pl.BlockSpec(memory_space=pltpu.SMEM), vmem, vmem, vmem],
+        in_specs=[pl.BlockSpec(memory_space=pltpu.SMEM), vmem, vmem],
         out_specs=vmem,
         out_shape=jax.ShapeDtypeStruct((group, rows, tok), bf16),
         compiler_params=pltpu.CompilerParams(vmem_limit_bytes=VMEM_MIB * 2**20),
         cost_estimate=cost(12 * group * rows * tok * 128, 8 * group * rows * tok),
         name="far_levels",
-    )(where, got, line, plane)
+    )(where, got, plane)
 
 
 def project(where_ref, pieces, normed_ref, out_ref):
@@ -362,14 +409,13 @@
     near, middle, last = [swapped(own, "x", k) for k in range(1, lax.axis_size("x"))]
     raw, own = lax.optimization_barrier((raw, own))
 
-    def summed(blocks):
-        return jnp.sum(blocks.astype(f32), axis=0).astype(bf16)
-
-    line = shared_along(summed(raw[:, :rows]), "x")
-    plane = shared_along(summed(line), "zl")
+    line = group_sum(raw, rows, lax.axis_size("zl"))
+    line = lax.all_to_all(line, "zl", 0, 0, tiled=True)
+    plane = column_sums(place, line, lax.axis_size("x"))
+    plane = lax.all_to_all(plane, "x", 0, 0, tiled=True)
     plane, own, near, last = lax.optimization_barrier((plane, own, near, last))
     pieces = weight_pieces([own, near, middle, last])
-    far = far_levels(place, raw, line, plane, heads, slot, tok)
+    far = far_levels(place, raw, plane, heads, slot, tok)
     far = lax.all_to_all(far, "y", 0, 0, tiled=True).reshape(width, tok)
 
     to_send, normed = finish(where, pieces, acc, silu, far, norm_gain[:, None])

time: 170 us -> 167 us (0.982)
  the two profiles are of different devices: /device:TPU:64 before, /device:TPU:6 now
where the time goes in v7:
time: 167 us; the launch traced here: 166 us
  starting transfers between devices  67.6 us (40%)
  waiting for transfers between devices  65.3 us (39%)
  Pallas kernels  26.3 us (16%)
  local copies, waits for them, and re-layouts  4.65 us (3%)
  other arithmetic  1.67 us (1%)
    ppermute x11, starting transfers between devices, swapped(): lax.ppermute(value, axis, [(i, i ^ mask) for i in range(lax.axis_size(axi...  40.8 us
    ppermute x11, waiting for transfers between devices, swapped(): lax.ppermute(value, axis, [(i, i ^ mask) for i in range(lax.axis_size(axi...  33.9 us
    all_to_all x1, waiting for transfers between devices, on_device(): plane = lax.all_to_all(plane, 'x', 0, 0, tiled=True)  11.3 us
    all_to_all x1, waiting for transfers between devices, on_device(): line = lax.all_to_all(line, 'zl', 0, 0, tiled=True)  9.02 us
    all_to_all x1, waiting for transfers between devices, shared_along(): return lax.all_to_all(spread, axis, 0, 0, tiled=True)  7.3 us
    all_to_all x1, starting transfers between devices, shared_along(): return lax.all_to_all(spread, axis, 0, 0, tiled=True)  7.1 us
    all_to_all x1, starting transfers between devices, on_device(): far = lax.all_to_all(far, 'y', 0, 0, tiled=True).reshape(width, tok)  6.93 us
    pallas_call x1, Pallas kernels, local_part(): pl.pallas_call(functools.partial(local_kernel, heads, tok // 2), grid=(st...  6.22 us
  transfers between devices with their start and end apart: 16, of which 9 were waited for; matrix products, arithmetic and copies ran while one was open for 1% of the time, Pallas kernels for 13%

profile of v7, /device:TPU:6, one launch (start us, length us, event | category | flops | bytes accessed | tf_op | source)
XLA Modules:
  0.0 165.7 jit_solution(14522330900402529969)
XLA Ops:
  1.6 7.1 %all-to-all-start = ((bf16[8,16,1024]{2,1,0:T(8,128)(2,1)}), bf16[8,16,1024]{2,1,0:T(8,128)(2,1)S(1)}, u32[]{:S(2)}, u32[]{:S(2)}) async-start(bf16[8,16,1024]{2,1,0:T(8,128)(2,1)} %broadcast_in_dim.4), calls=%async_computation | async-start | bytes 524288 | tf_op jit(solution)/shard_map/all_to_all | solution.py:364
  9.3 4.0 %to_group.1 = (bf16[2048,256]{1,0:T(8,128)(2,1)}, bf16[8,576,128]{2,1,0:T(8,128)(2,1)}) custom-call(f32[7]{0:T(128)} %convert_element_type.9.upper_ref, bf16[256,2048]{1,0:T(8,128)(2,1)} %values_ref.1, bf16[256,128]{1,0:T(8,128)(2,1)} %keys_ref.3, bf16[256,128]{1,0:T(8,128)(2,1)} %query_ref.3, bf16[16,32,256]{2,1,0:T(8,128)(2,1)} %w_ref.3), custom_call_target="tpu_custom_call" | custom-call | flops 134217728 | bytes 2097152 | tf_op jit(solution)/shard_map/to_group/pallas_call | solution.py:66
  13.2 7.3 %all-to-all-done = bf16[8,16,1024]{2,1,0:T(8,128)(2,1)S(1)} async-done(((bf16[8,16,1024]{2,1,0:T(8,128)(2,1)}), bf16[8,16,1024]{2,1,0:T(8,128)(2,1)S(1)}, u32[]{:S(2)}, u32[]{:S(2)}) %all-to-all-start) | async-done | bytes 262176 | tf_op jit(solution)/shard_map/all_to_all | solution.py:364
  20.6 3.6 %all-to-all-start.1 = ((bf16[8,576,128]{2,1,0:T(8,128)(2,1)}), bf16[8,576,128]{2,1,0:T(8,128)(2,1)S(1)}, u32[]{:S(2)}, u32[]{:S(2)}) async-start(bf16[8,576,128]{2,1,0:T(8,128)(2,1)} %get-tuple-element.25), calls=%async_computation.1 | async-start | bytes 2359296 | tf_op jit(solution)/shard_map/all_to_all | solution.py:404
  24.1 7.9 %collective-permute-start.2 = (bf16[128,1024]{1,0:T(8,128)(2,1)S(1)}, bf16[128,1024]{1,0:T(8,128)(2,1)S(1)}, u32[]{:S(2)}, u32[]{:S(2)}) collective-permute-start(bf16[128,1024]{1,0:T(8,128)(2,1)S(1)} %bitcast.22), channel_id=1, source_target_pairs={{0,384},{128,256},{256,128},{384,0},{1,385},{129,257},{257,129},{3... | collective-permute-start | bytes 786440 | tf_op jit(solution)/shard_map/ppermute | solution.py:30
  34.0 2.5 %collective-permute-start = (bf16[128,1024]{1,0:T(8,128)(2,1)S(1)}, bf16[128,1024]{1,0:T(8,128)(2,1)S(1)}, u32[]{:S(2)}, u32[]{:S(2)}) collective-permute-start(bf16[128,1024]{1,0:T(8,128)(2,1)S(1)} %bitcast.24), channel_id=1, source_target_pairs={{0,128},{128,0},{256,384},{384,256},{1,129},{129,1},{257,385},{385... | collective-permute-start | bytes 786440 | tf_op jit(solution)/shard_map/ppermute | solution.py:30
  36.4 6.2 %local_part.1 = (f32[2048,256]{1,0:T(8,128)}, f32[2048,256]{1,0:T(8,128)}) custom-call(f32[32]{0:T(128)} %skip_ref.1, bf16[2048,256]{1,0:T(8,128)(2,1)} %get-tuple-element.27.vt_ref, bf16[256,2048]{1,0:T(8,128)(2,1)} %gate_ref.1, bf16[256,128]{1,0:T(8,128)(2,1)} %keys_ref.3, bf16[256,128]{1,0:T(8,128)(2,1)} %query_ref.3, bf16[16,32,256]{2,1,0:T(8,128)(2,1)} %w_ref.3), custom_call_target="tpu_custom_call" | custom-call | flops 1073741824 | bytes 6291456 | tf_op jit(solution)/shard_map/local_part/pallas_call | solution.py:140
  42.7 8.9 %collective-permute-done.1 = bf16[128,1024]{1,0:T(8,128)(2,1)S(1)} collective-permute-done((bf16[128,1024]{1,0:T(8,128)(2,1)S(1)}, bf16[128,1024]{1,0:T(8,128)(2,1)S(1)}, u32[]{:S(2)}, u32[]{:S(2)}) %collective-permute-start.1) | collective-permute-done | bytes 262176 | tf_op jit(solution)/shard_map/ppermute | solution.py:30
  54.1 2.8 %collective-permute-start.3 = (bf16[4,128,1024]{2,1,0:T(8,128)(2,1)S(1)}, bf16[4,128,1024]{2,1,0:T(8,128)(2,1)}, u32[]{:S(2)}, u32[]{:S(2)}) collective-permute-start(bf16[4,128,1024]{2,1,0:T(8,128)(2,1)S(1)} %pad_maximum_fusion.refs_0_), channel_id=1, source_target_pairs={{0,32},{32,0},{64,96},{96,64},{1,33},{33,1},{65,97},{97,65},{2,34}... | collective-permute-start | bytes 3145736 | tf_op jit(solution)/shard_map/ppermute | solution.py:30
  58.0 4.4 %all-to-all-start.2 = ((bf16[4,256,128]{2,1,0:T(8,128)(2,1)}), bf16[4,256,128]{2,1,0:T(8,128)(2,1)S(1)}, u32[]{:S(2)}, u32[]{:S(2)}) async-start(bf16[4,256,128]{2,1,0:T(8,128)(2,1)} %group_sum.1), calls=%async_computation.2 | async-start | bytes 524288 | tf_op jit(solution)/shard_map/all_to_all | solution.py:413
  62.5 9.0 %all-to-all-done.2.line_ref = bf16[4,256,128]{2,1,0:T(8,128)(2,1)S(1)} async-done(((bf16[4,256,128]{2,1,0:T(8,128)(2,1)}), bf16[4,256,128]{2,1,0:T(8,128)(2,1)S(1)}, u32[]{:S(2)}, u32[]{:S(2)}) %all-to-all-start.2) | async-done | bytes 262176 | tf_op jit(solution)/shard_map/all_to_all | solution.py:413
  73.1 4.8 %all-to-all-start.3 = ((bf16[4,3,256,128]{3,2,1,0:T(8,128)(2,1)}), bf16[4,3,256,128]{3,2,1,0:T(8,128)(2,1)S(1)}, u32[]{:S(2)}, u32[]{:S(2)}) async-start(bf16[4,3,256,128]{3,2,1,0:T(8,128)(2,1)} %column_sums.1), calls=%async_computation.3 | async-start | bytes 1572864 | tf_op jit(solution)/shard_map/all_to_all | solution.py:415
  77.8 3.5 %collective-permute-start.7 = (bf16[4,128,1024]{2,1,0:T(8,128)(2,1)S(1)}, bf16[4,128,1024]{2,1,0:T(8,128)(2,1)}, u32[]{:S(2)}, u32[]{:S(2)}) collective-permute-start(bf16[4,128,1024]{2,1,0:T(8,128)(2,1)S(1)} %pad_maximum_fusion.refs_0_), channel_id=1, source_target_pairs={{0,64},{32,96},{64,0},{96,32},{1,65},{33,97},{65,1},{97,33},{2,66}... | collective-permute-start | bytes 3145736 | tf_op jit(solution)/shard_map/ppermute | solution.py:30
  81.3 11.3 %all-to-all-done.3.plane_ref = bf16[4,3,256,128]{3,2,1,0:T(8,128)(2,1)S(1)} async-done(((bf16[4,3,256,128]{3,2,1,0:T(8,128)(2,1)}), bf16[4,3,256,128]{3,2,1,0:T(8,128)(2,1)S(1)}, u32[]{:S(2)}, u32[]{:S(2)}) %all-to-all-start.3) | async-done | bytes 786464 | tf_op jit(solution)/shard_map/all_to_all | solution.py:415
  93.6 4.2 %far_levels.1 = bf16[8,256,256]{2,1,0:T(8,128)(2,1)} custom-call(s32[2]{0:T(128)} %copy-done.3, bf16[8,576,128]{2,1,0:T(8,128)(2,1)} %copy-done.1, bf16[4,3,256,128]{3,2,1,0:T(8,128)(2,1)} %copy-done.4), custom_call_target="tpu_custom_call" | custom-call | flops 805306368 | bytes 4194304 | tf_op jit(solution)/shard_map/far_levels/pallas_call | solution.py:259
  97.8 6.9 %all-to-all-start.4 = ((bf16[8,256,256]{2,1,0:T(8,128)(2,1)}), bf16[8,256,256]{2,1,0:T(8,128)(2,1)S(1)}, u32[]{:S(2)}, u32[]{:S(2)}) async-start(bf16[8,256,256]{2,1,0:T(8,128)(2,1)} %far_levels.1), calls=%async_computation.4 | async-start | bytes 2097152 | tf_op jit(solution)/shard_map/all_to_all | solution.py:419
  104.7 7.4 %collective-permute-done.7.refs_4_ = bf16[4,128,1024]{2,1,0:T(8,128)(2,1)} collective-permute-done((bf16[4,128,1024]{2,1,0:T(8,128)(2,1)S(1)}, bf16[4,128,1024]{2,1,0:T(8,128)(2,1)}, u32[]{:S(2)}, u32[]{:S(2)}) %collective-permute-start.7) | collective-permute-done | bytes 1048608 | tf_op jit(solution)/shard_map/ppermute | solution.py:30
  114.1 2.4 %collective-permute-start.5 = (bf16[4,128,1024]{2,1,0:T(8,128)(2,1)S(1)}, bf16[4,128,1024]{2,1,0:T(8,128)(2,1)}, u32[]{:S(2)}, u32[]{:S(2)}) collective-permute-start(bf16[4,128,1024]{2,1,0:T(8,128)(2,1)S(1)} %pad_maximum_fusion.refs_0_), channel_id=1, source_target_pairs={{0,1},{1,0},{2,3},{3,2},{4,5},{5,4},{6,7},{7,6},{8,9},{9,8},{10,11... | collective-permute-start | bytes 3145736 | tf_op jit(solution)/shard_map/ppermute | solution.py:30
  118.4 2.4 %collective-permute-start.9 = (bf16[4,128,1024]{2,1,0:T(8,128)(2,1)}, bf16[4,128,1024]{2,1,0:T(8,128)(2,1)}, u32[]{:S(2)}, u32[]{:S(2)}) collective-permute-start(bf16[4,128,1024]{2,1,0:T(8,128)(2,1)} %collective-permute-done.4.refs_6_), channel_id=1, source_target_pairs={{0,1},{1,0},{2,3},{3,2},{4,5},{5,4},{6,7},{7,6},{8,9},{9,8},{10,11... | collective-permute-start | bytes 3145736 | tf_op jit(solution)/shard_map/ppermute | solution.py:30
  123.4 3.7 %all-to-all-done.4 = bf16[8,256,256]{2,1,0:T(8,128)(2,1)S(1)} async-done(((bf16[8,256,256]{2,1,0:T(8,128)(2,1)}), bf16[8,256,256]{2,1,0:T(8,128)(2,1)S(1)}, u32[]{:S(2)}, u32[]{:S(2)}) %all-to-all-start.4) | async-done | bytes 1048608 | tf_op jit(solution)/shard_map/all_to_all | solution.py:419
  128.7 5.4 %finish.1 = (bf16[256,1024]{1,0:T(8,128)(2,1)S(1)}, bf16[2,1024,256]{2,1,0:T(8,128)(2,1)S(1)}) custom-call(s32[5]{0:T(128)S(1)} %stack.67.where_ref, bf16[4,128,1024]{2,1,0:T(8,128)(2,1)S(1)} %pad_maximum_fusion.refs_0_, bf16[4,128,1024]{2,1,0:T(8,128)(2,1)} %collective-permute-done.5.refs_1_, bf16[4,128,1024]{2,1,0:T(8,128)(2,1)} %collective-permute-done.3.refs_2_, ...), custom_call_target="tpu_custom_call" | custom-call | flops 1073741824 | bytes 16777216 | tf_op jit(solution)/shard_map/finish/pallas_call | solution.py:320
  134.2 11.2 %collective-permute-start.10 = (bf16[256,1024]{1,0:T(8,128)(2,1)S(1)}, bf16[256,1024]{1,0:T(8,128)(2,1)S(1)}, u32[]{:S(2)}, u32[]{:S(2)}) collective-permute-start(bf16[256,1024]{1,0:T(8,128)(2,1)S(1)} %get-tuple-element.42), channel_id=1, source_target_pairs={{0,2},{2,0},{1,3},{3,1},{4,6},{6,4},{5,7},{7,5},{8,10},{10,8},{9,1... | collective-permute-start | bytes 1572872 | tf_op jit(solution)/shard_map/ppermute | solution.py:30
  145.4 3.9 %keep.1 = f32[256,1024]{1,0:T(8,128)S(1)} custom-call(s32[5]{0:T(128)S(1)} %stack.67.where_ref, bf16[4,128,1024]{2,1,0:T(8,128)(2,1)S(1)} %pad_maximum_fusion.refs_0_, bf16[4,128,1024]{2,1,0:T(8,128)(2,1)} %collective-permute-done.5.refs_1_, bf16[4,128,1024]{2,1,0:T(8,128)(2,1)} %collective-permute-done.3.refs_2_, ...), custom_call_target="tpu_custom_call" | custom-call | flops 1073741824 | bytes 8388608 | tf_op jit(solution)/shard_map/keep/pallas_call | solution.py:346
  149.3 15.5 %collective-permute-done.10 = bf16[256,1024]{1,0:T(8,128)(2,1)S(1)} collective-permute-done((bf16[256,1024]{1,0:T(8,128)(2,1)S(1)}, bf16[256,1024]{1,0:T(8,128)(2,1)S(1)}, u32[]{:S(2)}, u32[]{:S(2)}) %collective-permute-start.10) | collective-permute-done | bytes 524320 | tf_op jit(solution)/shard_map/ppermute | solution.py:30
  (36 shorter events, 19.2 us)
Async XLA Ops:
  0.0 0.8 copy-start
  1.6 19.0 %all-to-all-start = ((bf16[8,16,1024]{2,1,0:T(8,128)(2,1)}), bf16[8,16,1024]{2,1,0:T(8,128)(2,1)S(1)}, u32[]{:S(2)}, u32[]{:S(2)}) async-start(bf16[8,16,1024]{2,1,0:T(8,128)(2,1)} %broadcast_in_dim.4), calls=%async_computation | async-start | bytes 524288 | tf_op jit(solution)/shard_map/all_to_all | solution.py:364
  20.6 36.4 %all-to-all-start.1 = ((bf16[8,576,128]{2,1,0:T(8,128)(2,1)}), bf16[8,576,128]{2,1,0:T(8,128)(2,1)S(1)}, u32[]{:S(2)}, u32[]{:S(2)}) async-start(bf16[8,576,128]{2,1,0:T(8,128)(2,1)} %get-tuple-element.25), calls=%async_computation.1 | async-start | bytes 2359296 | tf_op jit(solution)/shard_map/all_to_all | solution.py:404
  24.1 18.5 %collective-permute-start.2 = (bf16[128,1024]{1,0:T(8,128)(2,1)S(1)}, bf16[128,1024]{1,0:T(8,128)(2,1)S(1)}, u32[]{:S(2)}, u32[]{:S(2)}) collective-permute-start(bf16[128,1024]{1,0:T(8,128)(2,1)S(1)} %bitcast.22), channel_id=1, source_target_pairs={{0,384},{128,256},{256,128},{384,0},{1,385},{129,257},{257,129},{3... | collective-permute-start | bytes 786440 | tf_op jit(solution)/shard_map/ppermute | solution.py:30
  32.0 19.5 %collective-permute-start.1 = (bf16[128,1024]{1,0:T(8,128)(2,1)S(1)}, bf16[128,1024]{1,0:T(8,128)(2,1)S(1)}, u32[]{:S(2)}, u32[]{:S(2)}) collective-permute-start(bf16[128,1024]{1,0:T(8,128)(2,1)S(1)} %bitcast.23), channel_id=1, source_target_pairs={{0,256},{128,384},{256,0},{384,128},{1,257},{129,385},{257,1},{385... | collective-permute-start | bytes 786440 | tf_op jit(solution)/shard_map/ppermute | solution.py:30
  34.0 17.6 %collective-permute-start = (bf16[128,1024]{1,0:T(8,128)(2,1)S(1)}, bf16[128,1024]{1,0:T(8,128)(2,1)S(1)}, u32[]{:S(2)}, u32[]{:S(2)}) collective-permute-start(bf16[128,1024]{1,0:T(8,128)(2,1)S(1)} %bitcast.24), channel_id=1, source_target_pairs={{0,128},{128,0},{256,384},{384,256},{1,129},{129,1},{257,385},{385... | collective-permute-start | bytes 786440 | tf_op jit(solution)/shard_map/ppermute | solution.py:30
  51.7 29.6 %collective-permute-start.4 = (bf16[4,128,1024]{2,1,0:T(8,128)(2,1)S(1)}, bf16[4,128,1024]{2,1,0:T(8,128)(2,1)}, u32[]{:S(2)}, u32[]{:S(2)}) collective-permute-start(bf16[4,128,1024]{2,1,0:T(8,128)(2,1)S(1)} %pad_maximum_fusion.refs_0_), channel_id=1, source_target_pairs={{0,96},{32,64},{64,32},{96,0},{1,97},{33,65},{65,33},{97,1},{2,98}... | collective-permute-start | bytes 3145736 | tf_op jit(solution)/shard_map/ppermute | solution.py:30
  54.1 27.2 %collective-permute-start.3 = (bf16[4,128,1024]{2,1,0:T(8,128)(2,1)S(1)}, bf16[4,128,1024]{2,1,0:T(8,128)(2,1)}, u32[]{:S(2)}, u32[]{:S(2)}) collective-permute-start(bf16[4,128,1024]{2,1,0:T(8,128)(2,1)S(1)} %pad_maximum_fusion.refs_0_), channel_id=1, source_target_pairs={{0,32},{32,0},{64,96},{96,64},{1,33},{33,1},{65,97},{97,65},{2,34}... | collective-permute-start | bytes 3145736 | tf_op jit(solution)/shard_map/ppermute | solution.py:30
  56.9 16.1 %copy-start.1 = (bf16[8,576,128]{2,1,0:T(8,128)(2,1)}, bf16[8,576,128]{2,1,0:T(8,128)(2,1)S(1)}, u32[]{:S(2)}) copy-start(bf16[8,576,128]{2,1,0:T(8,128)(2,1)S(1)} %all-to-all-done.1.got_ref) | copy-start | bytes 3538948
  58.0 13.5 %all-to-all-start.2 = ((bf16[4,256,128]{2,1,0:T(8,128)(2,1)}), bf16[4,256,128]{2,1,0:T(8,128)(2,1)S(1)}, u32[]{:S(2)}, u32[]{:S(2)}) async-start(bf16[4,256,128]{2,1,0:T(8,128)(2,1)} %group_sum.1), calls=%async_computation.2 | async-start | bytes 524288 | tf_op jit(solution)/shard_map/all_to_all | solution.py:413
  62.5 30.2 %copy-start.3 = (s32[2]{0:T(128)}, s32[2]{0:T(128)S(1)}, u32[]{:S(2)}) copy-start(s32[2]{0:T(128)S(1)} %pad_add_fusion.where_ref) | copy-start | bytes 28
  73.1 19.6 %all-to-all-start.3 = ((bf16[4,3,256,128]{3,2,1,0:T(8,128)(2,1)}), bf16[4,3,256,128]{3,2,1,0:T(8,128)(2,1)S(1)}, u32[]{:S(2)}, u32[]{:S(2)}) async-start(bf16[4,3,256,128]{3,2,1,0:T(8,128)(2,1)} %column_sums.1), calls=%async_computation.3 | async-start | bytes 1572864 | tf_op jit(solution)/shard_map/all_to_all | solution.py:415
  77.8 43.0 %copy-start.5 = (f32[2048]{0:T(1024)S(1)}, f32[2048]{0:T(1024)}, u32[]{:S(2)}) copy-start(f32[2048]{0:T(1024)} %param.14) | copy-start | bytes 24580
  77.8 34.3 %collective-permute-start.7 = (bf16[4,128,1024]{2,1,0:T(8,128)(2,1)S(1)}, bf16[4,128,1024]{2,1,0:T(8,128)(2,1)}, u32[]{:S(2)}, u32[]{:S(2)}) collective-permute-start(bf16[4,128,1024]{2,1,0:T(8,128)(2,1)S(1)} %pad_maximum_fusion.refs_0_), channel_id=1, source_target_pairs={{0,64},{32,96},{64,0},{96,32},{1,65},{33,97},{65,1},{97,33},{2,66}... | collective-permute-start | bytes 3145736 | tf_op jit(solution)/shard_map/ppermute | solution.py:30
  92.6 0.9 copy-start.4
  97.8 29.4 %all-to-all-start.4 = ((bf16[8,256,256]{2,1,0:T(8,128)(2,1)}), bf16[8,256,256]{2,1,0:T(8,128)(2,1)S(1)}, u32[]{:S(2)}, u32[]{:S(2)}) async-start(bf16[8,256,256]{2,1,0:T(8,128)(2,1)} %far_levels.1), calls=%async_computation.4 | async-start | bytes 2097152 | tf_op jit(solution)/shard_map/all_to_all | solution.py:419
  112.1 9.2 %collective-permute-start.8 = (bf16[4,128,1024]{2,1,0:T(8,128)(2,1)}, bf16[4,128,1024]{2,1,0:T(8,128)(2,1)}, u32[]{:S(2)}, u32[]{:S(2)}) collective-permute-start(bf16[4,128,1024]{2,1,0:T(8,128)(2,1)} %collective-permute-done.7.refs_4_), channel_id=1, source_target_pairs={{0,1},{1,0},{2,3},{3,2},{4,5},{5,4},{6,7},{7,6},{8,9},{9,8},{10,11... | collective-permute-start | bytes 3145736 | tf_op jit(solution)/shard_map/ppermute | solution.py:30
  114.1 7.2 %collective-permute-start.5 = (bf16[4,128,1024]{2,1,0:T(8,128)(2,1)S(1)}, bf16[4,128,1024]{2,1,0:T(8,128)(2,1)}, u32[]{:S(2)}, u32[]{:S(2)}) collective-permute-start(bf16[4,128,1024]{2,1,0:T(8,128)(2,1)S(1)} %pad_maximum_fusion.refs_0_), channel_id=1, source_target_pairs={{0,1},{1,0},{2,3},{3,2},{4,5},{5,4},{6,7},{7,6},{8,9},{9,8},{10,11... | collective-permute-start | bytes 3145736 | tf_op jit(solution)/shard_map/ppermute | solution.py:30
  116.5 4.9 %collective-permute-start.6 = (bf16[4,128,1024]{2,1,0:T(8,128)(2,1)}, bf16[4,128,1024]{2,1,0:T(8,128)(2,1)}, u32[]{:S(2)}, u32[]{:S(2)}) collective-permute-start(bf16[4,128,1024]{2,1,0:T(8,128)(2,1)} %collective-permute-done.3.refs_2_), channel_id=1, source_target_pairs={{0,1},{1,0},{2,3},{3,2},{4,5},{5,4},{6,7},{7,6},{8,9},{9,8},{10,11... | collective-permute-start | bytes 3145736 | tf_op jit(solution)/shard_map/ppermute | solution.py:30
  118.4 5.0 %collective-permute-start.9 = (bf16[4,128,1024]{2,1,0:T(8,128)(2,1)}, bf16[4,128,1024]{2,1,0:T(8,128)(2,1)}, u32[]{:S(2)}, u32[]{:S(2)}) collective-permute-start(bf16[4,128,1024]{2,1,0:T(8,128)(2,1)} %collective-permute-done.4.refs_6_), channel_id=1, source_target_pairs={{0,1},{1,0},{2,3},{3,2},{4,5},{5,4},{6,7},{7,6},{8,9},{9,8},{10,11... | collective-permute-start | bytes 3145736 | tf_op jit(solution)/shard_map/ppermute | solution.py:30
  127.1 1.6 copy-start.2
  134.2 30.6 %collective-permute-start.10 = (bf16[256,1024]{1,0:T(8,128)(2,1)S(1)}, bf16[256,1024]{1,0:T(8,128)(2,1)S(1)}, u32[]{:S(2)}, u32[]{:S(2)}) collective-permute-start(bf16[256,1024]{1,0:T(8,128)(2,1)S(1)} %get-tuple-element.42), channel_id=1, source_target_pairs={{0,2},{2,0},{1,3},{3,1},{4,6},{6,4},{5,7},{7,5},{8,10},{10,8},{9,1... | collective-permute-start | bytes 1572872 | tf_op jit(solution)/shard_map/ppermute | solution.py:30

commit v8 on v7

--- a/solution.py
+++ b/solution.py
@@ -406,7 +406,7 @@
     acc, silu = local_part(vt, seq_gate, seq_keys, seq_queries, level_weights, skip_gain, head_size)
     planes, acc, silu = lax.optimization_barrier((planes, acc, silu))
     own = jnp.stack([weight, *planes])
-    near, middle, last = [swapped(own, "x", k) for k in range(1, lax.axis_size("x"))]
+    near, last = swapped(own, "x", 1), swapped(own, "x", 3)
     raw, own = lax.optimization_barrier((raw, own))
 
     line = group_sum(raw, rows, lax.axis_size("zl"))
@@ -414,6 +414,7 @@
     plane = column_sums(place, line, lax.axis_size("x"))
     plane = lax.all_to_all(plane, "x", 0, 0, tiled=True)
     plane, own, near, last = lax.optimization_barrier((plane, own, near, last))
+    middle = swapped(own, "x", 2)
     pieces = weight_pieces([own, near, middle, last])
     far = far_levels(place, raw, plane, heads, slot, tok)
     far = lax.all_to_all(far, "y", 0, 0, tiled=True).reshape(width, tok)

time: 167 us -> 171 us (1.024)
  the two profiles are of different devices: /device:TPU:6 before, /device:TPU:2 now
where the time goes in v8:
time: 171 us; the launch traced here: 170 us
  starting transfers between devices  70.1 us (41%)
  waiting for transfers between devices  67.7 us (40%)
  Pallas kernels  26.3 us (15%)
  local copies, waits for them, and re-layouts  3.72 us (2%)
    ppermute x11, starting transfers between devices, swapped(): lax.ppermute(value, axis, [(i, i ^ mask) for i in range(lax.axis_size(axi...  44 us
    ppermute x11, waiting for transfers between devices, swapped(): lax.ppermute(value, axis, [(i, i ^ mask) for i in range(lax.axis_size(axi...  35.2 us
    all_to_all x1, waiting for transfers between devices, on_device(): far = lax.all_to_all(far, 'y', 0, 0, tiled=True).reshape(width, tok)  12.3 us
    all_to_all x1, waiting for transfers between devices, on_device(): line = lax.all_to_all(line, 'zl', 0, 0, tiled=True)  7.74 us
    all_to_all x1, waiting for transfers between devices, shared_along(): return lax.all_to_all(spread, axis, 0, 0, tiled=True)  7.3 us
    all_to_all x1, starting transfers between devices, shared_along(): return lax.all_to_all(spread, axis, 0, 0, tiled=True)  7.1 us
    all_to_all x1, starting transfers between devices, on_device(): far = lax.all_to_all(far, 'y', 0, 0, tiled=True).reshape(width, tok)  6.82 us
    pallas_call x1, Pallas kernels, local_part(): pl.pallas_call(functools.partial(local_kernel, heads, tok // 2), grid=(st...  6.22 us
  transfers between devices with their start and end apart: 16, of which 8 were waited for; matrix products, arithmetic and copies ran while one was open for 1% of the time, Pallas kernels for 12%

profile of v8, /device:TPU:2, one launch (start us, length us, event | category | flops | bytes accessed | tf_op | source)
XLA Modules:
  0.0 169.6 jit_solution(4243850216785634984)
XLA Ops:
  1.6 7.1 %all-to-all-start = ((bf16[8,16,1024]{2,1,0:T(8,128)(2,1)}), bf16[8,16,1024]{2,1,0:T(8,128)(2,1)S(1)}, u32[]{:S(2)}, u32[]{:S(2)}) async-start(bf16[8,16,1024]{2,1,0:T(8,128)(2,1)} %broadcast_in_dim.4), calls=%async_computation | async-start | bytes 524288 | tf_op jit(solution)/shard_map/all_to_all | solution.py:364
  9.3 4.0 %to_group.1 = (bf16[2048,256]{1,0:T(8,128)(2,1)}, bf16[8,576,128]{2,1,0:T(8,128)(2,1)}) custom-call(f32[7]{0:T(128)} %convert_element_type.9.upper_ref, bf16[256,2048]{1,0:T(8,128)(2,1)} %values_ref.1, bf16[256,128]{1,0:T(8,128)(2,1)} %keys_ref.3, bf16[256,128]{1,0:T(8,128)(2,1)} %query_ref.3, bf16[16,32,256]{2,1,0:T(8,128)(2,1)} %w_ref.3), custom_call_target="tpu_custom_call" | custom-call | flops 134217728 | bytes 2097152 | tf_op jit(solution)/shard_map/to_group/pallas_call | solution.py:66
  13.3 7.3 %all-to-all-done = bf16[8,16,1024]{2,1,0:T(8,128)(2,1)S(1)} async-done(((bf16[8,16,1024]{2,1,0:T(8,128)(2,1)}), bf16[8,16,1024]{2,1,0:T(8,128)(2,1)S(1)}, u32[]{:S(2)}, u32[]{:S(2)}) %all-to-all-start) | async-done | bytes 262176 | tf_op jit(solution)/shard_map/all_to_all | solution.py:364
  20.6 3.6 %all-to-all-start.1 = ((bf16[8,576,128]{2,1,0:T(8,128)(2,1)}), bf16[8,576,128]{2,1,0:T(8,128)(2,1)S(1)}, u32[]{:S(2)}, u32[]{:S(2)}) async-start(bf16[8,576,128]{2,1,0:T(8,128)(2,1)} %get-tuple-element.25), calls=%async_computation.1 | async-start | bytes 2359296 | tf_op jit(solution)/shard_map/all_to_all | solution.py:404
  24.1 7.9 %collective-permute-start.2 = (bf16[128,1024]{1,0:T(8,128)(2,1)S(1)}, bf16[128,1024]{1,0:T(8,128)(2,1)S(1)}, u32[]{:S(2)}, u32[]{:S(2)}) collective-permute-start(bf16[128,1024]{1,0:T(8,128)(2,1)S(1)} %bitcast.22), channel_id=1, source_target_pairs={{0,384},{128,256},{256,128},{384,0},{1,385},{129,257},{257,129},{3... | collective-permute-start | bytes 786440 | tf_op jit(solution)/shard_map/ppermute | solution.py:30
  34.0 2.5 %collective-permute-start = (bf16[128,1024]{1,0:T(8,128)(2,1)S(1)}, bf16[128,1024]{1,0:T(8,128)(2,1)S(1)}, u32[]{:S(2)}, u32[]{:S(2)}) collective-permute-start(bf16[128,1024]{1,0:T(8,128)(2,1)S(1)} %bitcast.24), channel_id=1, source_target_pairs={{0,128},{128,0},{256,384},{384,256},{1,129},{129,1},{257,385},{385... | collective-permute-start | bytes 786440 | tf_op jit(solution)/shard_map/ppermute | solution.py:30
  36.4 6.2 %local_part.1 = (f32[2048,256]{1,0:T(8,128)}, f32[2048,256]{1,0:T(8,128)}) custom-call(f32[32]{0:T(128)} %skip_ref.1, bf16[2048,256]{1,0:T(8,128)(2,1)} %get-tuple-element.27.vt_ref, bf16[256,2048]{1,0:T(8,128)(2,1)} %gate_ref.1, bf16[256,128]{1,0:T(8,128)(2,1)} %keys_ref.3, bf16[256,128]{1,0:T(8,128)(2,1)} %query_ref.3, bf16[16,32,256]{2,1,0:T(8,128)(2,1)} %w_ref.3), custom_call_target="tpu_custom_call" | custom-call | flops 1073741824 | bytes 6291456 | tf_op jit(solution)/shard_map/local_part/pallas_call | solution.py:140
  42.7 8.9 %collective-permute-done.1 = bf16[128,1024]{1,0:T(8,128)(2,1)S(1)} collective-permute-done((bf16[128,1024]{1,0:T(8,128)(2,1)S(1)}, bf16[128,1024]{1,0:T(8,128)(2,1)S(1)}, u32[]{:S(2)}, u32[]{:S(2)}) %collective-permute-start.1) | collective-permute-done | bytes 262176 | tf_op jit(solution)/shard_map/ppermute | solution.py:30
  51.7 3.4 %collective-permute-start.4 = (bf16[4,128,1024]{2,1,0:T(8,128)(2,1)S(1)}, bf16[4,128,1024]{2,1,0:T(8,128)(2,1)}, u32[]{:S(2)}, u32[]{:S(2)}) collective-permute-start(bf16[4,128,1024]{2,1,0:T(8,128)(2,1)S(1)} %pad_maximum_fusion.refs_0_), channel_id=1, source_target_pairs={{0,96},{32,64},{64,32},{96,0},{1,97},{33,65},{65,33},{97,1},{2,98}... | collective-permute-start | bytes 3145736 | tf_op jit(solution)/shard_map/ppermute | solution.py:30
  55.1 3.7 %collective-permute-start.3 = (bf16[4,128,1024]{2,1,0:T(8,128)(2,1)S(1)}, bf16[4,128,1024]{2,1,0:T(8,128)(2,1)}, u32[]{:S(2)}, u32[]{:S(2)}) collective-permute-start(bf16[4,128,1024]{2,1,0:T(8,128)(2,1)S(1)} %pad_maximum_fusion.refs_0_), channel_id=1, source_target_pairs={{0,32},{32,0},{64,96},{96,64},{1,33},{33,1},{65,97},{97,65},{2,34}... | collective-permute-start | bytes 3145736 | tf_op jit(solution)/shard_map/ppermute | solution.py:30
  59.9 3.9 %all-to-all-start.2 = ((bf16[4,256,128]{2,1,0:T(8,128)(2,1)}), bf16[4,256,128]{2,1,0:T(8,128)(2,1)S(1)}, u32[]{:S(2)}, u32[]{:S(2)}) async-start(bf16[4,256,128]{2,1,0:T(8,128)(2,1)} %group_sum.1), calls=%async_computation.2 | async-start | bytes 524288 | tf_op jit(solution)/shard_map/all_to_all | solution.py:413
  63.9 7.7 %all-to-all-done.2.line_ref = bf16[4,256,128]{2,1,0:T(8,128)(2,1)S(1)} async-done(((bf16[4,256,128]{2,1,0:T(8,128)(2,1)}), bf16[4,256,128]{2,1,0:T(8,128)(2,1)S(1)}, u32[]{:S(2)}, u32[]{:S(2)}) %all-to-all-start.2) | async-done | bytes 262176 | tf_op jit(solution)/shard_map/all_to_all | solution.py:413
  73.2 4.7 %all-to-all-start.3 = ((bf16[4,3,256,128]{3,2,1,0:T(8,128)(2,1)}), bf16[4,3,256,128]{3,2,1,0:T(8,128)(2,1)S(1)}, u32[]{:S(2)}, u32[]{:S(2)}) async-start(bf16[4,3,256,128]{3,2,1,0:T(8,128)(2,1)} %column_sums.1), calls=%async_computation.3 | async-start | bytes 1572864 | tf_op jit(solution)/shard_map/all_to_all | solution.py:415
  77.8 5.4 %collective-permute-done.3.refs_2_ = bf16[4,128,1024]{2,1,0:T(8,128)(2,1)} collective-permute-done((bf16[4,128,1024]{2,1,0:T(8,128)(2,1)S(1)}, bf16[4,128,1024]{2,1,0:T(8,128)(2,1)}, u32[]{:S(2)}, u32[]{:S(2)}) %collective-permute-start.3) | collective-permute-done | bytes 1048608 | tf_op jit(solution)/shard_map/ppermute | solution.py:30
  83.2 5.1 %all-to-all-done.3.plane_ref = bf16[4,3,256,128]{3,2,1,0:T(8,128)(2,1)S(1)} async-done(((bf16[4,3,256,128]{3,2,1,0:T(8,128)(2,1)}), bf16[4,3,256,128]{3,2,1,0:T(8,128)(2,1)S(1)}, u32[]{:S(2)}, u32[]{:S(2)}) %all-to-all-start.3) | async-done | bytes 786464 | tf_op jit(solution)/shard_map/all_to_all | solution.py:415
  88.3 5.2 %collective-permute-start.7 = (bf16[4,128,1024]{2,1,0:T(8,128)(2,1)S(1)}, bf16[4,128,1024]{2,1,0:T(8,128)(2,1)}, u32[]{:S(2)}, u32[]{:S(2)}) collective-permute-start(bf16[4,128,1024]{2,1,0:T(8,128)(2,1)S(1)} %pad_maximum_fusion.refs_0_), channel_id=1, source_target_pairs={{0,64},{32,96},{64,0},{96,32},{1,65},{33,97},{65,1},{97,33},{2,66}... | collective-permute-start | bytes 3145736 | tf_op jit(solution)/shard_map/ppermute | solution.py:30
  93.6 4.2 %far_levels.1 = bf16[8,256,256]{2,1,0:T(8,128)(2,1)} custom-call(s32[2]{0:T(128)} %copy-done.3, bf16[8,576,128]{2,1,0:T(8,128)(2,1)} %copy-done.1, bf16[4,3,256,128]{3,2,1,0:T(8,128)(2,1)} %copy-done.4), custom_call_target="tpu_custom_call" | custom-call | flops 805306368 | bytes 4194304 | tf_op jit(solution)/shard_map/far_levels/pallas_call | solution.py:259
  97.8 6.8 %all-to-all-start.4 = ((bf16[8,256,256]{2,1,0:T(8,128)(2,1)}), bf16[8,256,256]{2,1,0:T(8,128)(2,1)S(1)}, u32[]{:S(2)}, u32[]{:S(2)}) async-start(bf16[8,256,256]{2,1,0:T(8,128)(2,1)} %far_levels.1), calls=%async_computation.4 | async-start | bytes 2097152 | tf_op jit(solution)/shard_map/all_to_all | solution.py:420
  110.9 4.3 %collective-permute-done.7.refs_4_ = bf16[4,128,1024]{2,1,0:T(8,128)(2,1)} collective-permute-done((bf16[4,128,1024]{2,1,0:T(8,128)(2,1)S(1)}, bf16[4,128,1024]{2,1,0:T(8,128)(2,1)}, u32[]{:S(2)}, u32[]{:S(2)}) %collective-permute-start.7) | collective-permute-done | bytes 1048608 | tf_op jit(solution)/shard_map/ppermute | solution.py:30
  117.6 12.3 %all-to-all-done.4 = bf16[8,256,256]{2,1,0:T(8,128)(2,1)S(1)} async-done(((bf16[8,256,256]{2,1,0:T(8,128)(2,1)}), bf16[8,256,256]{2,1,0:T(8,128)(2,1)S(1)}, u32[]{:S(2)}, u32[]{:S(2)}) %all-to-all-start.4) | async-done | bytes 1048608 | tf_op jit(solution)/shard_map/all_to_all | solution.py:420
  131.5 5.4 %finish.1 = (bf16[256,1024]{1,0:T(8,128)(2,1)S(1)}, bf16[2,1024,256]{2,1,0:T(8,128)(2,1)S(1)}) custom-call(s32[5]{0:T(128)S(1)} %stack.67.where_ref, bf16[4,128,1024]{2,1,0:T(8,128)(2,1)S(1)} %pad_maximum_fusion.refs_0_, bf16[4,128,1024]{2,1,0:T(8,128)(2,1)} %collective-permute-done.5.refs_1_, bf16[4,128,1024]{2,1,0:T(8,128)(2,1)} %collective-permute-done.3.refs_2_, ...), custom_call_target="tpu_custom_call" | custom-call | flops 1073741824 | bytes 16777216 | tf_op jit(solution)/shard_map/finish/pallas_call | solution.py:320
  137.0 11.2 %collective-permute-start.10 = (bf16[256,1024]{1,0:T(8,128)(2,1)S(1)}, bf16[256,1024]{1,0:T(8,128)(2,1)S(1)}, u32[]{:S(2)}, u32[]{:S(2)}) collective-permute-start(bf16[256,1024]{1,0:T(8,128)(2,1)S(1)} %get-tuple-element.42), channel_id=1, source_target_pairs={{0,2},{2,0},{1,3},{3,1},{4,6},{6,4},{5,7},{7,5},{8,10},{10,8},{9,1... | collective-permute-start | bytes 1572872 | tf_op jit(solution)/shard_map/ppermute | solution.py:30
  148.2 3.9 %keep.1 = f32[256,1024]{1,0:T(8,128)S(1)} custom-call(s32[5]{0:T(128)S(1)} %stack.67.where_ref, bf16[4,128,1024]{2,1,0:T(8,128)(2,1)S(1)} %pad_maximum_fusion.refs_0_, bf16[4,128,1024]{2,1,0:T(8,128)(2,1)} %collective-permute-done.5.refs_1_, bf16[4,128,1024]{2,1,0:T(8,128)(2,1)} %collective-permute-done.3.refs_2_, ...), custom_call_target="tpu_custom_call" | custom-call | flops 1073741824 | bytes 8388608 | tf_op jit(solution)/shard_map/keep/pallas_call | solution.py:346
  152.1 16.5 %collective-permute-done.10 = bf16[256,1024]{1,0:T(8,128)(2,1)S(1)} collective-permute-done((bf16[256,1024]{1,0:T(8,128)(2,1)S(1)}, bf16[256,1024]{1,0:T(8,128)(2,1)S(1)}, u32[]{:S(2)}, u32[]{:S(2)}) %collective-permute-start.10) | collective-permute-done | bytes 524320 | tf_op jit(solution)/shard_map/ppermute | solution.py:30
  (36 shorter events, 18.0 us)
Async XLA Ops:
  0.0 0.8 copy-start
  1.6 19.0 %all-to-all-start = ((bf16[8,16,1024]{2,1,0:T(8,128)(2,1)}), bf16[8,16,1024]{2,1,0:T(8,128)(2,1)S(1)}, u32[]{:S(2)}, u32[]{:S(2)}) async-start(bf16[8,16,1024]{2,1,0:T(8,128)(2,1)} %broadcast_in_dim.4), calls=%async_computation | async-start | bytes 524288 | tf_op jit(solution)/shard_map/all_to_all | solution.py:364
  20.6 38.3 %all-to-all-start.1 = ((bf16[8,576,128]{2,1,0:T(8,128)(2,1)}), bf16[8,576,128]{2,1,0:T(8,128)(2,1)S(1)}, u32[]{:S(2)}, u32[]{:S(2)}) async-start(bf16[8,576,128]{2,1,0:T(8,128)(2,1)} %get-tuple-element.25), calls=%async_computation.1 | async-start | bytes 2359296 | tf_op jit(solution)/shard_map/all_to_all | solution.py:404
  24.1 18.5 %collective-permute-start.2 = (bf16[128,1024]{1,0:T(8,128)(2,1)S(1)}, bf16[128,1024]{1,0:T(8,128)(2,1)S(1)}, u32[]{:S(2)}, u32[]{:S(2)}) collective-permute-start(bf16[128,1024]{1,0:T(8,128)(2,1)S(1)} %bitcast.22), channel_id=1, source_target_pairs={{0,384},{128,256},{256,128},{384,0},{1,385},{129,257},{257,129},{3... | collective-permute-start | bytes 786440 | tf_op jit(solution)/shard_map/ppermute | solution.py:30
  32.0 19.5 %collective-permute-start.1 = (bf16[128,1024]{1,0:T(8,128)(2,1)S(1)}, bf16[128,1024]{1,0:T(8,128)(2,1)S(1)}, u32[]{:S(2)}, u32[]{:S(2)}) collective-permute-start(bf16[128,1024]{1,0:T(8,128)(2,1)S(1)} %bitcast.23), channel_id=1, source_target_pairs={{0,256},{128,384},{256,0},{384,128},{1,257},{129,385},{257,1},{385... | collective-permute-start | bytes 786440 | tf_op jit(solution)/shard_map/ppermute | solution.py:30
  34.0 17.6 %collective-permute-start = (bf16[128,1024]{1,0:T(8,128)(2,1)S(1)}, bf16[128,1024]{1,0:T(8,128)(2,1)S(1)}, u32[]{:S(2)}, u32[]{:S(2)}) collective-permute-start(bf16[128,1024]{1,0:T(8,128)(2,1)S(1)} %bitcast.24), channel_id=1, source_target_pairs={{0,128},{128,0},{256,384},{384,256},{1,129},{129,1},{257,385},{385... | collective-permute-start | bytes 786440 | tf_op jit(solution)/shard_map/ppermute | solution.py:30
  51.7 26.1 %collective-permute-start.4 = (bf16[4,128,1024]{2,1,0:T(8,128)(2,1)S(1)}, bf16[4,128,1024]{2,1,0:T(8,128)(2,1)}, u32[]{:S(2)}, u32[]{:S(2)}) collective-permute-start(bf16[4,128,1024]{2,1,0:T(8,128)(2,1)S(1)} %pad_maximum_fusion.refs_0_), channel_id=1, source_target_pairs={{0,96},{32,64},{64,32},{96,0},{1,97},{33,65},{65,33},{97,1},{2,98}... | collective-permute-start | bytes 3145736 | tf_op jit(solution)/shard_map/ppermute | solution.py:30
  55.1 28.1 %collective-permute-start.3 = (bf16[4,128,1024]{2,1,0:T(8,128)(2,1)S(1)}, bf16[4,128,1024]{2,1,0:T(8,128)(2,1)}, u32[]{:S(2)}, u32[]{:S(2)}) collective-permute-start(bf16[4,128,1024]{2,1,0:T(8,128)(2,1)S(1)} %pad_maximum_fusion.refs_0_), channel_id=1, source_target_pairs={{0,32},{32,0},{64,96},{96,64},{1,33},{33,1},{65,97},{97,65},{2,34}... | collective-permute-start | bytes 3145736 | tf_op jit(solution)/shard_map/ppermute | solution.py:30
  58.9 14.3 %copy-start.1 = (bf16[8,576,128]{2,1,0:T(8,128)(2,1)}, bf16[8,576,128]{2,1,0:T(8,128)(2,1)S(1)}, u32[]{:S(2)}) copy-start(bf16[8,576,128]{2,1,0:T(8,128)(2,1)S(1)} %all-to-all-done.1.got_ref) | copy-start | bytes 3538948
  59.9 11.7 %all-to-all-start.2 = ((bf16[4,256,128]{2,1,0:T(8,128)(2,1)}), bf16[4,256,128]{2,1,0:T(8,128)(2,1)S(1)}, u32[]{:S(2)}, u32[]{:S(2)}) async-start(bf16[4,256,128]{2,1,0:T(8,128)(2,1)} %group_sum.1), calls=%async_computation.2 | async-start | bytes 524288 | tf_op jit(solution)/shard_map/all_to_all | solution.py:413
  63.9 29.7 %copy-start.3 = (s32[2]{0:T(128)}, s32[2]{0:T(128)S(1)}, u32[]{:S(2)}) copy-start(s32[2]{0:T(128)S(1)} %pad_add_fusion.where_ref) | copy-start | bytes 28
  73.2 15.2 %all-to-all-start.3 = ((bf16[4,3,256,128]{3,2,1,0:T(8,128)(2,1)}), bf16[4,3,256,128]{3,2,1,0:T(8,128)(2,1)S(1)}, u32[]{:S(2)}, u32[]{:S(2)}) async-start(bf16[4,3,256,128]{3,2,1,0:T(8,128)(2,1)} %column_sums.1), calls=%async_computation.3 | async-start | bytes 1572864 | tf_op jit(solution)/shard_map/all_to_all | solution.py:415
  77.8 39.3 %copy-start.5 = (f32[2048]{0:T(1024)S(1)}, f32[2048]{0:T(1024)}, u32[]{:S(2)}) copy-start(f32[2048]{0:T(1024)} %param.14) | copy-start | bytes 24580
  88.3 5.3 %copy-start.4 = (bf16[4,3,256,128]{3,2,1,0:T(8,128)(2,1)}, bf16[4,3,256,128]{3,2,1,0:T(8,128)(2,1)S(1)}, u32[]{:S(2)}) copy-start(bf16[4,3,256,128]{3,2,1,0:T(8,128)(2,1)S(1)} %all-to-all-done.3.plane_ref) | copy-start | bytes 2359300
  88.3 26.9 %collective-permute-start.7 = (bf16[4,128,1024]{2,1,0:T(8,128)(2,1)S(1)}, bf16[4,128,1024]{2,1,0:T(8,128)(2,1)}, u32[]{:S(2)}, u32[]{:S(2)}) collective-permute-start(bf16[4,128,1024]{2,1,0:T(8,128)(2,1)S(1)} %pad_maximum_fusion.refs_0_), channel_id=1, source_target_pairs={{0,64},{32,96},{64,0},{96,32},{1,65},{33,97},{65,1},{97,33},{2,66}... | collective-permute-start | bytes 3145736 | tf_op jit(solution)/shard_map/ppermute | solution.py:30
  97.8 32.1 %all-to-all-start.4 = ((bf16[8,256,256]{2,1,0:T(8,128)(2,1)}), bf16[8,256,256]{2,1,0:T(8,128)(2,1)S(1)}, u32[]{:S(2)}, u32[]{:S(2)}) async-start(bf16[8,256,256]{2,1,0:T(8,128)(2,1)} %far_levels.1), calls=%async_computation.4 | async-start | bytes 2097152 | tf_op jit(solution)/shard_map/all_to_all | solution.py:420
  104.6 13.0 %collective-permute-start.6 = (bf16[4,128,1024]{2,1,0:T(8,128)(2,1)}, bf16[4,128,1024]{2,1,0:T(8,128)(2,1)}, u32[]{:S(2)}, u32[]{:S(2)}) collective-permute-start(bf16[4,128,1024]{2,1,0:T(8,128)(2,1)} %collective-permute-done.3.refs_2_), channel_id=1, source_target_pairs={{0,1},{1,0},{2,3},{3,2},{4,5},{5,4},{6,7},{7,6},{8,9},{9,8},{10,11... | collective-permute-start | bytes 3145736 | tf_op jit(solution)/shard_map/ppermute | solution.py:30
  106.6 11.1 %collective-permute-start.9 = (bf16[4,128,1024]{2,1,0:T(8,128)(2,1)}, bf16[4,128,1024]{2,1,0:T(8,128)(2,1)}, u32[]{:S(2)}, u32[]{:S(2)}) collective-permute-start(bf16[4,128,1024]{2,1,0:T(8,128)(2,1)} %collective-permute-done.4.refs_6_), channel_id=1, source_target_pairs={{0,1},{1,0},{2,3},{3,2},{4,5},{5,4},{6,7},{7,6},{8,9},{9,8},{10,11... | collective-permute-start | bytes 3145736 | tf_op jit(solution)/shard_map/ppermute | solution.py:30
  109.0 8.7 %collective-permute-start.5 = (bf16[4,128,1024]{2,1,0:T(8,128)(2,1)S(1)}, bf16[4,128,1024]{2,1,0:T(8,128)(2,1)}, u32[]{:S(2)}, u32[]{:S(2)}) collective-permute-start(bf16[4,128,1024]{2,1,0:T(8,128)(2,1)S(1)} %pad_maximum_fusion.refs_0_), channel_id=1, source_target_pairs={{0,1},{1,0},{2,3},{3,2},{4,5},{5,4},{6,7},{7,6},{8,9},{9,8},{10,11... | collective-permute-start | bytes 3145736 | tf_op jit(solution)/shard_map/ppermute | solution.py:30
  115.2 14.7 %collective-permute-start.8 = (bf16[4,128,1024]{2,1,0:T(8,128)(2,1)}, bf16[4,128,1024]{2,1,0:T(8,128)(2,1)}, u32[]{:S(2)}, u32[]{:S(2)}) collective-permute-start(bf16[4,128,1024]{2,1,0:T(8,128)(2,1)} %collective-permute-done.7.refs_4_), channel_id=1, source_target_pairs={{0,1},{1,0},{2,3},{3,2},{4,5},{5,4},{6,7},{7,6},{8,9},{9,8},{10,11... | collective-permute-start | bytes 3145736 | tf_op jit(solution)/shard_map/ppermute | solution.py:30
  129.9 1.6 copy-start.2
  137.0 31.7 %collective-permute-start.10 = (bf16[256,1024]{1,0:T(8,128)(2,1)S(1)}, bf16[256,1024]{1,0:T(8,128)(2,1)S(1)}, u32[]{:S(2)}, u32[]{:S(2)}) collective-permute-start(bf16[256,1024]{1,0:T(8,128)(2,1)S(1)} %get-tuple-element.42), channel_id=1, source_target_pairs={{0,2},{2,0},{1,3},{3,1},{4,6},{6,4},{5,7},{7,5},{8,10},{10,8},{9,1... | collective-permute-start | bytes 1572872 | tf_op jit(solution)/shard_map/ppermute | solution.py:30

commit v9 on v7

--- a/solution.py
+++ b/solution.py
@@ -261,7 +261,7 @@
         in_specs=[pl.BlockSpec(memory_space=pltpu.SMEM), vmem, vmem],
         out_specs=vmem,
         out_shape=jax.ShapeDtypeStruct((group, rows, tok), bf16),
-        compiler_params=pltpu.CompilerParams(vmem_limit_bytes=VMEM_MIB * 2**20),
+        compiler_params=pltpu.CompilerParams(vmem_limit_bytes=48 * 2**20),
         cost_estimate=cost(12 * group * rows * tok * 128, 8 * group * rows * tok),
         name="far_levels",
     )(where, got, plane)

time: 167 us -> 167 us (level)
  the two profiles are of different devices: /device:TPU:6 before, /device:TPU:14 now
where the time goes in v9:
time: 167 us; the launch traced here: 166 us
  starting transfers between devices  70 us (42%)
  waiting for transfers between devices  64.9 us (39%)
  Pallas kernels  24.3 us (15%)
  local copies, waits for them, and re-layouts  4.63 us (3%)
  other arithmetic  1.69 us (1%)
    ppermute x11, waiting for transfers between devices, swapped(): lax.ppermute(value, axis, [(i, i ^ mask) for i in range(lax.axis_size(axi...  41.1 us
    ppermute x11, starting transfers between devices, swapped(): lax.ppermute(value, axis, [(i, i ^ mask) for i in range(lax.axis_size(axi...  40.8 us
    all_to_all x1, waiting for transfers between devices, on_device(): plane = lax.all_to_all(plane, 'x', 0, 0, tiled=True)  10.5 us
    all_to_all x1, starting transfers between devices, shared_along(): return lax.all_to_all(spread, axis, 0, 0, tiled=True)  7.55 us
    all_to_all x1, starting transfers between devices, on_device(): far = lax.all_to_all(far, 'y', 0, 0, tiled=True).reshape(width, tok)  7.23 us
    all_to_all x1, waiting for transfers between devices, on_device(): line = lax.all_to_all(line, 'zl', 0, 0, tiled=True)  6.7 us
    pallas_call x1, Pallas kernels, local_part(): pl.pallas_call(functools.partial(local_kernel, heads, tok // 2), grid=(st...  6.23 us
    all_to_all x1, waiting for transfers between devices, shared_along(): return lax.all_to_all(spread, axis, 0, 0, tiled=True)  5.8 us
  transfers between devices with their start and end apart: 16, of which 11 were waited for; matrix products, arithmetic and copies ran while one was open for 1% of the time, Pallas kernels for 11%

profile of v9, /device:TPU:14, one launch (start us, length us, event | category | flops | bytes accessed | tf_op | source)
XLA Modules:
  0.0 165.6 jit_solution(5205090323244417272)
XLA Ops:
  1.6 7.5 %all-to-all-start = ((bf16[8,16,1024]{2,1,0:T(8,128)(2,1)}), bf16[8,16,1024]{2,1,0:T(8,128)(2,1)S(1)}, u32[]{:S(2)}, u32[]{:S(2)}) async-start(bf16[8,16,1024]{2,1,0:T(8,128)(2,1)} %broadcast_in_dim.4), calls=%async_computation | async-start | bytes 524288 | tf_op jit(solution)/shard_map/all_to_all | solution.py:364
  9.8 4.0 %to_group.1 = (bf16[2048,256]{1,0:T(8,128)(2,1)}, bf16[8,576,128]{2,1,0:T(8,128)(2,1)}) custom-call(f32[7]{0:T(128)} %convert_element_type.9.upper_ref, bf16[256,2048]{1,0:T(8,128)(2,1)} %values_ref.1, bf16[256,128]{1,0:T(8,128)(2,1)} %keys_ref.3, bf16[256,128]{1,0:T(8,128)(2,1)} %query_ref.3, bf16[16,32,256]{2,1,0:T(8,128)(2,1)} %w_ref.3), custom_call_target="tpu_custom_call" | custom-call | flops 134217728 | bytes 2097152 | tf_op jit(solution)/shard_map/to_group/pallas_call | solution.py:66
  13.7 5.8 %all-to-all-done = bf16[8,16,1024]{2,1,0:T(8,128)(2,1)S(1)} async-done(((bf16[8,16,1024]{2,1,0:T(8,128)(2,1)}), bf16[8,16,1024]{2,1,0:T(8,128)(2,1)S(1)}, u32[]{:S(2)}, u32[]{:S(2)}) %all-to-all-start) | async-done | bytes 262176 | tf_op jit(solution)/shard_map/all_to_all | solution.py:364
  19.5 4.9 %all-to-all-start.1 = ((bf16[8,576,128]{2,1,0:T(8,128)(2,1)}), bf16[8,576,128]{2,1,0:T(8,128)(2,1)S(1)}, u32[]{:S(2)}, u32[]{:S(2)}) async-start(bf16[8,576,128]{2,1,0:T(8,128)(2,1)} %get-tuple-element.25), calls=%async_computation.1 | async-start | bytes 2359296 | tf_op jit(solution)/shard_map/all_to_all | solution.py:404
  24.5 7.9 %collective-permute-start.2 = (bf16[128,1024]{1,0:T(8,128)(2,1)S(1)}, bf16[128,1024]{1,0:T(8,128)(2,1)S(1)}, u32[]{:S(2)}, u32[]{:S(2)}) collective-permute-start(bf16[128,1024]{1,0:T(8,128)(2,1)S(1)} %bitcast.22), channel_id=1, source_target_pairs={{0,384},{128,256},{256,128},{384,0},{1,385},{129,257},{257,129},{3... | collective-permute-start | bytes 786440 | tf_op jit(solution)/shard_map/ppermute | solution.py:30
  34.3 2.5 %collective-permute-start = (bf16[128,1024]{1,0:T(8,128)(2,1)S(1)}, bf16[128,1024]{1,0:T(8,128)(2,1)S(1)}, u32[]{:S(2)}, u32[]{:S(2)}) collective-permute-start(bf16[128,1024]{1,0:T(8,128)(2,1)S(1)} %bitcast.24), channel_id=1, source_target_pairs={{0,128},{128,0},{256,384},{384,256},{1,129},{129,1},{257,385},{385... | collective-permute-start | bytes 786440 | tf_op jit(solution)/shard_map/ppermute | solution.py:30
  36.8 6.2 %local_part.1 = (f32[2048,256]{1,0:T(8,128)}, f32[2048,256]{1,0:T(8,128)}) custom-call(f32[32]{0:T(128)} %skip_ref.1, bf16[2048,256]{1,0:T(8,128)(2,1)} %get-tuple-element.27.vt_ref, bf16[256,2048]{1,0:T(8,128)(2,1)} %gate_ref.1, bf16[256,128]{1,0:T(8,128)(2,1)} %keys_ref.3, bf16[256,128]{1,0:T(8,128)(2,1)} %query_ref.3, bf16[16,32,256]{2,1,0:T(8,128)(2,1)} %w_ref.3), custom_call_target="tpu_custom_call" | custom-call | flops 1073741824 | bytes 6291456 | tf_op jit(solution)/shard_map/local_part/pallas_call | solution.py:140
  43.0 8.6 %collective-permute-done.1 = bf16[128,1024]{1,0:T(8,128)(2,1)S(1)} collective-permute-done((bf16[128,1024]{1,0:T(8,128)(2,1)S(1)}, bf16[128,1024]{1,0:T(8,128)(2,1)S(1)}, u32[]{:S(2)}, u32[]{:S(2)}) %collective-permute-start.1) | collective-permute-done | bytes 262176 | tf_op jit(solution)/shard_map/ppermute | solution.py:30
  51.8 2.4 %collective-permute-start.4 = (bf16[4,128,1024]{2,1,0:T(8,128)(2,1)S(1)}, bf16[4,128,1024]{2,1,0:T(8,128)(2,1)}, u32[]{:S(2)}, u32[]{:S(2)}) collective-permute-start(bf16[4,128,1024]{2,1,0:T(8,128)(2,1)S(1)} %pad_maximum_fusion.refs_0_), channel_id=1, source_target_pairs={{0,96},{32,64},{64,32},{96,0},{1,97},{33,65},{65,33},{97,1},{2,98}... | collective-permute-start | bytes 3145736 | tf_op jit(solution)/shard_map/ppermute | solution.py:30
  54.2 2.8 %collective-permute-start.3 = (bf16[4,128,1024]{2,1,0:T(8,128)(2,1)S(1)}, bf16[4,128,1024]{2,1,0:T(8,128)(2,1)}, u32[]{:S(2)}, u32[]{:S(2)}) collective-permute-start(bf16[4,128,1024]{2,1,0:T(8,128)(2,1)S(1)} %pad_maximum_fusion.refs_0_), channel_id=1, source_target_pairs={{0,32},{32,0},{64,96},{96,64},{1,33},{33,1},{65,97},{97,65},{2,34}... | collective-permute-start | bytes 3145736 | tf_op jit(solution)/shard_map/ppermute | solution.py:30
  57.8 3.9 %all-to-all-start.2 = ((bf16[4,256,128]{2,1,0:T(8,128)(2,1)}), bf16[4,256,128]{2,1,0:T(8,128)(2,1)S(1)}, u32[]{:S(2)}, u32[]{:S(2)}) async-start(bf16[4,256,128]{2,1,0:T(8,128)(2,1)} %group_sum.1), calls=%async_computation.2 | async-start | bytes 524288 | tf_op jit(solution)/shard_map/all_to_all | solution.py:413
  61.8 6.7 %all-to-all-done.2.line_ref = bf16[4,256,128]{2,1,0:T(8,128)(2,1)S(1)} async-done(((bf16[4,256,128]{2,1,0:T(8,128)(2,1)}), bf16[4,256,128]{2,1,0:T(8,128)(2,1)S(1)}, u32[]{:S(2)}, u32[]{:S(2)}) %all-to-all-start.2) | async-done | bytes 262176 | tf_op jit(solution)/shard_map/all_to_all | solution.py:413
  70.1 5.6 %all-to-all-start.3 = ((bf16[4,3,256,128]{3,2,1,0:T(8,128)(2,1)}), bf16[4,3,256,128]{3,2,1,0:T(8,128)(2,1)S(1)}, u32[]{:S(2)}, u32[]{:S(2)}) async-start(bf16[4,3,256,128]{3,2,1,0:T(8,128)(2,1)} %copy-done.1), calls=%async_computation.3 | async-start | bytes 1572864 | tf_op jit(solution)/shard_map/all_to_all | solution.py:415
  75.6 3.5 %collective-permute-start.7 = (bf16[4,128,1024]{2,1,0:T(8,128)(2,1)S(1)}, bf16[4,128,1024]{2,1,0:T(8,128)(2,1)}, u32[]{:S(2)}, u32[]{:S(2)}) collective-permute-start(bf16[4,128,1024]{2,1,0:T(8,128)(2,1)S(1)} %pad_maximum_fusion.refs_0_), channel_id=1, source_target_pairs={{0,64},{32,96},{64,0},{96,32},{1,65},{33,97},{65,1},{97,33},{2,66}... | collective-permute-start | bytes 3145736 | tf_op jit(solution)/shard_map/ppermute | solution.py:30
  82.3 10.5 %all-to-all-done.3.plane_ref = bf16[4,3,256,128]{3,2,1,0:T(8,128)(2,1)S(1)} async-done(((bf16[4,3,256,128]{3,2,1,0:T(8,128)(2,1)}), bf16[4,3,256,128]{3,2,1,0:T(8,128)(2,1)S(1)}, u32[]{:S(2)}, u32[]{:S(2)}) %all-to-all-start.3) | async-done | bytes 786464 | tf_op jit(solution)/shard_map/all_to_all | solution.py:415
  92.8 3.2 %far_levels.1 = bf16[8,256,256]{2,1,0:T(8,128)(2,1)} custom-call(s32[2]{0:T(128)S(1)} %pad_add_fusion.where_ref, bf16[8,576,128]{2,1,0:T(8,128)(2,1)S(1)} %all-to-all-done.1.got_ref, bf16[4,3,256,128]{3,2,1,0:T(8,128)(2,1)S(1)} %all-to-all-done.3.plane_ref), custom_call_target="tpu_custom_call" | custom-call | flops 805306368 | bytes 4194304 | tf_op jit(solution)/shard_map/far_levels/pallas_call | solution.py:259
  96.0 7.2 %all-to-all-start.4 = ((bf16[8,256,256]{2,1,0:T(8,128)(2,1)}), bf16[8,256,256]{2,1,0:T(8,128)(2,1)S(1)}, u32[]{:S(2)}, u32[]{:S(2)}) async-start(bf16[8,256,256]{2,1,0:T(8,128)(2,1)} %far_levels.1), calls=%async_computation.4 | async-start | bytes 2097152 | tf_op jit(solution)/shard_map/all_to_all | solution.py:419
  103.3 8.9 %collective-permute-done.7.refs_4_ = bf16[4,128,1024]{2,1,0:T(8,128)(2,1)} collective-permute-done((bf16[4,128,1024]{2,1,0:T(8,128)(2,1)S(1)}, bf16[4,128,1024]{2,1,0:T(8,128)(2,1)}, u32[]{:S(2)}, u32[]{:S(2)}) %collective-permute-start.7) | collective-permute-done | bytes 1048608 | tf_op jit(solution)/shard_map/ppermute | solution.py:30
  114.1 2.4 %collective-permute-start.5 = (bf16[4,128,1024]{2,1,0:T(8,128)(2,1)S(1)}, bf16[4,128,1024]{2,1,0:T(8,128)(2,1)}, u32[]{:S(2)}, u32[]{:S(2)}) collective-permute-start(bf16[4,128,1024]{2,1,0:T(8,128)(2,1)S(1)} %pad_maximum_fusion.refs_0_), channel_id=1, source_target_pairs={{0,1},{1,0},{2,3},{3,2},{4,5},{5,4},{6,7},{7,6},{8,9},{9,8},{10,11... | collective-permute-start | bytes 3145736 | tf_op jit(solution)/shard_map/ppermute | solution.py:30
  118.4 2.4 %collective-permute-start.9 = (bf16[4,128,1024]{2,1,0:T(8,128)(2,1)}, bf16[4,128,1024]{2,1,0:T(8,128)(2,1)}, u32[]{:S(2)}, u32[]{:S(2)}) collective-permute-start(bf16[4,128,1024]{2,1,0:T(8,128)(2,1)} %collective-permute-done.4.refs_6_), channel_id=1, source_target_pairs={{0,1},{1,0},{2,3},{3,2},{4,5},{5,4},{6,7},{7,6},{8,9},{9,8},{10,11... | collective-permute-start | bytes 3145736 | tf_op jit(solution)/shard_map/ppermute | solution.py:30
  125.8 5.4 %finish.1 = (bf16[256,1024]{1,0:T(8,128)(2,1)S(1)}, bf16[2,1024,256]{2,1,0:T(8,128)(2,1)S(1)}) custom-call(s32[5]{0:T(128)S(1)} %stack.67.where_ref, bf16[4,128,1024]{2,1,0:T(8,128)(2,1)S(1)} %pad_maximum_fusion.refs_0_, bf16[4,128,1024]{2,1,0:T(8,128)(2,1)} %collective-permute-done.5.refs_1_, bf16[4,128,1024]{2,1,0:T(8,128)(2,1)} %collective-permute-done.3.refs_2_, ...), custom_call_target="tpu_custom_call" | custom-call | flops 1073741824 | bytes 16777216 | tf_op jit(solution)/shard_map/finish/pallas_call | solution.py:320
  131.2 11.2 %collective-permute-start.10 = (bf16[256,1024]{1,0:T(8,128)(2,1)S(1)}, bf16[256,1024]{1,0:T(8,128)(2,1)S(1)}, u32[]{:S(2)}, u32[]{:S(2)}) collective-permute-start(bf16[256,1024]{1,0:T(8,128)(2,1)S(1)} %get-tuple-element.42), channel_id=1, source_target_pairs={{0,2},{2,0},{1,3},{3,1},{4,6},{6,4},{5,7},{7,5},{8,10},{10,8},{9,1... | collective-permute-start | bytes 1572872 | tf_op jit(solution)/shard_map/ppermute | solution.py:30
  142.5 3.9 %keep.1 = f32[256,1024]{1,0:T(8,128)S(1)} custom-call(s32[5]{0:T(128)S(1)} %stack.67.where_ref, bf16[4,128,1024]{2,1,0:T(8,128)(2,1)S(1)} %pad_maximum_fusion.refs_0_, bf16[4,128,1024]{2,1,0:T(8,128)(2,1)} %collective-permute-done.5.refs_1_, bf16[4,128,1024]{2,1,0:T(8,128)(2,1)} %collective-permute-done.3.refs_2_, ...), custom_call_target="tpu_custom_call" | custom-call | flops 1073741824 | bytes 8388608 | tf_op jit(solution)/shard_map/keep/pallas_call | solution.py:346
  146.4 18.3 %collective-permute-done.10 = bf16[256,1024]{1,0:T(8,128)(2,1)S(1)} collective-permute-done((bf16[256,1024]{1,0:T(8,128)(2,1)S(1)}, bf16[256,1024]{1,0:T(8,128)(2,1)S(1)}, u32[]{:S(2)}, u32[]{:S(2)}) %collective-permute-start.10) | collective-permute-done | bytes 524320 | tf_op jit(solution)/shard_map/ppermute | solution.py:30
  (32 shorter events, 19.5 us)
Async XLA Ops:
  0.0 0.8 copy-start
  1.6 18.0 %all-to-all-start = ((bf16[8,16,1024]{2,1,0:T(8,128)(2,1)}), bf16[8,16,1024]{2,1,0:T(8,128)(2,1)S(1)}, u32[]{:S(2)}, u32[]{:S(2)}) async-start(bf16[8,16,1024]{2,1,0:T(8,128)(2,1)} %broadcast_in_dim.4), calls=%async_computation | async-start | bytes 524288 | tf_op jit(solution)/shard_map/all_to_all | solution.py:364
  19.5 37.4 %all-to-all-start.1 = ((bf16[8,576,128]{2,1,0:T(8,128)(2,1)}), bf16[8,576,128]{2,1,0:T(8,128)(2,1)S(1)}, u32[]{:S(2)}, u32[]{:S(2)}) async-start(bf16[8,576,128]{2,1,0:T(8,128)(2,1)} %get-tuple-element.25), calls=%async_computation.1 | async-start | bytes 2359296 | tf_op jit(solution)/shard_map/all_to_all | solution.py:404
  24.5 18.5 %collective-permute-start.2 = (bf16[128,1024]{1,0:T(8,128)(2,1)S(1)}, bf16[128,1024]{1,0:T(8,128)(2,1)S(1)}, u32[]{:S(2)}, u32[]{:S(2)}) collective-permute-start(bf16[128,1024]{1,0:T(8,128)(2,1)S(1)} %bitcast.22), channel_id=1, source_target_pairs={{0,384},{128,256},{256,128},{384,0},{1,385},{129,257},{257,129},{3... | collective-permute-start | bytes 786440 | tf_op jit(solution)/shard_map/ppermute | solution.py:30
  32.4 19.3 %collective-permute-start.1 = (bf16[128,1024]{1,0:T(8,128)(2,1)S(1)}, bf16[128,1024]{1,0:T(8,128)(2,1)S(1)}, u32[]{:S(2)}, u32[]{:S(2)}) collective-permute-start(bf16[128,1024]{1,0:T(8,128)(2,1)S(1)} %bitcast.23), channel_id=1, source_target_pairs={{0,256},{128,384},{256,0},{384,128},{1,257},{129,385},{257,1},{385... | collective-permute-start | bytes 786440 | tf_op jit(solution)/shard_map/ppermute | solution.py:30
  34.3 17.3 %collective-permute-start = (bf16[128,1024]{1,0:T(8,128)(2,1)S(1)}, bf16[128,1024]{1,0:T(8,128)(2,1)S(1)}, u32[]{:S(2)}, u32[]{:S(2)}) collective-permute-start(bf16[128,1024]{1,0:T(8,128)(2,1)S(1)} %bitcast.24), channel_id=1, source_target_pairs={{0,128},{128,0},{256,384},{384,256},{1,129},{129,1},{257,385},{385... | collective-permute-start | bytes 786440 | tf_op jit(solution)/shard_map/ppermute | solution.py:30
  51.8 28.5 %collective-permute-start.4 = (bf16[4,128,1024]{2,1,0:T(8,128)(2,1)S(1)}, bf16[4,128,1024]{2,1,0:T(8,128)(2,1)}, u32[]{:S(2)}, u32[]{:S(2)}) collective-permute-start(bf16[4,128,1024]{2,1,0:T(8,128)(2,1)S(1)} %pad_maximum_fusion.refs_0_), channel_id=1, source_target_pairs={{0,96},{32,64},{64,32},{96,0},{1,97},{33,65},{65,33},{97,1},{2,98}... | collective-permute-start | bytes 3145736 | tf_op jit(solution)/shard_map/ppermute | solution.py:30
  54.2 28.1 %collective-permute-start.3 = (bf16[4,128,1024]{2,1,0:T(8,128)(2,1)S(1)}, bf16[4,128,1024]{2,1,0:T(8,128)(2,1)}, u32[]{:S(2)}, u32[]{:S(2)}) collective-permute-start(bf16[4,128,1024]{2,1,0:T(8,128)(2,1)S(1)} %pad_maximum_fusion.refs_0_), channel_id=1, source_target_pairs={{0,32},{32,0},{64,96},{96,64},{1,33},{33,1},{65,97},{97,65},{2,34}... | collective-permute-start | bytes 3145736 | tf_op jit(solution)/shard_map/ppermute | solution.py:30
  57.8 10.7 %all-to-all-start.2 = ((bf16[4,256,128]{2,1,0:T(8,128)(2,1)}), bf16[4,256,128]{2,1,0:T(8,128)(2,1)S(1)}, u32[]{:S(2)}, u32[]{:S(2)}) async-start(bf16[4,256,128]{2,1,0:T(8,128)(2,1)} %group_sum.1), calls=%async_computation.2 | async-start | bytes 524288 | tf_op jit(solution)/shard_map/all_to_all | solution.py:413
  69.1 0.9 copy-start.1
  70.1 22.7 %all-to-all-start.3 = ((bf16[4,3,256,128]{3,2,1,0:T(8,128)(2,1)}), bf16[4,3,256,128]{3,2,1,0:T(8,128)(2,1)S(1)}, u32[]{:S(2)}, u32[]{:S(2)}) async-start(bf16[4,3,256,128]{3,2,1,0:T(8,128)(2,1)} %copy-done.1), calls=%async_computation.3 | async-start | bytes 1572864 | tf_op jit(solution)/shard_map/all_to_all | solution.py:415
  75.6 45.2 %copy-start.3 = (f32[2048]{0:T(1024)S(1)}, f32[2048]{0:T(1024)}, u32[]{:S(2)}) copy-start(f32[2048]{0:T(1024)} %param.14) | copy-start | bytes 24580
  75.6 36.5 %collective-permute-start.7 = (bf16[4,128,1024]{2,1,0:T(8,128)(2,1)S(1)}, bf16[4,128,1024]{2,1,0:T(8,128)(2,1)}, u32[]{:S(2)}, u32[]{:S(2)}) collective-permute-start(bf16[4,128,1024]{2,1,0:T(8,128)(2,1)S(1)} %pad_maximum_fusion.refs_0_), channel_id=1, source_target_pairs={{0,64},{32,96},{64,0},{96,32},{1,65},{33,97},{65,1},{97,33},{2,66}... | collective-permute-start | bytes 3145736 | tf_op jit(solution)/shard_map/ppermute | solution.py:30
  96.0 28.2 %all-to-all-start.4 = ((bf16[8,256,256]{2,1,0:T(8,128)(2,1)}), bf16[8,256,256]{2,1,0:T(8,128)(2,1)S(1)}, u32[]{:S(2)}, u32[]{:S(2)}) async-start(bf16[8,256,256]{2,1,0:T(8,128)(2,1)} %far_levels.1), calls=%async_computation.4 | async-start | bytes 2097152 | tf_op jit(solution)/shard_map/all_to_all | solution.py:419
  112.2 9.2 %collective-permute-start.8 = (bf16[4,128,1024]{2,1,0:T(8,128)(2,1)}, bf16[4,128,1024]{2,1,0:T(8,128)(2,1)}, u32[]{:S(2)}, u32[]{:S(2)}) collective-permute-start(bf16[4,128,1024]{2,1,0:T(8,128)(2,1)} %collective-permute-done.7.refs_4_), channel_id=1, source_target_pairs={{0,1},{1,0},{2,3},{3,2},{4,5},{5,4},{6,7},{7,6},{8,9},{9,8},{10,11... | collective-permute-start | bytes 3145736 | tf_op jit(solution)/shard_map/ppermute | solution.py:30
  114.1 7.2 %collective-permute-start.5 = (bf16[4,128,1024]{2,1,0:T(8,128)(2,1)S(1)}, bf16[4,128,1024]{2,1,0:T(8,128)(2,1)}, u32[]{:S(2)}, u32[]{:S(2)}) collective-permute-start(bf16[4,128,1024]{2,1,0:T(8,128)(2,1)S(1)} %pad_maximum_fusion.refs_0_), channel_id=1, source_target_pairs={{0,1},{1,0},{2,3},{3,2},{4,5},{5,4},{6,7},{7,6},{8,9},{9,8},{10,11... | collective-permute-start | bytes 3145736 | tf_op jit(solution)/shard_map/ppermute | solution.py:30
  116.5 4.9 %collective-permute-start.6 = (bf16[4,128,1024]{2,1,0:T(8,128)(2,1)}, bf16[4,128,1024]{2,1,0:T(8,128)(2,1)}, u32[]{:S(2)}, u32[]{:S(2)}) collective-permute-start(bf16[4,128,1024]{2,1,0:T(8,128)(2,1)} %collective-permute-done.3.refs_2_), channel_id=1, source_target_pairs={{0,1},{1,0},{2,3},{3,2},{4,5},{5,4},{6,7},{7,6},{8,9},{9,8},{10,11... | collective-permute-start | bytes 3145736 | tf_op jit(solution)/shard_map/ppermute | solution.py:30
  118.4 5.0 %collective-permute-start.9 = (bf16[4,128,1024]{2,1,0:T(8,128)(2,1)}, bf16[4,128,1024]{2,1,0:T(8,128)(2,1)}, u32[]{:S(2)}, u32[]{:S(2)}) collective-permute-start(bf16[4,128,1024]{2,1,0:T(8,128)(2,1)} %collective-permute-done.4.refs_6_), channel_id=1, source_target_pairs={{0,1},{1,0},{2,3},{3,2},{4,5},{5,4},{6,7},{7,6},{8,9},{9,8},{10,11... | collective-permute-start | bytes 3145736 | tf_op jit(solution)/shard_map/ppermute | solution.py:30
  124.2 1.6 copy-start.2
  131.2 33.4 %collective-permute-start.10 = (bf16[256,1024]{1,0:T(8,128)(2,1)S(1)}, bf16[256,1024]{1,0:T(8,128)(2,1)S(1)}, u32[]{:S(2)}, u32[]{:S(2)}) collective-permute-start(bf16[256,1024]{1,0:T(8,128)(2,1)S(1)} %get-tuple-element.42), channel_id=1, source_target_pairs={{0,2},{2,0},{1,3},{3,1},{4,6},{6,4},{5,7},{7,5},{8,10},{10,8},{9,1... | collective-permute-start | bytes 1572872 | tf_op jit(solution)/shard_map/ppermute | solution.py:30
